TPU v7x, 256 devices: a whole 4x4x8 slice. The times are simulated.
256 devices in a mesh: dp: 2 (over y_hi), ctx: 128 (over x, z, y_lo, core).
Axes of the slice: x: 4, y: 4 (y_hi: 2, y_lo: 2; y = y_hi * 2 + y_lo), z: 8, core: 2. Of those that a mesh axis runs over, the one named last changes fastest.
Arguments:
- projected: bfloat16 [3, 2, 16384, 4096], P(None, 'dp', 'ctx'), may hold values from -6 to 6
- short_taps: float32 [3, 3, 4096], replicated, may hold values from -3 to 3
- long_filter: float32 [4096, 16384], P('ctx'), may hold values from -3 to 3
- grad_out: bfloat16 [2, 16384, 4096], P('dp', 'ctx'), may hold values from -6 to 6
Outputs:
- grad_projected: bfloat16 [3, 2, 16384, 4096], P(None, 'dp', 'ctx')
- grad_taps: float32 [3, 3, 4096], replicated
- grad_filter: float32 [4096, 16384], P('ctx', 'dp')
All inputs are finite; a program needn't handle non-finite values.
Results may differ from a plain program's by a relative error of at most 0.01.
Values may be sent and summed in bfloat16 or wider, within the bound.
No kernel may reach another device: no remote copies, remote signals or barrier semaphores. Data moves between devices by JAX's collectives and lax.ppermute only.
A program may use at most 192 MiB of HBM per device.

v0:
```python
import functools
import math

import jax
import jax.numpy as jnp
import numpy as np
from jax import lax
from jax.experimental import pallas as pl
from jax.experimental.pallas import tpu as pltpu
from jax.sharding import PartitionSpec as P

ROWS = 128
MIB = 2**20


def rounded(table):
    high = table.astype(jnp.bfloat16)
    low = (table - high.astype(np.float64)).astype(jnp.bfloat16)
    return high, low


@functools.cache
def tables():
    idx = np.arange(ROWS, dtype=np.float64)
    quarter = idx + 0.25
    ang_a = 2.0 * math.pi * np.outer(quarter, idx) / ROWS
    fwd_a = np.concatenate([np.cos(ang_a), -np.sin(ang_a)], axis=0)
    inv_a = np.concatenate([np.cos(ang_a.T), -np.sin(ang_a.T)], axis=1) / ROWS**2
    ang_w = 2.0 * math.pi * np.outer(quarter, idx) / ROWS**2
    turn = np.stack([np.cos(ang_w), -np.sin(ang_w)]).astype(np.float32)
    ang_b = 2.0 * math.pi * (np.outer(idx, idx) % ROWS) / ROWS
    cos_b, sin_b = np.cos(ang_b), np.sin(ang_b)
    fwd_b = np.block([[cos_b, -sin_b], [sin_b, cos_b]])
    inv_b = np.block([[cos_b, sin_b], [-sin_b, cos_b]])
    return {
        "fwd_a": np.concatenate(rounded(fwd_a), axis=1),
        "turn": turn,
        "fwd_b": np.stack(rounded(fwd_b)),
        "inv_b": np.stack(rounded(inv_b)),
        "inv_a": np.stack(rounded(inv_a)),
    }


def dot(lhs, rhs):
    return lax.dot_general(lhs, rhs, (((1,), (0,)), ((), ())), preferred_element_type=jnp.float32)


def split(value):
    high = value.astype(jnp.bfloat16)
    return high, (value - high.astype(jnp.float32)).astype(jnp.bfloat16)


def halves(value):
    return value[:, :ROWS], value[:, ROWS:]


def params(mib=48):
    return pltpu.CompilerParams(vmem_limit_bytes=mib * MIB)


def shifted(ext_ref, stream, tap):
    return ext_ref[stream, pl.ds(8 - tap, ROWS), :]


def fill_ext(ext_ref, proj_ref, edge_ref):
    for stream in range(3):
        ext_ref[stream, pl.ds(8, ROWS), :] = proj_ref[stream].astype(jnp.float32)
        ext_ref[stream, pl.ds(6, 2), :] = edge_ref[pl.ds(2 * stream, 2), :]


def feature(ext_ref, taps_ref, stream):
    total = taps_ref[stream, pl.ds(0, 1), :] * shifted(ext_ref, stream, 0)
    for tap in (1, 2):
        total += taps_ref[stream, pl.ds(tap, 1), :] * shifted(ext_ref, stream, tap)
    return total


def edge_kernel(proj_ref, out_ref):
    out_ref[...] = jnp.zeros_like(out_ref)
    for stream in range(3):
        tail = proj_ref[stream].astype(jnp.float32)
        out_ref[pl.ds(2 * stream, 2), :] = tail[14:16, :]


def edges(proj):
    channels = proj.shape[-1]
    return pl.pallas_call(
        edge_kernel,
        grid=(1,),
        in_specs=[pl.BlockSpec((3, 16, channels), lambda i: (0, ROWS // 16 - 1, 0))],
        out_specs=pl.BlockSpec((8, channels), lambda i: (0, 0)),
        out_shape=jax.ShapeDtypeStruct((8, channels), jnp.float32),
        compiler_params=params(16),
    )(proj)


def gate_kernel(proj_ref, edge_ref, taps_ref, grad_ref, out_ref, ext_ref):
    fill_ext(ext_ref, proj_ref, edge_ref)
    query, key, value = (feature(ext_ref, taps_ref, stream) for stream in range(3))
    gated = key * value
    grad_gate = grad_ref[...].astype(jnp.float32) * query
    count, _, width, _ = out_ref.shape
    for at, rows in enumerate((gated, grad_gate)):
        out_ref[:, at] = rows.T.astype(jnp.bfloat16).reshape(count, width, ROWS)


def gates(proj, edge, taps, grad_out, width):
    channels = proj.shape[-1]
    block = min(512, channels)
    return pl.pallas_call(
        gate_kernel,
        grid=(channels // block,),
        in_specs=[
            pl.BlockSpec((3, ROWS, block), lambda i: (0, 0, i)),
            pl.BlockSpec((8, block), lambda i: (0, i)),
            pl.BlockSpec((3, 3, block), lambda i: (0, 0, i)),
            pl.BlockSpec((ROWS, block), lambda i: (0, i)),
        ],
        out_specs=pl.BlockSpec((block // width, 2, width, ROWS), lambda i: (i, 0, 0, 0)),
        out_shape=jax.ShapeDtypeStruct((channels // width, 2, width, ROWS), jnp.bfloat16),
        scratch_shapes=[pltpu.VMEM((3, ROWS + 8, block), jnp.float32)],
        compiler_params=params(32),
    )(proj, edge, taps, grad_out)


def spectrum_kernel(filter_ref, fwd_a_ref, turn_ref, fwd_b_ref, out_ref):
    cos_w, sin_w = turn_ref[0], turn_ref[1]

    def one(ch, carry):
        high, low = split(filter_ref[ch])
        y = dot(fwd_a_ref[...], jnp.concatenate([high, high], axis=0))
        y += dot(fwd_a_ref[...], jnp.concatenate([low, low], axis=0))
        y_re, y_im = y[:ROWS], y[ROWS:]
        turned = jnp.concatenate(
            [y_re * cos_w - y_im * sin_w, y_re * sin_w + y_im * cos_w], axis=1
        )
        high, low = split(turned)
        out_ref[ch] = dot(high, fwd_b_ref[0]) + dot(high, fwd_b_ref[1]) + dot(low, fwd_b_ref[0])
        return carry

    lax.fori_loop(0, filter_ref.shape[0], one, 0, unroll=2)


def whole(shape):
    return pl.BlockSpec(shape, lambda i: (0,) * len(shape))


def spectrum(filter_sq, tab):
    width = filter_sq.shape[0]
    block = min(8, width)
    return pl.pallas_call(
        spectrum_kernel,
        grid=(width // block,),
        in_specs=[
            pl.BlockSpec((block, ROWS, ROWS), lambda i: (i, 0, 0)),
            whole((2 * ROWS, 2 * ROWS)),
            whole((2, ROWS, ROWS)),
            whole((2, 2 * ROWS, 2 * ROWS)),
        ],
        out_specs=pl.BlockSpec((block, ROWS, 2 * ROWS), lambda i: (i, 0, 0)),
        out_shape=jax.ShapeDtypeStruct((width, ROWS, 2 * ROWS), jnp.float32),
        compiler_params=params(32),
        cost_estimate=pl.CostEstimate(
            flops=width * 5 * 2 * (2 * ROWS) ** 3, bytes_accessed=width * 3 * 4 * ROWS**2,
            transcendentals=0,
        ),
    )(filter_sq, tab["fwd_a"], tab["turn"], tab["fwd_b"])


def conv_kernel(
    in_ref, spec_ref, fwd_a_ref, turn_ref, fwd_b_ref, inv_b_ref, inv_a_ref,
    out_ref, lag_ref, rows_ref, *, group,
):
    block = in_ref.shape[2]
    for at in range(2):
        rows_ref[at] = in_ref[:, at].astype(jnp.float32).reshape(ROWS * block, ROWS)
    cos_w, sin_w = turn_ref[0], turn_ref[1]

    def one(ch):
        strided = pl.ds(ch, ROWS, stride=block)
        both = jnp.concatenate(
            [rows_ref[at, strided, :].astype(jnp.bfloat16) for at in range(2)], axis=1
        )
        y = dot(fwd_a_ref[...], jnp.concatenate([both, both], axis=0))
        stacked = []
        for at in range(2):
            y_re = y[:ROWS, at * ROWS : (at + 1) * ROWS]
            y_im = y[ROWS:, at * ROWS : (at + 1) * ROWS]
            stacked.append(
                jnp.concatenate(
                    [
                        (y_re * cos_w - y_im * sin_w).astype(jnp.bfloat16),
                        (y_re * sin_w + y_im * cos_w).astype(jnp.bfloat16),
                    ],
                    axis=1,
                )
            )
        stacked = jnp.concatenate(stacked, axis=0)
        z = dot(stacked, fwd_b_ref[0]) + dot(stacked, fwd_b_ref[1])
        x_re, x_im = halves(z[:ROWS])
        g_re, g_im = halves(z[ROWS:])
        h_re, h_im = halves(spec_ref[ch])
        products = jnp.concatenate(
            [
                jnp.concatenate([re.astype(jnp.bfloat16), im.astype(jnp.bfloat16)], axis=1)
                for re, im in (
                    (x_re * h_re - x_im * h_im, x_re * h_im + x_im * h_re),
                    (h_re * g_re + h_im * g_im, h_re * g_im - h_im * g_re),
                    (g_re * x_re + g_im * x_im, g_im * x_re - g_re * x_im),
                )
            ],
            axis=0,
        )
        v = dot(products, inv_b_ref[0]) + dot(products, inv_b_ref[1])
        parts_re, parts_im = [], []
        for at in range(3):
            v_re, v_im = halves(v[at * ROWS : (at + 1) * ROWS])
            parts_re.append((v_re * cos_w + v_im * sin_w).astype(jnp.bfloat16))
            parts_im.append((v_im * cos_w - v_re * sin_w).astype(jnp.bfloat16))
        turned = jnp.concatenate(
            [jnp.concatenate(parts_re, axis=1), jnp.concatenate(parts_im, axis=1)], axis=0
        )
        res = dot(inv_a_ref[0], turned) + dot(inv_a_ref[1], turned)
        for at in range(2):
            rows_ref[at, strided, :] = res[:, at * ROWS : (at + 1) * ROWS]
        lag_ref[ch] = res[:, 2 * ROWS :]

    def some(step, carry):
        for at in range(group):
            one(step * group + at)
        return carry

    lax.fori_loop(0, block // group, some, 0)
    for at in range(2):
        out_ref[:, at] = rows_ref[at].astype(jnp.bfloat16).reshape(ROWS, block, ROWS)


def convolve(received, spec, tab):
    width = received.shape[2]
    block = min(16, width)
    return pl.pallas_call(
        functools.partial(conv_kernel, group=2),
        grid=(width // block,),
        in_specs=[
            pl.BlockSpec((ROWS, 2, block, ROWS), lambda i: (0, 0, i, 0)),
            pl.BlockSpec((block, ROWS, 2 * ROWS), lambda i: (i, 0, 0)),
            whole((2 * ROWS, 2 * ROWS)),
            whole((2, ROWS, ROWS)),
            whole((2, 2 * ROWS, 2 * ROWS)),
            whole((2, 2 * ROWS, 2 * ROWS)),
            whole((2, ROWS, 2 * ROWS)),
        ],
        out_specs=[
            pl.BlockSpec((ROWS, 2, block, ROWS), lambda i: (0, 0, i, 0)),
            pl.BlockSpec((block, ROWS, ROWS), lambda i: (i, 0, 0)),
        ],
        out_shape=[
            jax.ShapeDtypeStruct((ROWS, 2, width, ROWS), jnp.bfloat16),
            jax.ShapeDtypeStruct((width, ROWS, ROWS), jnp.float32),
        ],
        scratch_shapes=[pltpu.VMEM((2, ROWS * block, ROWS), jnp.float32)],
        compiler_params=params(56),
    )(received, spec, tab["fwd_a"], tab["turn"], tab["fwd_b"], tab["inv_b"], tab["inv_a"])


def grads_kernel(
    ret_ref, proj_ref, edge_ref, taps_ref, grad_ref,
    out_ref, sums_ref, first_ref, last_ref, ext_ref, grads_ref,
):
    fill_ext(ext_ref, proj_ref, edge_ref)
    block = grad_ref.shape[1]
    conv, corr = (
        ret_ref[:, at].reshape(block, ROWS).astype(jnp.float32).T for at in range(2)
    )
    key, value = (feature(ext_ref, taps_ref, stream) for stream in (1, 2))
    grads = (grad_ref[...].astype(jnp.float32) * conv, corr * value, corr * key)
    first_ref[...] = jnp.zeros_like(first_ref)
    for stream in range(3):
        grads_ref[stream, pl.ds(0, ROWS), :] = grads[stream]
        grads_ref[stream, pl.ds(ROWS, 8), :] = jnp.zeros((8, block), jnp.float32)
        first_ref[pl.ds(2 * stream, 2), :] = grads[stream][:2]
        for tap in range(3):
            sums = jnp.sum(grads[stream] * shifted(ext_ref, stream, tap), axis=0, keepdims=True)
            sums_ref[pl.ds(3 * stream + tap, 1)] = sums.reshape(1, block // ROWS, ROWS)
        total = taps_ref[stream, pl.ds(0, 1), :] * grads[stream]
        for tap in (1, 2):
            total += taps_ref[stream, pl.ds(tap, 1), :] * grads_ref[stream, pl.ds(tap, ROWS), :]
        out_ref[stream] = total.astype(jnp.bfloat16)
        last_ref[stream] = total[ROWS - 16 :]


def stream_grads(returned, proj, edge, taps, grad_out):
    channels = proj.shape[-1]
    width = returned.shape[2]
    block = min(1024, channels)
    return pl.pallas_call(
        grads_kernel,
        grid=(channels // block,),
        in_specs=[
            pl.BlockSpec((block // width, 2, width, ROWS), lambda i: (i, 0, 0, 0)),
            pl.BlockSpec((3, ROWS, block), lambda i: (0, 0, i)),
            pl.BlockSpec((8, block), lambda i: (0, i)),
            pl.BlockSpec((3, 3, block), lambda i: (0, 0, i)),
            pl.BlockSpec((ROWS, block), lambda i: (0, i)),
        ],
        out_specs=[
            pl.BlockSpec((3, ROWS, block), lambda i: (0, 0, i)),
            pl.BlockSpec((9, block // ROWS, ROWS), lambda i: (0, i, 0)),
            pl.BlockSpec((8, block), lambda i: (0, i)),
            pl.BlockSpec((3, 16, block), lambda i: (0, 0, i)),
        ],
        out_shape=[
            jax.ShapeDtypeStruct((3, ROWS, channels), jnp.bfloat16),
            jax.ShapeDtypeStruct((9, channels // ROWS, ROWS), jnp.float32),
            jax.ShapeDtypeStruct((8, channels), jnp.float32),
            jax.ShapeDtypeStruct((3, 16, channels), jnp.float32),
        ],
        scratch_shapes=[
            pltpu.VMEM((3, ROWS + 8, block), jnp.float32),
            pltpu.VMEM((3, ROWS + 8, block), jnp.float32),
        ],
        compiler_params=params(48),
    )(returned, proj, edge, taps, grad_out)


def last_kernel(whole_ref, last_ref, later_ref, taps_ref, out_ref):
    del whole_ref
    for stream in range(3):
        later = later_ref[pl.ds(2 * stream, 2), :]
        tap_1, tap_2 = (taps_ref[stream, pl.ds(tap, 1), :] for tap in (1, 2))
        rows = last_ref[stream]
        row_14 = rows[14:15] + tap_2 * later[:1]
        row_15 = rows[15:] + tap_1 * later[:1] + tap_2 * later[1:]
        out_ref[stream] = jnp.concatenate([rows[:14], row_14, row_15], axis=0).astype(jnp.bfloat16)


def finish_rows(grad_rows, last, later, taps):
    channels = grad_rows.shape[-1]
    return pl.pallas_call(
        last_kernel,
        grid=(1,),
        in_specs=[
            pl.BlockSpec(memory_space=pl.ANY),
            whole((3, 16, channels)),
            whole((8, channels)),
            whole((3, 3, channels)),
        ],
        out_specs=pl.BlockSpec((3, 16, channels), lambda i: (0, ROWS // 16 - 1, 0)),
        out_shape=jax.ShapeDtypeStruct(grad_rows.shape, grad_rows.dtype),
        input_output_aliases={0: 0},
        compiler_params=params(16),
    )(grad_rows, last, later, taps)


def passed_along(value, steps):
    count = lax.axis_size("ctx")
    initial, last = (max(0, -steps), min(count, count - steps))
    return lax.ppermute(value, "ctx", [(source, source + steps) for source in range(initial, last)])


def exchanged(value, axes):
    return lax.all_to_all(value, axes, split_axis=0, concat_axis=0, tiled=True)


def sum_everywhere(sums):
    taps, blocks, _ = sums.shape
    devices = lax.axis_size("dp") * lax.axis_size("ctx")
    owners = taps * blocks // 2
    pieces = jnp.pad(sums.reshape(owners, 2, ROWS), ((0, devices - owners), (0, 0), (0, 0)))
    own = jnp.sum(exchanged(pieces, ("dp", "ctx")), axis=0)
    spread = exchanged(jnp.broadcast_to(own[None], (devices, 2, ROWS)), ("dp", "ctx"))
    return spread[:owners].reshape(3, 3, blocks * ROWS)


def local(projected, short_taps, long_filter, grad_out):
    tab = tables()
    proj = projected[:, 0]
    grad_rows = grad_out[0]
    width = long_filter.shape[0]
    edge = passed_along(edges(proj), 1)
    sent = gates(proj, edge, short_taps, grad_rows, width)
    received = exchanged(sent, "ctx")
    spec = spectrum(long_filter.reshape(width, ROWS, ROWS), tab)
    results, lag = convolve(received, spec, tab)
    returned = exchanged(results, "ctx")
    second = lax.axis_index("dp") == 1
    lower, upper = lag[:, : ROWS // 2], lag[:, ROWS // 2 :]
    other = lax.ppermute(
        jnp.where(second, lower, upper).astype(jnp.bfloat16), "dp", [(0, 1), (1, 0)]
    )
    lag_sum = jnp.where(second, upper, lower) + other.astype(jnp.float32)
    grad_filter = lag_sum.reshape(width, ROWS // 2 * ROWS)
    grad_in, sums, first, last = stream_grads(returned, proj, edge, short_taps, grad_rows)
    later = passed_along(first, -1)
    grad_in = finish_rows(grad_in, last, later, short_taps)
    return (grad_in[:, None], sum_everywhere(sums), grad_filter)


def solution(mesh):
    return jax.shard_map(
        local,
        mesh=mesh,
        in_specs=(P(None, "dp", "ctx", None), P(), P("ctx", None), P("dp", "ctx", None)),
        out_specs=(P(None, "dp", "ctx", None), P(), P("ctx", "dp")),
        check_vma=False,
    )
```

profile of v0, /device:TPU:1, one launch (start us, length us, event | category | flops | bytes accessed | tf_op | source)
XLA Modules:
  0.0 234.8 jit_solution(15455019462013540522)
XLA Ops:
  0.6 0.0 copy-start
  0.6 1.9 copy-done
  2.6 4.9 %collective-permute-start = (f32[8,4096]{1,0:T(8,128)S(1)}, f32[8,4096]{1,0:T(8,128)S(1)}, u32[]{:S(2)}, u32[]{:S(2)}) collective-permute-start(f32[8,4096]{1,0:T(8,128)S(1)} %shard_map.112), channel_id=1, source_target_pairs={{0,1},{1,2},{2,3},{3,4},{4,5},{5,6},{6,7},{7,8},{8,9},{9,10},{10,1... | collective-permute-start | bytes 393224 | tf_op jit(solution)/shard_map/ppermute | solution.py:358
  7.4 1.9 collective-permute-done.edge_ref
  9.4 0.0 copy-done.1
  9.4 1.2 copy-done.2
  10.6 0.9 copy-done.5
  11.5 5.1 %shard_map.113 = bf16[128,2,32,128]{3,2,1,0:T(8,128)(2,1)} custom-call(bf16[3,128,4096]{2,1,0:T(8,128)(2,1)S(1)} %bitcast.14, f32[8,4096]{1,0:T(8,128)S(1)} %collective-permute-done.edge_ref, f32[3,3,4096]{2,1,0:T(4,128)S(1)} %copy-done.5, bf16[128,4096]{1,0:T(8,128)(2,1)S(1)} %bitcast.15), custom_call_target="tpu_custom_call" | custom-call | tf_op jit(solution)/shard_map/pallas_call | solution.py:110
  16.6 15.6 %all-to-all-start = ((bf16[128,2,32,128]{3,2,1,0:T(8,128)(2,1)}), bf16[128,2,32,128]{3,2,1,0:T(8,128)(2,1)S(1)}, u32[]{:S(2)}, u32[]{:S(2)}) async-start(bf16[128,2,32,128]{3,2,1,0:T(8,128)(2,1)} %shard_map.113), calls=%async_computation | async-start | bytes 4194304 | tf_op jit(solution)/shard_map/all_to_all | solution.py:362
  32.2 0.0 copy-start.9
  32.3 0.0 copy-start.10
  32.3 0.0 copy-start.11
  32.3 2.0 copy.14
  34.3 0.0 copy-done.9
  34.3 0.0 copy-done.10
  34.3 0.0 copy-done.11
  34.3 9.4 %shard_map.114.spec_ref = f32[32,128,256]{2,1,0:T(8,128)S(1)} custom-call(f32[32,128,128]{2,1,0:T(8,128)S(1)} %bitcast.17, bf16[256,256]{1,0:T(8,128)(2,1)S(1)} %copy-done.10, f32[2,128,128]{2,1,0:T(8,128)S(1)} %copy-done.11, bf16[2,256,256]{2,1,0:T(8,128)(2,1)S(1)} %copy-done.9), custom_call_target="tpu_custom_call" | custom-call | flops 5368709120 | bytes 6291456 | tf_op jit(solution)/shard_map/pallas_call | solution.py:151
  43.7 0.0 copy-start.4
  43.7 1.9 copy-done.4
  45.7 36.8 %all-to-all-done.in_ref = bf16[128,2,32,128]{3,2,1,0:T(8,128)(2,1)S(1)} async-done(((bf16[128,2,32,128]{3,2,1,0:T(8,128)(2,1)}), bf16[128,2,32,128]{3,2,1,0:T(8,128)(2,1)S(1)}, u32[]{:S(2)}, u32[]{:S(2)}) %all-to-all-start) | async-done | bytes 2097184 | tf_op jit(solution)/shard_map/all_to_all | solution.py:362
  82.4 1.3 copy-done.14
  83.7 30.5 %shard_map.115 = (bf16[128,2,32,128]{3,2,1,0:T(8,128)(2,1)}, f32[32,128,128]{2,1,0:T(8,128)}) custom-call(bf16[128,2,32,128]{3,2,1,0:T(8,128)(2,1)} %copy-done.14, f32[32,128,256]{2,1,0:T(8,128)} %copy-done.4, bf16[256,256]{1,0:T(8,128)(2,1)} %constant.22.clone.fwd_a_ref, f32[2,128,128]{2,1,0:T(8,128)} %constant.23.clone.turn_ref, ...), custom_call_target="tpu_custom_call" | custom-call | tf_op jit(solution)/shard_map/pallas_call | solution.py:241
  114.2 8.9 %all-to-all-start.1 = ((bf16[128,2,32,128]{3,2,1,0:T(8,128)(2,1)}), bf16[128,2,32,128]{3,2,1,0:T(8,128)(2,1)S(1)}, u32[]{:S(2)}, u32[]{:S(2)}) async-start(bf16[128,2,32,128]{3,2,1,0:T(8,128)(2,1)} %get-tuple-element.9), calls=%async_computation.1 | async-start | bytes 4194304 | tf_op jit(solution)/shard_map/all_to_all | solution.py:362
  123.2 50.2 %all-to-all-done.1.ret_ref = bf16[128,2,32,128]{3,2,1,0:T(8,128)(2,1)S(1)} async-done(((bf16[128,2,32,128]{3,2,1,0:T(8,128)(2,1)}), bf16[128,2,32,128]{3,2,1,0:T(8,128)(2,1)S(1)}, u32[]{:S(2)}, u32[]{:S(2)}) %all-to-all-start.1) | async-done | bytes 2097184 | tf_op jit(solution)/shard_map/all_to_all | solution.py:362
  173.3 0.0 copy-done.3
  173.4 0.0 copy-done.6
  173.4 10.0 %shard_map.116 = (bf16[3,128,4096]{2,1,0:T(8,128)(2,1)}, f32[9,32,128]{2,1,0:T(8,128)S(1)}, f32[8,4096]{1,0:T(8,128)S(1)}, f32[3,16,4096]{2,1,0:T(8,128)S(1)}) custom-call(bf16[128,2,32,128]{3,2,1,0:T(8,128)(2,1)S(1)} %all-to-all-done.1.ret_ref, bf16[3,128,4096]{2,1,0:T(8,128)(2,1)} %bitcast.12, f32[8,4096]{1,0:T(8,128)S(1)} %collective-permute-done.edge_ref, ...), custom_call_target="tpu_custom_call" | custom-call | tf_op jit(solution)/shard_map/pallas_call | solution.py:296
  183.4 0.9 copy-done.7
  184.3 0.7 copy-done.12
  184.9 0.8 pad.4
  185.7 9.8 %all-to-all-start.2 = ((f32[256,2,128]{2,1,0:T(2,128)}), f32[256,2,128]{2,1,0:T(2,128)S(1)}, u32[]{:S(2)}, u32[]{:S(2)}) async-start(f32[256,2,128]{2,1,0:T(2,128)} %pad.4), calls=%async_computation.2 | async-start | bytes 524288 | tf_op jit(solution)/shard_map/all_to_all | solution.py:362
  195.5 1.7 select_convert_fusion
  197.2 3.0 %collective-permute-start.2 = (bf16[32,64,128]{2,1,0:T(8,128)(2,1)S(1)}, bf16[32,64,128]{2,1,0:T(8,128)(2,1)}, u32[]{:S(2)}, u32[]{:S(2)}) collective-permute-start(bf16[32,64,128]{2,1,0:T(8,128)(2,1)S(1)} %select_convert_fusion), channel_id=1, source_target_pairs={{0,128},{128,0},{1,129},{129,1},{2,130},{130,2},{3,131},{131,3},{4... | collective-permute-start | bytes 1572872 | tf_op jit(solution)/shard_map/ppermute | solution.py:388
  200.2 11.0 %all-to-all-done.2 = f32[256,2,128]{2,1,0:T(2,128)S(1)} async-done(((f32[256,2,128]{2,1,0:T(2,128)}), f32[256,2,128]{2,1,0:T(2,128)S(1)}, u32[]{:S(2)}, u32[]{:S(2)}) %all-to-all-start.2) | async-done | bytes 262176 | tf_op jit(solution)/shard_map/all_to_all | solution.py:362
  211.1 0.3 reduce_sum.9
  211.4 0.8 broadcast_in_dim.10
  212.2 6.0 %all-to-all-start.3 = ((f32[256,2,128]{2,1,0:T(2,128)}), f32[256,2,128]{2,1,0:T(2,128)S(1)}, u32[]{:S(2)}, u32[]{:S(2)}) async-start(f32[256,2,128]{2,1,0:T(2,128)} %broadcast_in_dim.10), calls=%async_computation.3 | async-start | bytes 524288 | tf_op jit(solution)/shard_map/all_to_all | solution.py:362
  218.2 0.0 copy-done.13
  218.2 0.0 copy-start.8
  218.2 4.3 %collective-permute-start.1 = (f32[8,4096]{1,0:T(8,128)S(1)}, f32[8,4096]{1,0:T(8,128)S(1)}, u32[]{:S(2)}, u32[]{:S(2)}) collective-permute-start(f32[8,4096]{1,0:T(8,128)S(1)} %copy-done.13), channel_id=1, source_target_pairs={{1,0},{2,1},{3,2},{4,3},{5,4},{6,5},{7,6},{8,7},{9,8},{10,9},{11,1... | collective-permute-start | bytes 393224 | tf_op jit(solution)/shard_map/ppermute | solution.py:358
  222.6 0.0 collective-permute-done.2
  222.6 1.3 convert_add_fusion
  223.9 1.6 copy.17
  225.5 0.3 collective-permute-done.1.later_ref
  225.8 0.0 copy-done.8
  225.8 0.9 shard_map.117
  226.7 7.3 %all-to-all-done.3 = f32[256,2,128]{2,1,0:T(2,128)S(1)} async-done(((f32[256,2,128]{2,1,0:T(2,128)}), f32[256,2,128]{2,1,0:T(2,128)S(1)}, u32[]{:S(2)}, u32[]{:S(2)}) %all-to-all-start.3) | async-done | bytes 262176 | tf_op jit(solution)/shard_map/all_to_all | solution.py:362
  234.0 0.8 reshape.21
  (13 shorter events, 0.1 us)
Async XLA Ops:
  0.6 1.9 copy-start
  2.5 6.8 %copy-start.1 = (bf16[3,1,128,4096]{3,2,1,0:T(8,128)(2,1)S(1)}, bf16[3,1,128,4096]{3,2,1,0:T(8,128)(2,1)}, u32[]{:S(2)}) copy-start(bf16[3,1,128,4096]{3,2,1,0:T(8,128)(2,1)} %param.9) | copy-start | bytes 9437188
  2.6 6.8 %collective-permute-start = (f32[8,4096]{1,0:T(8,128)S(1)}, f32[8,4096]{1,0:T(8,128)S(1)}, u32[]{:S(2)}, u32[]{:S(2)}) collective-permute-start(f32[8,4096]{1,0:T(8,128)S(1)} %shard_map.112), channel_id=1, source_target_pairs={{0,1},{1,2},{2,3},{3,4},{4,5},{5,6},{6,7},{7,8},{8,9},{9,10},{10,1... | collective-permute-start | bytes 393224 | tf_op jit(solution)/shard_map/ppermute | solution.py:358
  9.4 1.2 copy-start.2
  10.6 0.9 copy-start.5
  16.6 65.8 %all-to-all-start = ((bf16[128,2,32,128]{3,2,1,0:T(8,128)(2,1)}), bf16[128,2,32,128]{3,2,1,0:T(8,128)(2,1)S(1)}, u32[]{:S(2)}, u32[]{:S(2)}) async-start(bf16[128,2,32,128]{3,2,1,0:T(8,128)(2,1)} %shard_map.113), calls=%async_computation | async-start | bytes 4194304 | tf_op jit(solution)/shard_map/all_to_all | solution.py:362
  32.2 2.1 copy-start.9
  32.3 2.1 copy-start.10
  32.3 2.1 copy-start.11
  43.7 1.9 copy-start.4
  82.4 1.3 copy-start.14
  114.2 59.1 %copy-start.3 = (bf16[1,128,4096]{2,1,0:T(8,128)(2,1)S(1)}, bf16[1,128,4096]{2,1,0:T(8,128)(2,1)}, u32[]{:S(2)}) copy-start(bf16[1,128,4096]{2,1,0:T(8,128)(2,1)} %param.12) | copy-start | bytes 3145732
  114.2 59.1 %copy-start.6 = (f32[3,3,4096]{2,1,0:T(4,128)S(1)}, f32[3,3,4096]{2,1,0:T(4,128)}, u32[]{:S(2)}) copy-start(f32[3,3,4096]{2,1,0:T(4,128)} %taps_ref.5) | copy-start | bytes 442372
  114.2 59.1 %all-to-all-start.1 = ((bf16[128,2,32,128]{3,2,1,0:T(8,128)(2,1)}), bf16[128,2,32,128]{3,2,1,0:T(8,128)(2,1)S(1)}, u32[]{:S(2)}, u32[]{:S(2)}) async-start(bf16[128,2,32,128]{3,2,1,0:T(8,128)(2,1)} %get-tuple-element.9), calls=%async_computation.1 | async-start | bytes 4194304 | tf_op jit(solution)/shard_map/all_to_all | solution.py:362
  183.4 0.9 copy-start.7
  184.3 0.7 copy-start.12
  184.9 37.7 %copy-start.15 = (f32[32,128,128]{2,1,0:T(8,128)S(1)}, f32[32,128,128]{2,1,0:T(8,128)}, u32[]{:S(2)}) copy-start(f32[32,128,128]{2,1,0:T(8,128)} %get-tuple-element.14) | copy-start | bytes 6291460
  184.9 33.3 %copy-start.13 = (f32[8,4096]{1,0:T(8,128)S(1)}, f32[8,4096]{1,0:T(8,128)}, u32[]{:S(2)}) copy-start(f32[8,4096]{1,0:T(8,128)} %copy-done.12) | copy-start | bytes 393220
  185.7 25.4 %all-to-all-start.2 = ((f32[256,2,128]{2,1,0:T(2,128)}), f32[256,2,128]{2,1,0:T(2,128)S(1)}, u32[]{:S(2)}, u32[]{:S(2)}) async-start(f32[256,2,128]{2,1,0:T(2,128)} %pad.4), calls=%async_computation.2 | async-start | bytes 524288 | tf_op jit(solution)/shard_map/all_to_all | solution.py:362
  197.2 25.4 %collective-permute-start.2 = (bf16[32,64,128]{2,1,0:T(8,128)(2,1)S(1)}, bf16[32,64,128]{2,1,0:T(8,128)(2,1)}, u32[]{:S(2)}, u32[]{:S(2)}) collective-permute-start(bf16[32,64,128]{2,1,0:T(8,128)(2,1)S(1)} %select_convert_fusion), channel_id=1, source_target_pairs={{0,128},{128,0},{1,129},{129,1},{2,130},{130,2},{3,131},{131,3},{4... | collective-permute-start | bytes 1572872 | tf_op jit(solution)/shard_map/ppermute | solution.py:388
  212.2 21.8 %all-to-all-start.3 = ((f32[256,2,128]{2,1,0:T(2,128)}), f32[256,2,128]{2,1,0:T(2,128)S(1)}, u32[]{:S(2)}, u32[]{:S(2)}) async-start(f32[256,2,128]{2,1,0:T(2,128)} %broadcast_in_dim.10), calls=%async_computation.3 | async-start | bytes 524288 | tf_op jit(solution)/shard_map/all_to_all | solution.py:362
  218.2 7.5 %copy-start.8 = (f32[3,16,4096]{2,1,0:T(8,128)S(1)}, f32[3,16,4096]{2,1,0:T(8,128)}, u32[]{:S(2)}) copy-start(f32[3,16,4096]{2,1,0:T(8,128)} %copy-done.7) | copy-start | bytes 2359300
  218.2 7.5 %collective-permute-start.1 = (f32[8,4096]{1,0:T(8,128)S(1)}, f32[8,4096]{1,0:T(8,128)S(1)}, u32[]{:S(2)}, u32[]{:S(2)}) collective-permute-start(f32[8,4096]{1,0:T(8,128)S(1)} %copy-done.13), channel_id=1, source_target_pairs={{1,0},{2,1},{3,2},{4,3},{5,4},{6,5},{7,6},{8,7},{9,8},{10,9},{11,1... | collective-permute-start | bytes 393224 | tf_op jit(solution)/shard_map/ppermute | solution.py:358
where the time goes:
time: 235 us
  waiting for transfers between devices  107 us (46%)
  Pallas kernels  55.9 us (24%)
  starting transfers between devices  52.6 us (22%)
  local copies, waits for them, and re-layouts  14.9 us (6%)
  other arithmetic  3.22 us (1%)
    all_to_all x4, waiting for transfers between devices, exchanged(): return lax.all_to_all(value, axes, split_axis=0, concat_axis=0, tiled=True)  105 us
    all_to_all x4, starting transfers between devices, exchanged(): return lax.all_to_all(value, axes, split_axis=0, concat_axis=0, tiled=True)  40.4 us
    pallas_call x1, Pallas kernels, convolve(): pl.pallas_call(functools.partial(conv_kernel, group=2), grid=(width // bl...  30.5 us
    unnamed x34, local copies, waits for them, and re-layouts  12.5 us
    pallas_call x1, Pallas kernels, stream_grads(): pl.pallas_call(grads_kernel, grid=(channels // block,), in_specs=[pl.Bloc...  10 us
    pallas_call x1, Pallas kernels, spectrum(): pl.pallas_call(spectrum_kernel, grid=(width // block,), in_specs=[pl.Bloc...  9.37 us
    ppermute x2, starting transfers between devices, passed_along(): lax.ppermute(value, 'ctx', [(source, source + steps) for source in range(...  9.18 us
    pallas_call x1, Pallas kernels, gates(): pl.pallas_call(gate_kernel, grid=(channels // block,), in_specs=[pl.Block...  5.09 us
  transfers between devices with their start and end apart: 7, of which 6 were waited for; matrix products, arithmetic and copies ran while one was open for 3% of the time, Pallas kernels for 4%

commit v1 on v0

--- a/solution.py
+++ b/solution.py
@@ -36,8 +36,11 @@
         "fwd_a": np.concatenate(rounded(fwd_a), axis=1),
         "turn": turn,
         "fwd_b": np.stack(rounded(fwd_b)),
+        "fwd_b_high": np.stack(rounded(fwd_b)[:1]),
         "inv_b": np.stack(rounded(inv_b)),
+        "inv_b_high": np.stack(rounded(inv_b)[:1]),
         "inv_a": np.stack(rounded(inv_a)),
+        "inv_a_high": np.stack(rounded(inv_a)[:1]),
     }
 
 
@@ -52,6 +55,10 @@
 
 def halves(value):
     return value[:, :ROWS], value[:, ROWS:]
+
+
+def held(value):
+    return pltpu.with_memory_space_constraint(value, pltpu.HBM)
 
 
 def params(mib=48):
@@ -91,7 +98,7 @@
         out_specs=pl.BlockSpec((8, channels), lambda i: (0, 0)),
         out_shape=jax.ShapeDtypeStruct((8, channels), jnp.float32),
         compiler_params=params(16),
-    )(proj)
+    )(held(proj))
 
 
 def gate_kernel(proj_ref, edge_ref, taps_ref, grad_ref, out_ref, ext_ref):
@@ -101,12 +108,12 @@
     grad_gate = grad_ref[...].astype(jnp.float32) * query
     count, _, width, _ = out_ref.shape
     for at, rows in enumerate((gated, grad_gate)):
-        out_ref[:, at] = rows.T.astype(jnp.bfloat16).reshape(count, width, ROWS)
+        out_ref[:, at] = rows.astype(jnp.bfloat16).T.reshape(count, width, ROWS)
 
 
 def gates(proj, edge, taps, grad_out, width):
     channels = proj.shape[-1]
-    block = min(512, channels)
+    block = min(1024, channels)
     return pl.pallas_call(
         gate_kernel,
         grid=(channels // block,),
@@ -120,7 +127,7 @@
         out_shape=jax.ShapeDtypeStruct((channels // width, 2, width, ROWS), jnp.bfloat16),
         scratch_shapes=[pltpu.VMEM((3, ROWS + 8, block), jnp.float32)],
         compiler_params=params(32),
-    )(proj, edge, taps, grad_out)
+    )(held(proj), edge, taps, held(grad_out))
 
 
 def spectrum_kernel(filter_ref, fwd_a_ref, turn_ref, fwd_b_ref, out_ref):
@@ -158,7 +165,7 @@
             whole((2, 2 * ROWS, 2 * ROWS)),
         ],
         out_specs=pl.BlockSpec((block, ROWS, 2 * ROWS), lambda i: (i, 0, 0)),
-        out_shape=jax.ShapeDtypeStruct((width, ROWS, 2 * ROWS), jnp.float32),
+        out_shape=pltpu.HBM((width, ROWS, 2 * ROWS), jnp.float32),
         compiler_params=params(32),
         cost_estimate=pl.CostEstimate(
             flops=width * 5 * 2 * (2 * ROWS) ** 3, bytes_accessed=width * 3 * 4 * ROWS**2,
@@ -167,100 +174,123 @@
     )(filter_sq, tab["fwd_a"], tab["turn"], tab["fwd_b"])
 
 
+def apply_right(rows, table_ref):
+    total = dot(rows, table_ref[0])
+    for term in range(1, table_ref.shape[0]):
+        total += dot(rows, table_ref[term])
+    return total
+
+
+def apply_left(table_ref, columns):
+    total = dot(table_ref[0], columns)
+    for term in range(1, table_ref.shape[0]):
+        total += dot(table_ref[term], columns)
+    return total
+
+
+def side(left, right):
+    return jnp.concatenate([left.astype(jnp.bfloat16), right.astype(jnp.bfloat16)], axis=1)
+
+
+def turned_back(spectra, inv_b_ref, inv_a_ref, cos_w, sin_w):
+    v = apply_right(spectra, inv_b_ref)
+    parts_re, parts_im = [], []
+    for at in range(spectra.shape[0] // ROWS):
+        v_re, v_im = halves(v[at * ROWS : (at + 1) * ROWS])
+        parts_re.append((v_re * cos_w + v_im * sin_w).astype(jnp.bfloat16))
+        parts_im.append((v_im * cos_w - v_re * sin_w).astype(jnp.bfloat16))
+    parts = [jnp.concatenate(parts_re, axis=1), jnp.concatenate(parts_im, axis=1)]
+    return apply_left(inv_a_ref, jnp.concatenate(parts, axis=0))
+
+
 def conv_kernel(
     in_ref, spec_ref, fwd_a_ref, turn_ref, fwd_b_ref, inv_b_ref, inv_a_ref,
-    out_ref, lag_ref, rows_ref, *, group,
+    out_ref, lag_ref, rows_ref, outs_ref, *, group,
 ):
     block = in_ref.shape[2]
     for at in range(2):
         rows_ref[at] = in_ref[:, at].astype(jnp.float32).reshape(ROWS * block, ROWS)
     cos_w, sin_w = turn_ref[0], turn_ref[1]
 
-    def one(ch):
-        strided = pl.ds(ch, ROWS, stride=block)
-        both = jnp.concatenate(
-            [rows_ref[at, strided, :].astype(jnp.bfloat16) for at in range(2)], axis=1
-        )
-        y = dot(fwd_a_ref[...], jnp.concatenate([both, both], axis=0))
-        stacked = []
-        for at in range(2):
+    def some(step, carry):
+        chans = [step * group + at for at in range(group)]
+        places = [(at, pl.ds(ch, ROWS, stride=block)) for ch in chans for at in range(2)]
+        rows = [rows_ref[at, strided, :].astype(jnp.bfloat16) for at, strided in places]
+        columns = jnp.concatenate(rows, axis=1)
+        y = dot(fwd_a_ref[...], jnp.concatenate([columns, columns], axis=0))
+        turned = []
+        for at in range(2 * group):
             y_re = y[:ROWS, at * ROWS : (at + 1) * ROWS]
             y_im = y[ROWS:, at * ROWS : (at + 1) * ROWS]
-            stacked.append(
-                jnp.concatenate(
-                    [
-                        (y_re * cos_w - y_im * sin_w).astype(jnp.bfloat16),
-                        (y_re * sin_w + y_im * cos_w).astype(jnp.bfloat16),
-                    ],
-                    axis=1,
-                )
-            )
-        stacked = jnp.concatenate(stacked, axis=0)
-        z = dot(stacked, fwd_b_ref[0]) + dot(stacked, fwd_b_ref[1])
-        x_re, x_im = halves(z[:ROWS])
-        g_re, g_im = halves(z[ROWS:])
-        h_re, h_im = halves(spec_ref[ch])
-        products = jnp.concatenate(
-            [
-                jnp.concatenate([re.astype(jnp.bfloat16), im.astype(jnp.bfloat16)], axis=1)
-                for re, im in (
-                    (x_re * h_re - x_im * h_im, x_re * h_im + x_im * h_re),
-                    (h_re * g_re + h_im * g_im, h_re * g_im - h_im * g_re),
-                    (g_re * x_re + g_im * x_im, g_im * x_re - g_re * x_im),
-                )
-            ],
-            axis=0,
-        )
-        v = dot(products, inv_b_ref[0]) + dot(products, inv_b_ref[1])
-        parts_re, parts_im = [], []
-        for at in range(3):
-            v_re, v_im = halves(v[at * ROWS : (at + 1) * ROWS])
-            parts_re.append((v_re * cos_w + v_im * sin_w).astype(jnp.bfloat16))
-            parts_im.append((v_im * cos_w - v_re * sin_w).astype(jnp.bfloat16))
-        turned = jnp.concatenate(
-            [jnp.concatenate(parts_re, axis=1), jnp.concatenate(parts_im, axis=1)], axis=0
-        )
-        res = dot(inv_a_ref[0], turned) + dot(inv_a_ref[1], turned)
-        for at in range(2):
-            rows_ref[at, strided, :] = res[:, at * ROWS : (at + 1) * ROWS]
-        lag_ref[ch] = res[:, 2 * ROWS :]
-
-    def some(step, carry):
-        for at in range(group):
-            one(step * group + at)
+            turned.append(side(y_re * cos_w - y_im * sin_w, y_re * sin_w + y_im * cos_w))
+        z = apply_right(jnp.concatenate(turned, axis=0), fwd_b_ref)
+        products = []
+        for at, ch in enumerate(chans):
+            x_re, x_im = halves(z[2 * at * ROWS : (2 * at + 1) * ROWS])
+            g_re, g_im = halves(z[(2 * at + 1) * ROWS : (2 * at + 2) * ROWS])
+            h_re, h_im = halves(spec_ref[ch])
+            lag_ref[ch] = side(g_re * x_re + g_im * x_im, g_im * x_re - g_re * x_im)
+            products.append(side(x_re * h_re - x_im * h_im, x_re * h_im + x_im * h_re))
+            products.append(side(h_re * g_re + h_im * g_im, h_re * g_im - h_im * g_re))
+        res = turned_back(jnp.concatenate(products, axis=0), inv_b_ref, inv_a_ref, cos_w, sin_w)
+        for column, (at, strided) in enumerate(places):
+            outs_ref[at, strided, :] = res[:, column * ROWS : (column + 1) * ROWS]
         return carry
 
     lax.fori_loop(0, block // group, some, 0)
     for at in range(2):
-        out_ref[:, at] = rows_ref[at].astype(jnp.bfloat16).reshape(ROWS, block, ROWS)
-
-
-def convolve(received, spec, tab):
+        out_ref[:, at] = outs_ref[at].astype(jnp.bfloat16).reshape(ROWS, block, ROWS)
+
+
+def convolve(received, spec, tab, group=8, block=16):
     width = received.shape[2]
-    block = min(16, width)
-    return pl.pallas_call(
-        functools.partial(conv_kernel, group=2),
+    names = ("fwd_a", "turn", "fwd_b_high", "inv_b_high", "inv_a_high")
+    return pl.pallas_call(
+        functools.partial(conv_kernel, group=group),
         grid=(width // block,),
         in_specs=[
             pl.BlockSpec((ROWS, 2, block, ROWS), lambda i: (0, 0, i, 0)),
             pl.BlockSpec((block, ROWS, 2 * ROWS), lambda i: (i, 0, 0)),
-            whole((2 * ROWS, 2 * ROWS)),
-            whole((2, ROWS, ROWS)),
-            whole((2, 2 * ROWS, 2 * ROWS)),
-            whole((2, 2 * ROWS, 2 * ROWS)),
-            whole((2, ROWS, 2 * ROWS)),
-        ],
+        ]
+        + [whole(tab[name].shape) for name in names],
         out_specs=[
             pl.BlockSpec((ROWS, 2, block, ROWS), lambda i: (0, 0, i, 0)),
-            pl.BlockSpec((block, ROWS, ROWS), lambda i: (i, 0, 0)),
+            pl.BlockSpec((block, ROWS, 2 * ROWS), lambda i: (i, 0, 0)),
         ],
         out_shape=[
-            jax.ShapeDtypeStruct((ROWS, 2, width, ROWS), jnp.bfloat16),
-            jax.ShapeDtypeStruct((width, ROWS, ROWS), jnp.float32),
-        ],
-        scratch_shapes=[pltpu.VMEM((2, ROWS * block, ROWS), jnp.float32)],
-        compiler_params=params(56),
-    )(received, spec, tab["fwd_a"], tab["turn"], tab["fwd_b"], tab["inv_b"], tab["inv_a"])
+            pltpu.HBM((ROWS, 2, width, ROWS), jnp.bfloat16),
+            pltpu.HBM((width, ROWS, 2 * ROWS), jnp.bfloat16),
+        ],
+        scratch_shapes=[pltpu.VMEM((2, ROWS * block, ROWS), jnp.float32)] * 2,
+        compiler_params=params(40),
+    )(received, held(spec), *(tab[name] for name in names))
+
+
+def lag_kernel(products_ref, turn_ref, inv_b_ref, inv_a_ref, out_ref):
+    count = products_ref.shape[0]
+    products = products_ref[...].reshape(count * ROWS, 2 * ROWS)
+    res = turned_back(products, inv_b_ref, inv_a_ref, turn_ref[0], turn_ref[1])
+    for ch in range(count):
+        out_ref[ch] = res[:, ch * ROWS : (ch + 1) * ROWS]
+
+
+def lags(products, tab):
+    width = products.shape[0]
+    block = min(8, width)
+    names = ("turn", "inv_b", "inv_a")
+    return pl.pallas_call(
+        lag_kernel,
+        grid=(width // block,),
+        in_specs=[pl.BlockSpec((block, ROWS, 2 * ROWS), lambda i: (i, 0, 0))]
+        + [whole(tab[name].shape) for name in names],
+        out_specs=pl.BlockSpec((block, ROWS, ROWS), lambda i: (i, 0, 0)),
+        out_shape=jax.ShapeDtypeStruct((width, ROWS, ROWS), jnp.float32),
+        compiler_params=params(32),
+        cost_estimate=pl.CostEstimate(
+            flops=width * 4 * 2 * (2 * ROWS) ** 3, bytes_accessed=width * 8 * ROWS**2,
+            transcendentals=0,
+        ),
+    )(products, *(tab[name] for name in names))
 
 
 def grads_kernel(
@@ -270,11 +300,12 @@
     fill_ext(ext_ref, proj_ref, edge_ref)
     block = grad_ref.shape[1]
     conv, corr = (
-        ret_ref[:, at].reshape(block, ROWS).astype(jnp.float32).T for at in range(2)
+        ret_ref[:, at].reshape(block, ROWS).T.astype(jnp.float32) for at in range(2)
     )
     key, value = (feature(ext_ref, taps_ref, stream) for stream in (1, 2))
     grads = (grad_ref[...].astype(jnp.float32) * conv, corr * value, corr * key)
     first_ref[...] = jnp.zeros_like(first_ref)
+    sums_ref[...] = jnp.zeros_like(sums_ref)
     for stream in range(3):
         grads_ref[stream, pl.ds(0, ROWS), :] = grads[stream]
         grads_ref[stream, pl.ds(ROWS, 8), :] = jnp.zeros((8, block), jnp.float32)
@@ -305,22 +336,22 @@
         ],
         out_specs=[
             pl.BlockSpec((3, ROWS, block), lambda i: (0, 0, i)),
-            pl.BlockSpec((9, block // ROWS, ROWS), lambda i: (0, i, 0)),
+            pl.BlockSpec((16, block // ROWS, ROWS), lambda i: (0, i, 0)),
             pl.BlockSpec((8, block), lambda i: (0, i)),
             pl.BlockSpec((3, 16, block), lambda i: (0, 0, i)),
         ],
         out_shape=[
             jax.ShapeDtypeStruct((3, ROWS, channels), jnp.bfloat16),
-            jax.ShapeDtypeStruct((9, channels // ROWS, ROWS), jnp.float32),
-            jax.ShapeDtypeStruct((8, channels), jnp.float32),
-            jax.ShapeDtypeStruct((3, 16, channels), jnp.float32),
+            jax.ShapeDtypeStruct((16, channels // ROWS, ROWS), jnp.float32),
+            pltpu.HBM((8, channels), jnp.float32),
+            pltpu.HBM((3, 16, channels), jnp.float32),
         ],
         scratch_shapes=[
             pltpu.VMEM((3, ROWS + 8, block), jnp.float32),
             pltpu.VMEM((3, ROWS + 8, block), jnp.float32),
         ],
         compiler_params=params(48),
-    )(returned, proj, edge, taps, grad_out)
+    )(returned, held(proj), edge, taps, held(grad_out))
 
 
 def last_kernel(whole_ref, last_ref, later_ref, taps_ref, out_ref):
@@ -363,13 +394,12 @@
 
 
 def sum_everywhere(sums):
-    taps, blocks, _ = sums.shape
+    channels = sums.shape[1] * ROWS
     devices = lax.axis_size("dp") * lax.axis_size("ctx")
-    owners = taps * blocks // 2
-    pieces = jnp.pad(sums.reshape(owners, 2, ROWS), ((0, devices - owners), (0, 0), (0, 0)))
+    pieces = sums.reshape(devices, 2, ROWS)
     own = jnp.sum(exchanged(pieces, ("dp", "ctx")), axis=0)
-    spread = exchanged(jnp.broadcast_to(own[None], (devices, 2, ROWS)), ("dp", "ctx"))
-    return spread[:owners].reshape(3, 3, blocks * ROWS)
+    spread = exchanged(jnp.broadcast_to(own[None], pieces.shape), ("dp", "ctx"))
+    return spread.reshape(16, channels)[:9].reshape(3, 3, channels)
 
 
 def local(projected, short_taps, long_filter, grad_out):
@@ -381,8 +411,9 @@
     sent = gates(proj, edge, short_taps, grad_rows, width)
     received = exchanged(sent, "ctx")
     spec = spectrum(long_filter.reshape(width, ROWS, ROWS), tab)
-    results, lag = convolve(received, spec, tab)
+    results, products = convolve(received, spec, tab)
     returned = exchanged(results, "ctx")
+    lag = lags(products, tab)
     second = lax.axis_index("dp") == 1
     lower, upper = lag[:, : ROWS // 2], lag[:, ROWS // 2 :]
     other = lax.ppermute(

time: 235 us -> 209 us (0.89)
  Pallas kernels: 55.9 us -> 42.3 us
  local copies, waits for them, and re-layouts: 14.9 us -> 8.18 us
  waiting for transfers between devices: 107 us -> 102 us
    pallas_call x1 -> x2, Pallas kernels: 30.5 us -> 15 us  [the longest x1 11.5 us: convolve(): pl.pallas_call(functools.partial(conv_kernel, group=group), grid=(width /...]
    unnamed x34 -> x30, local copies, waits for them, and re-layouts: 12.5 us -> 6.58 us
    all_to_all x4, waiting for transfers between devices: 105 us -> 99.5 us  [exchanged(): return lax.all_to_all(value, axes, split_axis=0, concat_axis=0, tiled=True)]
  transfers between devices with their start and end apart: 7 -> 7, of which waited for: 6 -> 6; matrix products, arithmetic and copies ran while one was open for 3% -> 4% of each run, Pallas kernels for 4% -> 7%
where the time goes in v1:
time: 209 us
  waiting for transfers between devices  102 us (49%)
  starting transfers between devices  52.3 us (25%)
  Pallas kernels  42.3 us (20%)
  local copies, waits for them, and re-layouts  8.18 us (4%)
  other arithmetic  3.22 us (2%)
    all_to_all x4, waiting for transfers between devices, exchanged(): return lax.all_to_all(value, axes, split_axis=0, concat_axis=0, tiled=True)  99.5 us
    all_to_all x4, starting transfers between devices, exchanged(): return lax.all_to_all(value, axes, split_axis=0, concat_axis=0, tiled=True)  40.2 us
    pallas_call x1, Pallas kernels, convolve(): pl.pallas_call(functools.partial(conv_kernel, group=group), grid=(width /...  11.5 us
    pallas_call x1, Pallas kernels, spectrum(): pl.pallas_call(spectrum_kernel, grid=(width // block,), in_specs=[pl.Bloc...  10.4 us
    pallas_call x1, Pallas kernels, stream_grads(): pl.pallas_call(grads_kernel, grid=(channels // block,), in_specs=[pl.Bloc...  9.25 us
    ppermute x2, starting transfers between devices, passed_along(): lax.ppermute(value, 'ctx', [(source, source + steps) for source in range(...  8.92 us
    unnamed x30, local copies, waits for them, and re-layouts  6.58 us
    pallas_call x1, Pallas kernels, gates(): pl.pallas_call(gate_kernel, grid=(channels // block,), in_specs=[pl.Block...  5.64 us
  transfers between devices with their start and end apart: 7, of which 6 were waited for; matrix products, arithmetic and copies ran while one was open for 4% of the time, Pallas kernels for 7%

profile of v1, /device:TPU:1, one launch (start us, length us, event | category | flops | bytes accessed | tf_op | source)
XLA Modules:
  0.0 208.5 jit_solution(15888533231849754623)
XLA Ops:
  0.6 0.0 copy-start.2
  0.6 1.1 shard_map.139
  1.7 4.6 %collective-permute-start = (f32[8,4096]{1,0:T(8,128)S(1)}, f32[8,4096]{1,0:T(8,128)S(1)}, u32[]{:S(2)}, u32[]{:S(2)}) collective-permute-start(f32[8,4096]{1,0:T(8,128)S(1)} %shard_map.139), channel_id=1, source_target_pairs={{0,1},{1,2},{2,3},{3,4},{4,5},{5,6},{6,7},{7,8},{8,9},{9,10},{10,1... | collective-permute-start | bytes 393224 | tf_op jit(solution)/shard_map/ppermute | solution.py:389
  6.3 1.9 collective-permute-done.edge_ref
  8.2 0.0 copy-done.2
  8.3 5.6 %shard_map.140 = bf16[128,2,32,128]{3,2,1,0:T(8,128)(2,1)} custom-call(bf16[3,128,4096]{2,1,0:T(8,128)(2,1)} %bitcast.14, f32[8,4096]{1,0:T(8,128)S(1)} %collective-permute-done.edge_ref, f32[3,3,4096]{2,1,0:T(4,128)S(1)} %copy-done.2, bf16[128,4096]{1,0:T(8,128)(2,1)} %bitcast.16), custom_call_target="tpu_custom_call" | custom-call | tf_op jit(solution)/shard_map/pallas_call | solution.py:117
  13.9 15.6 %all-to-all-start = ((bf16[128,2,32,128]{3,2,1,0:T(8,128)(2,1)}), bf16[128,2,32,128]{3,2,1,0:T(8,128)(2,1)S(1)}, u32[]{:S(2)}, u32[]{:S(2)}) async-start(bf16[128,2,32,128]{3,2,1,0:T(8,128)(2,1)} %shard_map.140), calls=%async_computation | async-start | bytes 4194304 | tf_op jit(solution)/shard_map/all_to_all | solution.py:393
  29.5 0.0 copy-start.4
  29.5 0.0 copy-start.5
  29.6 0.0 copy-start.11
  29.6 2.0 copy.17
  31.6 0.0 copy-done.4
  31.6 0.0 copy-done.5
  31.6 0.0 copy-done.11
  31.6 0.0 copy-start.6
  31.6 0.0 copy-start.7
  31.7 0.0 copy-start.8
  31.7 10.4 %shard_map.141.spec_ref = f32[32,128,256]{2,1,0:T(8,128)} custom-call(f32[32,128,128]{2,1,0:T(8,128)S(1)} %bitcast.12, bf16[256,256]{1,0:T(8,128)(2,1)S(1)} %copy-done.5, f32[2,128,128]{2,1,0:T(8,128)S(1)} %copy-done.4, bf16[2,256,256]{2,1,0:T(8,128)(2,1)S(1)} %copy-done.11), custom_call_target="tpu_custom_call" | custom-call | flops 5368709120 | bytes 6291456 | tf_op jit(solution)/shard_map/pallas_call | solution.py:158
  42.0 37.7 %all-to-all-done.in_ref = bf16[128,2,32,128]{3,2,1,0:T(8,128)(2,1)S(1)} async-done(((bf16[128,2,32,128]{3,2,1,0:T(8,128)(2,1)}), bf16[128,2,32,128]{3,2,1,0:T(8,128)(2,1)S(1)}, u32[]{:S(2)}, u32[]{:S(2)}) %all-to-all-start) | async-done | bytes 2097184 | tf_op jit(solution)/shard_map/all_to_all | solution.py:393
  79.7 0.0 copy-done.6
  79.7 0.0 copy-done.7
  79.7 0.0 copy-done.8
  79.7 11.5 %shard_map.142 = (bf16[128,2,32,128]{3,2,1,0:T(8,128)(2,1)}, bf16[32,128,256]{2,1,0:T(8,128)(2,1)}) custom-call(bf16[128,2,32,128]{3,2,1,0:T(8,128)(2,1)S(1)} %all-to-all-done.in_ref, f32[32,128,256]{2,1,0:T(8,128)} %shard_map.141.spec_ref, bf16[256,256]{1,0:T(8,128)(2,1)S(1)} %copy-done.5, f32[2,128,128]{2,1,0:T(8,128)S(1)} %copy-done.4, ...), custom_call_target="tpu_custom_call" | custom-call | tf_op jit(solution)/shard_map/pallas_call | solution.py:248
  91.3 8.9 %all-to-all-start.1 = ((bf16[128,2,32,128]{3,2,1,0:T(8,128)(2,1)}), bf16[128,2,32,128]{3,2,1,0:T(8,128)(2,1)S(1)}, u32[]{:S(2)}, u32[]{:S(2)}) async-start(bf16[128,2,32,128]{3,2,1,0:T(8,128)(2,1)} %get-tuple-element.9), calls=%async_computation.1 | async-start | bytes 4194304 | tf_op jit(solution)/shard_map/all_to_all | solution.py:393
  100.2 0.0 copy-done.10
  100.2 0.0 copy-done.12
  100.2 0.0 copy-start.9
  100.3 1.6 copy-done.9
  101.8 3.5 %shard_map.145 = f32[32,128,128]{2,1,0:T(8,128)S(1)} custom-call(bf16[32,128,256]{2,1,0:T(8,128)(2,1)S(1)} %copy-done.9, f32[2,128,128]{2,1,0:T(8,128)S(1)} %copy-done.4, bf16[2,256,256]{2,1,0:T(8,128)(2,1)S(1)} %copy-done.10, bf16[2,128,256]{2,1,0:T(8,128)(2,1)S(1)} %copy-done.12), custom_call_target="tpu_custom_call" | custom-call | flops 4294967296 | bytes 4194304 | tf_op jit(solution)/shard_map/pallas_call | solution.py:281
  105.4 1.3 copy-done
  106.7 43.7 %all-to-all-done.1.ret_ref = bf16[128,2,32,128]{3,2,1,0:T(8,128)(2,1)S(1)} async-done(((bf16[128,2,32,128]{3,2,1,0:T(8,128)(2,1)}), bf16[128,2,32,128]{3,2,1,0:T(8,128)(2,1)S(1)}, u32[]{:S(2)}, u32[]{:S(2)}) %all-to-all-start.1) | async-done | bytes 2097184 | tf_op jit(solution)/shard_map/all_to_all | solution.py:393
  150.4 9.2 %shard_map.143 = (bf16[3,128,4096]{2,1,0:T(8,128)(2,1)}, f32[16,32,128]{2,1,0:T(8,128)}, f32[8,4096]{1,0:T(8,128)}, f32[3,16,4096]{2,1,0:T(8,128)}) custom-call(bf16[128,2,32,128]{3,2,1,0:T(8,128)(2,1)S(1)} %all-to-all-done.1.ret_ref, bf16[3,128,4096]{2,1,0:T(8,128)(2,1)} %bitcast.15, f32[8,4096]{1,0:T(8,128)S(1)} %collective-permute-done.edge_ref, ...), custom_call_target="tpu_custom_call" | custom-call | tf_op jit(solution)/shard_map/pallas_call | solution.py:327
  159.7 9.8 %all-to-all-start.2 = ((f32[256,2,128]{2,1,0:T(2,128)}), f32[256,2,128]{2,1,0:T(2,128)S(1)}, u32[]{:S(2)}, u32[]{:S(2)}) async-start(f32[256,2,128]{2,1,0:T(2,128)} %bitcast.4), calls=%async_computation.2 | async-start | bytes 524288 | tf_op jit(solution)/shard_map/all_to_all | solution.py:393
  169.5 1.7 select_convert_fusion
  171.1 3.2 %collective-permute-start.2 = (bf16[32,64,128]{2,1,0:T(8,128)(2,1)S(1)}, bf16[32,64,128]{2,1,0:T(8,128)(2,1)}, u32[]{:S(2)}, u32[]{:S(2)}) collective-permute-start(bf16[32,64,128]{2,1,0:T(8,128)(2,1)S(1)} %select_convert_fusion), channel_id=1, source_target_pairs={{0,128},{128,0},{1,129},{129,1},{2,130},{130,2},{3,131},{131,3},{4... | collective-permute-start | bytes 1572872 | tf_op jit(solution)/shard_map/ppermute | solution.py:419
  174.3 10.8 %all-to-all-done.2 = f32[256,2,128]{2,1,0:T(2,128)S(1)} async-done(((f32[256,2,128]{2,1,0:T(2,128)}), f32[256,2,128]{2,1,0:T(2,128)S(1)}, u32[]{:S(2)}, u32[]{:S(2)}) %all-to-all-start.2) | async-done | bytes 262176 | tf_op jit(solution)/shard_map/all_to_all | solution.py:393
  185.1 0.3 reduce_sum.9
  185.4 0.8 broadcast_in_dim.10
  186.1 5.8 %all-to-all-start.3 = ((f32[256,2,128]{2,1,0:T(2,128)}), f32[256,2,128]{2,1,0:T(2,128)S(1)}, u32[]{:S(2)}, u32[]{:S(2)}) async-start(f32[256,2,128]{2,1,0:T(2,128)} %broadcast_in_dim.10), calls=%async_computation.3 | async-start | bytes 524288 | tf_op jit(solution)/shard_map/all_to_all | solution.py:393
  192.0 4.3 %collective-permute-start.1 = (f32[8,4096]{1,0:T(8,128)S(1)}, f32[8,4096]{1,0:T(8,128)S(1)}, u32[]{:S(2)}, u32[]{:S(2)}) collective-permute-start(f32[8,4096]{1,0:T(8,128)S(1)} %copy-done.13), channel_id=1, source_target_pairs={{1,0},{2,1},{3,2},{4,3},{5,4},{6,5},{7,6},{8,7},{9,8},{10,9},{11,1... | collective-permute-start | bytes 393224 | tf_op jit(solution)/shard_map/ppermute | solution.py:389
  196.3 0.0 collective-permute-done.2
  196.3 0.0 copy-done.1
  196.3 1.3 convert_add_fusion
  197.6 1.6 copy.20
  199.2 0.3 collective-permute-done.1.later_ref
  199.5 0.9 shard_map.144
  200.4 7.3 %all-to-all-done.3 = f32[256,2,128]{2,1,0:T(2,128)S(1)} async-done(((f32[256,2,128]{2,1,0:T(2,128)}), f32[256,2,128]{2,1,0:T(2,128)S(1)}, u32[]{:S(2)}, u32[]{:S(2)}) %all-to-all-start.3) | async-done | bytes 262176 | tf_op jit(solution)/shard_map/all_to_all | solution.py:393
  207.7 0.8 reshape.24
  (9 shorter events, 0.0 us)
Async XLA Ops:
  0.6 7.6 %copy-start.2 = (f32[3,3,4096]{2,1,0:T(4,128)S(1)}, f32[3,3,4096]{2,1,0:T(4,128)}, u32[]{:S(2)}) copy-start(f32[3,3,4096]{2,1,0:T(4,128)} %taps_ref.5) | copy-start | bytes 442372
  1.7 6.5 %collective-permute-start = (f32[8,4096]{1,0:T(8,128)S(1)}, f32[8,4096]{1,0:T(8,128)S(1)}, u32[]{:S(2)}, u32[]{:S(2)}) collective-permute-start(f32[8,4096]{1,0:T(8,128)S(1)} %shard_map.139), channel_id=1, source_target_pairs={{0,1},{1,2},{2,3},{3,4},{4,5},{5,6},{6,7},{7,8},{8,9},{9,10},{10,1... | collective-permute-start | bytes 393224 | tf_op jit(solution)/shard_map/ppermute | solution.py:389
  13.9 65.8 %all-to-all-start = ((bf16[128,2,32,128]{3,2,1,0:T(8,128)(2,1)}), bf16[128,2,32,128]{3,2,1,0:T(8,128)(2,1)S(1)}, u32[]{:S(2)}, u32[]{:S(2)}) async-start(bf16[128,2,32,128]{3,2,1,0:T(8,128)(2,1)} %shard_map.140), calls=%async_computation | async-start | bytes 4194304 | tf_op jit(solution)/shard_map/all_to_all | solution.py:393
  29.5 2.1 copy-start.4
  29.5 2.1 copy-start.5
  29.6 2.1 copy-start.11
  31.6 48.1 %copy-start.6 = (bf16[1,256,256]{2,1,0:T(8,128)(2,1)S(1)}, bf16[1,256,256]{2,1,0:T(8,128)(2,1)}, u32[]{:S(2)}) copy-start(bf16[1,256,256]{2,1,0:T(8,128)(2,1)} %constant.29.clone.fwd_b_ref) | copy-start | bytes 393220
  31.6 48.1 %copy-start.7 = (bf16[1,256,256]{2,1,0:T(8,128)(2,1)S(1)}, bf16[1,256,256]{2,1,0:T(8,128)(2,1)}, u32[]{:S(2)}) copy-start(bf16[1,256,256]{2,1,0:T(8,128)(2,1)} %constant.30.clone.inv_b_ref) | copy-start | bytes 393220
  31.7 48.1 %copy-start.8 = (bf16[1,128,256]{2,1,0:T(8,128)(2,1)S(1)}, bf16[1,128,256]{2,1,0:T(8,128)(2,1)}, u32[]{:S(2)}) copy-start(bf16[1,128,256]{2,1,0:T(8,128)(2,1)} %constant.31.clone.inv_a_ref) | copy-start | bytes 196612
  91.3 9.0 %copy-start.10 = (bf16[2,256,256]{2,1,0:T(8,128)(2,1)S(1)}, bf16[2,256,256]{2,1,0:T(8,128)(2,1)}, u32[]{:S(2)}) copy-start(bf16[2,256,256]{2,1,0:T(8,128)(2,1)} %constant.32.clone.inv_b_ref) | copy-start | bytes 786436
  91.3 9.0 %copy-start.12 = (bf16[2,128,256]{2,1,0:T(8,128)(2,1)S(1)}, bf16[2,128,256]{2,1,0:T(8,128)(2,1)}, u32[]{:S(2)}) copy-start(bf16[2,128,256]{2,1,0:T(8,128)(2,1)} %constant.33.clone.inv_a_ref) | copy-start | bytes 393220
  91.3 59.1 %all-to-all-start.1 = ((bf16[128,2,32,128]{3,2,1,0:T(8,128)(2,1)}), bf16[128,2,32,128]{3,2,1,0:T(8,128)(2,1)S(1)}, u32[]{:S(2)}, u32[]{:S(2)}) async-start(bf16[128,2,32,128]{3,2,1,0:T(8,128)(2,1)} %get-tuple-element.9), calls=%async_computation.1 | async-start | bytes 4194304 | tf_op jit(solution)/shard_map/all_to_all | solution.py:393
  100.2 1.6 copy-start.9
  105.3 1.3 copy-start
  159.6 32.3 %copy-start.13 = (f32[8,4096]{1,0:T(8,128)S(1)}, f32[8,4096]{1,0:T(8,128)}, u32[]{:S(2)}) copy-start(f32[8,4096]{1,0:T(8,128)} %get-tuple-element.12) | copy-start | bytes 393220
  159.7 36.7 %copy-start.1 = (f32[32,128,128]{2,1,0:T(8,128)S(1)}, f32[32,128,128]{2,1,0:T(8,128)}, u32[]{:S(2)}) copy-start(f32[32,128,128]{2,1,0:T(8,128)} %copy-done) | copy-start | bytes 6291460
  159.7 25.4 %all-to-all-start.2 = ((f32[256,2,128]{2,1,0:T(2,128)}), f32[256,2,128]{2,1,0:T(2,128)S(1)}, u32[]{:S(2)}, u32[]{:S(2)}) async-start(f32[256,2,128]{2,1,0:T(2,128)} %bitcast.4), calls=%async_computation.2 | async-start | bytes 524288 | tf_op jit(solution)/shard_map/all_to_all | solution.py:393
  171.1 25.2 %collective-permute-start.2 = (bf16[32,64,128]{2,1,0:T(8,128)(2,1)S(1)}, bf16[32,64,128]{2,1,0:T(8,128)(2,1)}, u32[]{:S(2)}, u32[]{:S(2)}) collective-permute-start(bf16[32,64,128]{2,1,0:T(8,128)(2,1)S(1)} %select_convert_fusion), channel_id=1, source_target_pairs={{0,128},{128,0},{1,129},{129,1},{2,130},{130,2},{3,131},{131,3},{4... | collective-permute-start | bytes 1572872 | tf_op jit(solution)/shard_map/ppermute | solution.py:419
  186.1 21.6 %all-to-all-start.3 = ((f32[256,2,128]{2,1,0:T(2,128)}), f32[256,2,128]{2,1,0:T(2,128)S(1)}, u32[]{:S(2)}, u32[]{:S(2)}) async-start(f32[256,2,128]{2,1,0:T(2,128)} %broadcast_in_dim.10), calls=%async_computation.3 | async-start | bytes 524288 | tf_op jit(solution)/shard_map/all_to_all | solution.py:393
  192.0 7.5 %copy-start.3 = (f32[3,16,4096]{2,1,0:T(8,128)S(1)}, f32[3,16,4096]{2,1,0:T(8,128)}, u32[]{:S(2)}) copy-start(f32[3,16,4096]{2,1,0:T(8,128)} %get-tuple-element.11.last_ref) | copy-start | bytes 2359300
  192.0 7.5 %collective-permute-start.1 = (f32[8,4096]{1,0:T(8,128)S(1)}, f32[8,4096]{1,0:T(8,128)S(1)}, u32[]{:S(2)}, u32[]{:S(2)}) collective-permute-start(f32[8,4096]{1,0:T(8,128)S(1)} %copy-done.13), channel_id=1, source_target_pairs={{1,0},{2,1},{3,2},{4,3},{5,4},{6,5},{7,6},{8,7},{9,8},{10,9},{11,1... | collective-permute-start | bytes 393224 | tf_op jit(solution)/shard_map/ppermute | solution.py:389

commit v2 on v1

--- a/solution.py
+++ b/solution.py
@@ -65,21 +65,10 @@
     return pltpu.CompilerParams(vmem_limit_bytes=mib * MIB)
 
 
-def shifted(ext_ref, stream, tap):
-    return ext_ref[stream, pl.ds(8 - tap, ROWS), :]
-
-
 def fill_ext(ext_ref, proj_ref, edge_ref):
     for stream in range(3):
         ext_ref[stream, pl.ds(8, ROWS), :] = proj_ref[stream].astype(jnp.float32)
         ext_ref[stream, pl.ds(6, 2), :] = edge_ref[pl.ds(2 * stream, 2), :]
-
-
-def feature(ext_ref, taps_ref, stream):
-    total = taps_ref[stream, pl.ds(0, 1), :] * shifted(ext_ref, stream, 0)
-    for tap in (1, 2):
-        total += taps_ref[stream, pl.ds(tap, 1), :] * shifted(ext_ref, stream, tap)
-    return total
 
 
 def edge_kernel(proj_ref, out_ref):
@@ -101,25 +90,52 @@
     )(held(proj))
 
 
-def gate_kernel(proj_ref, edge_ref, taps_ref, grad_ref, out_ref, ext_ref):
-    fill_ext(ext_ref, proj_ref, edge_ref)
-    query, key, value = (feature(ext_ref, taps_ref, stream) for stream in range(3))
-    gated = key * value
-    grad_gate = grad_ref[...].astype(jnp.float32) * query
-    count, _, width, _ = out_ref.shape
-    for at, rows in enumerate((gated, grad_gate)):
-        out_ref[:, at] = rows.astype(jnp.bfloat16).T.reshape(count, width, ROWS)
-
-
-def gates(proj, edge, taps, grad_out, width):
+STEP = 32
+
+
+def lanes_of(width):
+    return [pl.ds(at, ROWS) for at in range(0, width, ROWS)]
+
+
+def inputs_at(ext_ref, stream, row, lanes):
+    rows = ext_ref[stream, pl.ds(row, STEP + 8), lanes]
+    return [rows[8:]] + [pltpu.roll(rows, tap, 0)[8:] for tap in (1, 2)]
+
+
+def filtered(taps_ref, stream, lanes, shifted):
+    rows = taps_ref[stream, :, lanes]
+    return sum(rows[tap : tap + 1] * shifted[tap] for tap in range(3))
+
+
+def gate_kernel(proj_ref, taps_ref, grad_ref, out_ref, ext_ref):
+    for stream in range(3):
+        ext_ref[stream, pl.ds(8, ROWS), :] = proj_ref[stream].astype(jnp.float32)
+        ext_ref[stream, pl.ds(0, 8), :] = jnp.zeros((8, grad_ref.shape[1]), jnp.float32)
+    width = out_ref.shape[2]
+    per = ROWS // width
+    for at, lanes in enumerate(lanes_of(grad_ref.shape[1])):
+        gated, grad_gate = [], []
+        for row in range(0, ROWS, STEP):
+            query, key, value = (
+                filtered(taps_ref, stream, lanes, inputs_at(ext_ref, stream, row, lanes))
+                for stream in range(3)
+            )
+            grad = grad_ref[pl.ds(row, STEP), lanes].astype(jnp.float32)
+            gated.append((key * value).astype(jnp.bfloat16))
+            grad_gate.append((grad * query).astype(jnp.bfloat16))
+        for which, parts in enumerate((gated, grad_gate)):
+            turned = jnp.concatenate(parts, axis=0).T
+            out_ref[pl.ds(at * per, per), which] = turned.reshape(per, width, ROWS)
+
+
+def gates(proj, taps, grad_out, width):
     channels = proj.shape[-1]
-    block = min(1024, channels)
+    block = min(2048, channels)
     return pl.pallas_call(
         gate_kernel,
         grid=(channels // block,),
         in_specs=[
             pl.BlockSpec((3, ROWS, block), lambda i: (0, 0, i)),
-            pl.BlockSpec((8, block), lambda i: (0, i)),
             pl.BlockSpec((3, 3, block), lambda i: (0, 0, i)),
             pl.BlockSpec((ROWS, block), lambda i: (0, i)),
         ],
@@ -127,7 +143,51 @@
         out_shape=jax.ShapeDtypeStruct((channels // width, 2, width, ROWS), jnp.bfloat16),
         scratch_shapes=[pltpu.VMEM((3, ROWS + 8, block), jnp.float32)],
         compiler_params=params(32),
-    )(held(proj), edge, taps, held(grad_out))
+        cost_estimate=pl.CostEstimate(
+            flops=40 * ROWS * channels, bytes_accessed=12 * ROWS * channels, transcendentals=0
+        ),
+    )(held(proj), taps, held(grad_out))
+
+
+def head_kernel(rough_ref, proj_ref, edge_ref, taps_ref, grad_ref, out_ref):
+    per, _, width, _ = out_ref.shape
+    block = per * width
+    features = []
+    for stream in range(3):
+        before = edge_ref[pl.ds(2 * stream, 2), :]
+        rows = jnp.concatenate([before, proj_ref[stream].astype(jnp.float32)[:2]], axis=0)
+        features.append(
+            sum(taps_ref[stream, pl.ds(tap, 1), :] * rows[2 - tap : 4 - tap] for tap in range(3))
+        )
+    query, key, value = features
+    grad = grad_ref[...].astype(jnp.float32)[:2]
+    below = jnp.zeros((ROWS - 2, block), jnp.float32)
+    head = lax.broadcasted_iota(jnp.int32, (block, ROWS), 1) < 2
+    for which, rows in enumerate((key * value, grad * query)):
+        turned = jnp.concatenate([rows, below], axis=0).astype(jnp.bfloat16).T
+        kept = rough_ref[:, which].reshape(block, ROWS)
+        out_ref[:, which] = jnp.where(head, turned, kept).reshape(per, width, ROWS)
+
+
+def headed(rough, proj, edge, taps, grad_out):
+    channels = proj.shape[-1]
+    width = rough.shape[2]
+    block = min(2048, channels)
+    shape = (block // width, 2, width, ROWS)
+    return pl.pallas_call(
+        head_kernel,
+        grid=(channels // block,),
+        in_specs=[
+            pl.BlockSpec(shape, lambda i: (i, 0, 0, 0)),
+            pl.BlockSpec((3, 16, block), lambda i: (0, 0, i)),
+            pl.BlockSpec((8, block), lambda i: (0, i)),
+            pl.BlockSpec((3, 3, block), lambda i: (0, 0, i)),
+            pl.BlockSpec((16, block), lambda i: (0, i)),
+        ],
+        out_specs=pl.BlockSpec(shape, lambda i: (i, 0, 0, 0)),
+        out_shape=pltpu.HBM(rough.shape, jnp.bfloat16),
+        compiler_params=params(32),
+    )(rough, held(proj), edge, taps, held(grad_out))
 
 
 def spectrum_kernel(filter_ref, fwd_a_ref, turn_ref, fwd_b_ref, out_ref):
@@ -149,7 +209,7 @@
 
 
 def whole(shape):
-    return pl.BlockSpec(shape, lambda i: (0,) * len(shape))
+    return pl.BlockSpec(shape, lambda *_: (0,) * len(shape))
 
 
 def spectrum(filter_sq, tab):
@@ -208,12 +268,17 @@
     out_ref, lag_ref, rows_ref, outs_ref, *, group,
 ):
     block = in_ref.shape[2]
-    for at in range(2):
-        rows_ref[at] = in_ref[:, at].astype(jnp.float32).reshape(ROWS * block, ROWS)
+    part = pl.program_id(1)
+
+    @pl.when(part == 0)
+    def _():
+        for at in range(2):
+            rows_ref[at] = in_ref[:, at].astype(jnp.float32).reshape(ROWS * block, ROWS)
+
     cos_w, sin_w = turn_ref[0], turn_ref[1]
 
-    def some(step, carry):
-        chans = [step * group + at for at in range(group)]
+    def some():
+        chans = [part * group + at for at in range(group)]
         places = [(at, pl.ds(ch, ROWS, stride=block)) for ch in chans for at in range(2)]
         rows = [rows_ref[at, strided, :].astype(jnp.bfloat16) for at, strided in places]
         columns = jnp.concatenate(rows, axis=1)
@@ -225,21 +290,23 @@
             turned.append(side(y_re * cos_w - y_im * sin_w, y_re * sin_w + y_im * cos_w))
         z = apply_right(jnp.concatenate(turned, axis=0), fwd_b_ref)
         products = []
-        for at, ch in enumerate(chans):
+        for at in range(group):
             x_re, x_im = halves(z[2 * at * ROWS : (2 * at + 1) * ROWS])
             g_re, g_im = halves(z[(2 * at + 1) * ROWS : (2 * at + 2) * ROWS])
-            h_re, h_im = halves(spec_ref[ch])
-            lag_ref[ch] = side(g_re * x_re + g_im * x_im, g_im * x_re - g_re * x_im)
+            h_re, h_im = halves(spec_ref[at])
+            lag_ref[at] = side(g_re * x_re + g_im * x_im, g_im * x_re - g_re * x_im)
             products.append(side(x_re * h_re - x_im * h_im, x_re * h_im + x_im * h_re))
             products.append(side(h_re * g_re + h_im * g_im, h_re * g_im - h_im * g_re))
         res = turned_back(jnp.concatenate(products, axis=0), inv_b_ref, inv_a_ref, cos_w, sin_w)
         for column, (at, strided) in enumerate(places):
             outs_ref[at, strided, :] = res[:, column * ROWS : (column + 1) * ROWS]
-        return carry
-
-    lax.fori_loop(0, block // group, some, 0)
-    for at in range(2):
-        out_ref[:, at] = outs_ref[at].astype(jnp.bfloat16).reshape(ROWS, block, ROWS)
+
+    some()
+
+    @pl.when(part == pl.num_programs(1) - 1)
+    def _():
+        for at in range(2):
+            out_ref[:, at] = outs_ref[at].astype(jnp.bfloat16).reshape(ROWS, block, ROWS)
 
 
 def convolve(received, spec, tab, group=8, block=16):
@@ -247,15 +314,15 @@
     names = ("fwd_a", "turn", "fwd_b_high", "inv_b_high", "inv_a_high")
     return pl.pallas_call(
         functools.partial(conv_kernel, group=group),
-        grid=(width // block,),
+        grid=(width // block, block // group),
         in_specs=[
-            pl.BlockSpec((ROWS, 2, block, ROWS), lambda i: (0, 0, i, 0)),
-            pl.BlockSpec((block, ROWS, 2 * ROWS), lambda i: (i, 0, 0)),
+            pl.BlockSpec((ROWS, 2, block, ROWS), lambda i, j: (0, 0, i, 0)),
+            pl.BlockSpec((group, ROWS, 2 * ROWS), lambda i, j: (i * (block // group) + j, 0, 0)),
         ]
         + [whole(tab[name].shape) for name in names],
         out_specs=[
-            pl.BlockSpec((ROWS, 2, block, ROWS), lambda i: (0, 0, i, 0)),
-            pl.BlockSpec((block, ROWS, 2 * ROWS), lambda i: (i, 0, 0)),
+            pl.BlockSpec((ROWS, 2, block, ROWS), lambda i, j: (0, 0, i, 0)),
+            pl.BlockSpec((group, ROWS, 2 * ROWS), lambda i, j: (i * (block // group) + j, 0, 0)),
         ],
         out_shape=[
             pltpu.HBM((ROWS, 2, width, ROWS), jnp.bfloat16),
@@ -293,94 +360,116 @@
     )(products, *(tab[name] for name in names))
 
 
-def grads_kernel(
-    ret_ref, proj_ref, edge_ref, taps_ref, grad_ref,
-    out_ref, sums_ref, first_ref, last_ref, ext_ref, grads_ref,
+def fill_turned(turned_ref, ret_ref):
+    block = turned_ref.shape[2]
+    for at in range(2):
+        turned_ref[at] = ret_ref[:, at].reshape(block, ROWS).T.astype(jnp.float32)
+
+
+def grads_at(turned_ref, taps_ref, grad_ref, row, lanes, keys, values):
+    rows = pl.ds(row, STEP)
+    conv, corr = turned_ref[0, rows, lanes], turned_ref[1, rows, lanes]
+    key = filtered(taps_ref, 1, lanes, keys)
+    value = filtered(taps_ref, 2, lanes, values)
+    return (grad_ref[rows, lanes].astype(jnp.float32) * conv, corr * value, corr * key)
+
+
+def sums_kernel(
+    ret_ref, proj_ref, edge_ref, taps_ref, grad_ref, sums_ref, first_ref, ext_ref, turned_ref
 ):
     fill_ext(ext_ref, proj_ref, edge_ref)
-    block = grad_ref.shape[1]
-    conv, corr = (
-        ret_ref[:, at].reshape(block, ROWS).T.astype(jnp.float32) for at in range(2)
-    )
-    key, value = (feature(ext_ref, taps_ref, stream) for stream in (1, 2))
-    grads = (grad_ref[...].astype(jnp.float32) * conv, corr * value, corr * key)
+    fill_turned(turned_ref, ret_ref)
     first_ref[...] = jnp.zeros_like(first_ref)
     sums_ref[...] = jnp.zeros_like(sums_ref)
+    for at, lanes in enumerate(lanes_of(grad_ref.shape[1])):
+        sums = [jnp.zeros((8, ROWS), jnp.float32)] * 9
+        for row in range(0, ROWS, STEP):
+            shifted = [inputs_at(ext_ref, stream, row, lanes) for stream in range(3)]
+            grads = grads_at(turned_ref, taps_ref, grad_ref, row, lanes, shifted[1], shifted[2])
+            for stream in range(3):
+                for tap in range(3):
+                    terms = (grads[stream] * shifted[stream][tap]).reshape(STEP // 8, 8, ROWS)
+                    sums[3 * stream + tap] = sums[3 * stream + tap] + jnp.sum(terms, axis=0)
+                if row == 0:
+                    first_ref[pl.ds(2 * stream, 2), lanes] = grads[stream][:2]
+        for which in range(9):
+            sums_ref[which, pl.ds(at, 1)] = jnp.sum(sums[which], axis=0, keepdims=True)
+
+
+def local_specs(block, width):
+    return [
+        pl.BlockSpec((block // width, 2, width, ROWS), lambda i: (i, 0, 0, 0)),
+        pl.BlockSpec((3, ROWS, block), lambda i: (0, 0, i)),
+        pl.BlockSpec((8, block), lambda i: (0, i)),
+        pl.BlockSpec((3, 3, block), lambda i: (0, 0, i)),
+        pl.BlockSpec((ROWS, block), lambda i: (0, i)),
+    ]
+
+
+def tap_sums(returned, proj, edge, taps, grad_out):
+    channels = proj.shape[-1]
+    block = min(1024, channels)
+    return pl.pallas_call(
+        sums_kernel,
+        grid=(channels // block,),
+        in_specs=local_specs(block, returned.shape[2]),
+        out_specs=[
+            pl.BlockSpec((16, block // ROWS, ROWS), lambda i: (0, i, 0)),
+            pl.BlockSpec((8, block), lambda i: (0, i)),
+        ],
+        out_shape=[
+            jax.ShapeDtypeStruct((16, channels // ROWS, ROWS), jnp.float32),
+            jax.ShapeDtypeStruct((8, channels), jnp.float32),
+        ],
+        scratch_shapes=[
+            pltpu.VMEM((3, ROWS + 8, block), jnp.float32),
+            pltpu.VMEM((2, ROWS, block), jnp.float32),
+        ],
+        compiler_params=params(40),
+    )(returned, held(proj), edge, taps, held(grad_out))
+
+
+def grads_kernel(
+    ret_ref, proj_ref, edge_ref, taps_ref, grad_ref, later_ref,
+    out_ref, ext_ref, turned_ref, grads_ref,
+):
+    fill_ext(ext_ref, proj_ref, edge_ref)
+    fill_turned(turned_ref, ret_ref)
     for stream in range(3):
-        grads_ref[stream, pl.ds(0, ROWS), :] = grads[stream]
-        grads_ref[stream, pl.ds(ROWS, 8), :] = jnp.zeros((8, block), jnp.float32)
-        first_ref[pl.ds(2 * stream, 2), :] = grads[stream][:2]
-        for tap in range(3):
-            sums = jnp.sum(grads[stream] * shifted(ext_ref, stream, tap), axis=0, keepdims=True)
-            sums_ref[pl.ds(3 * stream + tap, 1)] = sums.reshape(1, block // ROWS, ROWS)
-        total = taps_ref[stream, pl.ds(0, 1), :] * grads[stream]
-        for tap in (1, 2):
-            total += taps_ref[stream, pl.ds(tap, 1), :] * grads_ref[stream, pl.ds(tap, ROWS), :]
-        out_ref[stream] = total.astype(jnp.bfloat16)
-        last_ref[stream] = total[ROWS - 16 :]
-
-
-def stream_grads(returned, proj, edge, taps, grad_out):
+        grads_ref[stream, pl.ds(ROWS, 2), :] = later_ref[pl.ds(2 * stream, 2), :]
+    for lanes in lanes_of(grad_ref.shape[1]):
+        for row in range(0, ROWS, STEP):
+            shifted = [inputs_at(ext_ref, stream, row, lanes) for stream in (1, 2)]
+            grads = grads_at(turned_ref, taps_ref, grad_ref, row, lanes, *shifted)
+            for stream in range(3):
+                grads_ref[stream, pl.ds(row, STEP), lanes] = grads[stream]
+        for stream in range(3):
+            for row in range(0, ROWS, STEP):
+                ahead = [grads_ref[stream, pl.ds(row + tap, STEP), lanes] for tap in range(3)]
+                total = filtered(taps_ref, stream, lanes, ahead)
+                out_ref[stream, pl.ds(row, STEP), lanes] = total.astype(jnp.bfloat16)
+
+
+def stream_grads(returned, proj, edge, taps, grad_out, later):
     channels = proj.shape[-1]
-    width = returned.shape[2]
     block = min(1024, channels)
     return pl.pallas_call(
         grads_kernel,
         grid=(channels // block,),
-        in_specs=[
-            pl.BlockSpec((block // width, 2, width, ROWS), lambda i: (i, 0, 0, 0)),
-            pl.BlockSpec((3, ROWS, block), lambda i: (0, 0, i)),
-            pl.BlockSpec((8, block), lambda i: (0, i)),
-            pl.BlockSpec((3, 3, block), lambda i: (0, 0, i)),
-            pl.BlockSpec((ROWS, block), lambda i: (0, i)),
-        ],
-        out_specs=[
-            pl.BlockSpec((3, ROWS, block), lambda i: (0, 0, i)),
-            pl.BlockSpec((16, block // ROWS, ROWS), lambda i: (0, i, 0)),
-            pl.BlockSpec((8, block), lambda i: (0, i)),
-            pl.BlockSpec((3, 16, block), lambda i: (0, 0, i)),
-        ],
-        out_shape=[
-            jax.ShapeDtypeStruct((3, ROWS, channels), jnp.bfloat16),
-            jax.ShapeDtypeStruct((16, channels // ROWS, ROWS), jnp.float32),
-            pltpu.HBM((8, channels), jnp.float32),
-            pltpu.HBM((3, 16, channels), jnp.float32),
-        ],
+        in_specs=local_specs(block, returned.shape[2])
+        + [pl.BlockSpec((8, block), lambda i: (0, i))],
+        out_specs=pl.BlockSpec((3, ROWS, block), lambda i: (0, 0, i)),
+        out_shape=jax.ShapeDtypeStruct((3, ROWS, channels), jnp.bfloat16),
         scratch_shapes=[
             pltpu.VMEM((3, ROWS + 8, block), jnp.float32),
+            pltpu.VMEM((2, ROWS, block), jnp.float32),
             pltpu.VMEM((3, ROWS + 8, block), jnp.float32),
         ],
-        compiler_params=params(48),
-    )(returned, held(proj), edge, taps, held(grad_out))
-
-
-def last_kernel(whole_ref, last_ref, later_ref, taps_ref, out_ref):
-    del whole_ref
-    for stream in range(3):
-        later = later_ref[pl.ds(2 * stream, 2), :]
-        tap_1, tap_2 = (taps_ref[stream, pl.ds(tap, 1), :] for tap in (1, 2))
-        rows = last_ref[stream]
-        row_14 = rows[14:15] + tap_2 * later[:1]
-        row_15 = rows[15:] + tap_1 * later[:1] + tap_2 * later[1:]
-        out_ref[stream] = jnp.concatenate([rows[:14], row_14, row_15], axis=0).astype(jnp.bfloat16)
-
-
-def finish_rows(grad_rows, last, later, taps):
-    channels = grad_rows.shape[-1]
-    return pl.pallas_call(
-        last_kernel,
-        grid=(1,),
-        in_specs=[
-            pl.BlockSpec(memory_space=pl.ANY),
-            whole((3, 16, channels)),
-            whole((8, channels)),
-            whole((3, 3, channels)),
-        ],
-        out_specs=pl.BlockSpec((3, 16, channels), lambda i: (0, ROWS // 16 - 1, 0)),
-        out_shape=jax.ShapeDtypeStruct(grad_rows.shape, grad_rows.dtype),
-        input_output_aliases={0: 0},
-        compiler_params=params(16),
-    )(grad_rows, last, later, taps)
+        compiler_params=params(40),
+        cost_estimate=pl.CostEstimate(
+            flops=60 * ROWS * channels, bytes_accessed=18 * ROWS * channels, transcendentals=0
+        ),
+    )(returned, held(proj), edge, taps, held(grad_out), later)
 
 
 def passed_along(value, steps):
@@ -393,13 +482,14 @@
     return lax.all_to_all(value, axes, split_axis=0, concat_axis=0, tiled=True)
 
 
-def sum_everywhere(sums):
+def sum_everywhere(sums, beside):
     channels = sums.shape[1] * ROWS
     devices = lax.axis_size("dp") * lax.axis_size("ctx")
     pieces = sums.reshape(devices, 2, ROWS)
     own = jnp.sum(exchanged(pieces, ("dp", "ctx")), axis=0)
+    own, beside = lax.optimization_barrier((own.astype(jnp.bfloat16), beside))
     spread = exchanged(jnp.broadcast_to(own[None], pieces.shape), ("dp", "ctx"))
-    return spread.reshape(16, channels)[:9].reshape(3, 3, channels)
+    return spread.reshape(16, channels)[:9].reshape(3, 3, channels).astype(jnp.float32), beside
 
 
 def local(projected, short_taps, long_filter, grad_out):
@@ -408,7 +498,8 @@
     grad_rows = grad_out[0]
     width = long_filter.shape[0]
     edge = passed_along(edges(proj), 1)
-    sent = gates(proj, edge, short_taps, grad_rows, width)
+    rough = gates(proj, short_taps, grad_rows, width)
+    sent = headed(rough, proj, edge, short_taps, grad_rows)
     received = exchanged(sent, "ctx")
     spec = spectrum(long_filter.reshape(width, ROWS, ROWS), tab)
     results, products = convolve(received, spec, tab)
@@ -421,10 +512,11 @@
     )
     lag_sum = jnp.where(second, upper, lower) + other.astype(jnp.float32)
     grad_filter = lag_sum.reshape(width, ROWS // 2 * ROWS)
-    grad_in, sums, first, last = stream_grads(returned, proj, edge, short_taps, grad_rows)
-    later = passed_along(first, -1)
-    grad_in = finish_rows(grad_in, last, later, short_taps)
-    return (grad_in[:, None], sum_everywhere(sums), grad_filter)
+    late_edge, grad_filter = lax.optimization_barrier((edge, grad_filter))
+    sums, first = tap_sums(returned, proj, late_edge, short_taps, grad_rows)
+    grad_taps, later = sum_everywhere(sums, passed_along(first, -1))
+    grad_in = stream_grads(returned, proj, edge, short_taps, grad_rows, later)
+    return (grad_in[:, None], grad_taps, grad_filter)
 
 
 def solution(mesh):

time: 209 us -> 200 us (0.957)
  waiting for transfers between devices: 102 us -> 94.5 us
  Pallas kernels: 42.3 us -> 46.4 us
  other arithmetic: 3.22 us -> 0.68 us
  starting transfers between devices: 52.3 us -> 49.8 us
    all_to_all x4, waiting for transfers between devices: 99.5 us -> 73.9 us  [exchanged(): return lax.all_to_all(value, axes, split_axis=0, concat_axis=0, tiled=True)]
    ppermute x1, waiting for transfers between devices: 0.01 us -> 20.6 us  [local(): lax.ppermute(jnp.where(second, lower, upper).astype(jnp.bfloat16), 'dp',...]
    pallas_call x2 -> x3, Pallas kernels: 10.2 us -> 16.2 us  [the longest x1 7.43 us: stream_grads(): pl.pallas_call(grads_kernel, grid=(channels // block,), in_specs=local_sp...]
    ppermute x2, waiting for transfers between devices: 2.22 us -> 0.01 us  [passed_along(): lax.ppermute(value, 'ctx', [(source, source + steps) for source in range(...]
    all_to_all x4, starting transfers between devices: 40.2 us -> 38 us  [exchanged(): return lax.all_to_all(value, axes, split_axis=0, concat_axis=0, tiled=True)]
    unnamed x30 -> x22, local copies, waits for them, and re-layouts: 6.58 us -> 5.24 us
  transfers between devices with their start and end apart: 7 -> 7, of which waited for: 6 -> 5; matrix products, arithmetic and copies ran while one was open for 4% -> 2% of each run, Pallas kernels for 7% -> 13%
where the time goes in v2:
time: 200 us; the launch traced here: 199 us
  waiting for transfers between devices  94.5 us (47%)
  starting transfers between devices  49.8 us (25%)
  Pallas kernels  46.4 us (23%)
  local copies, waits for them, and re-layouts  6.79 us (3%)
    all_to_all x4, waiting for transfers between devices, exchanged(): return lax.all_to_all(value, axes, split_axis=0, concat_axis=0, tiled=True)  73.9 us
    all_to_all x4, starting transfers between devices, exchanged(): return lax.all_to_all(value, axes, split_axis=0, concat_axis=0, tiled=True)  38 us
    ppermute x1, waiting for transfers between devices, local(): lax.ppermute(jnp.where(second, lower, upper).astype(jnp.bfloat16), 'dp',...  20.6 us
    pallas_call x1, Pallas kernels, convolve(): pl.pallas_call(functools.partial(conv_kernel, group=group), grid=(width /...  11.1 us
    pallas_call x1, Pallas kernels, spectrum(): pl.pallas_call(spectrum_kernel, grid=(width // block,), in_specs=[pl.Bloc...  10.4 us
    ppermute x2, starting transfers between devices, passed_along(): lax.ppermute(value, 'ctx', [(source, source + steps) for source in range(...  8.65 us
    pallas_call x1, Pallas kernels, stream_grads(): pl.pallas_call(grads_kernel, grid=(channels // block,), in_specs=local_sp...  7.43 us
    pallas_call x1, Pallas kernels, tap_sums(): pl.pallas_call(sums_kernel, grid=(channels // block,), in_specs=local_spe...  6.1 us
  transfers between devices with their start and end apart: 7, of which 5 were waited for; matrix products, arithmetic and copies ran while one was open for 2% of the time, Pallas kernels for 13%

profile of v2, /device:TPU:1, one launch (start us, length us, event | category | flops | bytes accessed | tf_op | source)
XLA Modules:
  0.0 199.0 jit_solution(8052531824008042509)
XLA Ops:
  0.6 0.0 copy-start
  0.6 1.1 shard_map.140
  1.7 4.6 %collective-permute-start = (f32[8,4096]{1,0:T(8,128)S(1)}, f32[8,4096]{1,0:T(8,128)S(1)}, u32[]{:S(2)}, u32[]{:S(2)}) collective-permute-start(f32[8,4096]{1,0:T(8,128)S(1)} %shard_map.140), channel_id=1, source_target_pairs={{0,1},{1,2},{2,3},{3,4},{4,5},{5,6},{6,7},{7,8},{8,9},{9,10},{10,1... | collective-permute-start | bytes 393224 | tf_op jit(solution)/shard_map/ppermute | solution.py:478
  6.3 0.0 copy-done
  6.3 4.1 %shard_map.139.rough_ref = bf16[128,2,32,128]{3,2,1,0:T(8,128)(2,1)S(1)} custom-call(bf16[3,128,4096]{2,1,0:T(8,128)(2,1)} %bitcast.14, f32[3,3,4096]{2,1,0:T(4,128)S(1)} %copy-done, bf16[128,4096]{1,0:T(8,128)(2,1)} %bitcast.18), custom_call_target="tpu_custom_call" | custom-call | flops 20971520 | bytes 6291456 | tf_op jit(solution)/shard_map/pallas_call | solution.py:134
  10.4 0.0 collective-permute-done.edge_ref
  10.4 2.7 %shard_map.141 = bf16[128,2,32,128]{3,2,1,0:T(8,128)(2,1)} custom-call(bf16[128,2,32,128]{3,2,1,0:T(8,128)(2,1)S(1)} %shard_map.139.rough_ref, bf16[3,128,4096]{2,1,0:T(8,128)(2,1)} %bitcast.15, f32[8,4096]{1,0:T(8,128)S(1)} %collective-permute-done.edge_ref, f32[3,3,4096]{2,1,0:T(4,128)S(1)} %copy-done, bf16[128,4096]{1,0:T(8,128)(2,1)} %bitcast.19), custom_call_target="tpu_custom_call" | custom-call | tf_op jit(solution)/shard_map/pallas_call | solution.py:177
  13.1 13.4 %all-to-all-start = ((bf16[128,2,32,128]{3,2,1,0:T(8,128)(2,1)}), bf16[128,2,32,128]{3,2,1,0:T(8,128)(2,1)S(1)}, u32[]{:S(2)}, u32[]{:S(2)}) async-start(bf16[128,2,32,128]{3,2,1,0:T(8,128)(2,1)} %shard_map.141), calls=%async_computation | async-start | bytes 4194304 | tf_op jit(solution)/shard_map/all_to_all | solution.py:482
  26.5 0.0 copy-start.1
  26.6 0.0 copy-start.2
  26.6 0.0 copy-start.8
  26.6 2.0 %copy.16 = f32[4,8,128,128]{3,2,1,0:T(8,128)S(1)} copy(f32[4,8,128,128]{3,1,2,0:T(8,128)} %bitcast.24) | data formatting | bytes 4194304
  28.6 0.0 copy-done.1
  28.6 0.0 copy-done.2
  28.6 0.0 copy-done.8
  28.6 0.0 copy-start.3
  28.6 0.0 copy-start.4
  28.7 0.0 copy-start.5
  28.7 10.4 %shard_map.142.spec_ref = f32[32,128,256]{2,1,0:T(8,128)} custom-call(f32[32,128,128]{2,1,0:T(8,128)S(1)} %bitcast.12, bf16[256,256]{1,0:T(8,128)(2,1)S(1)} %copy-done.2, f32[2,128,128]{2,1,0:T(8,128)S(1)} %copy-done.1, bf16[2,256,256]{2,1,0:T(8,128)(2,1)S(1)} %copy-done.8), custom_call_target="tpu_custom_call" | custom-call | flops 5368709120 | bytes 6291456 | tf_op jit(solution)/shard_map/pallas_call | solution.py:218
  39.1 37.7 %all-to-all-done.in_ref = bf16[128,2,32,128]{3,2,1,0:T(8,128)(2,1)S(1)} async-done(((bf16[128,2,32,128]{3,2,1,0:T(8,128)(2,1)}), bf16[128,2,32,128]{3,2,1,0:T(8,128)(2,1)S(1)}, u32[]{:S(2)}, u32[]{:S(2)}) %all-to-all-start) | async-done | bytes 2097184 | tf_op jit(solution)/shard_map/all_to_all | solution.py:482
  76.7 0.0 copy-done.3
  76.7 0.0 copy-done.4
  76.7 0.0 copy-done.5
  76.7 11.1 %shard_map.143 = (bf16[128,2,32,128]{3,2,1,0:T(8,128)(2,1)}, bf16[32,128,256]{2,1,0:T(8,128)(2,1)}) custom-call(bf16[128,2,32,128]{3,2,1,0:T(8,128)(2,1)S(1)} %all-to-all-done.in_ref, f32[32,128,256]{2,1,0:T(8,128)} %shard_map.142.spec_ref, bf16[256,256]{1,0:T(8,128)(2,1)S(1)} %copy-done.2, f32[2,128,128]{2,1,0:T(8,128)S(1)} %copy-done.1, ...), custom_call_target="tpu_custom_call" | custom-call | tf_op jit(solution)/shard_map/pallas_call | solution.py:315
  87.9 8.9 %all-to-all-start.1 = ((bf16[128,2,32,128]{3,2,1,0:T(8,128)(2,1)}), bf16[128,2,32,128]{3,2,1,0:T(8,128)(2,1)S(1)}, u32[]{:S(2)}, u32[]{:S(2)}) async-start(bf16[128,2,32,128]{3,2,1,0:T(8,128)(2,1)} %get-tuple-element.11), calls=%async_computation.1 | async-start | bytes 4194304 | tf_op jit(solution)/shard_map/all_to_all | solution.py:482
  96.8 0.0 copy-done.7
  96.8 0.0 copy-done.9
  96.8 0.0 copy-start.6
  96.8 1.6 copy-done.6
  98.4 3.5 %shard_map.144 = f32[32,128,128]{2,1,0:T(8,128)S(1)} custom-call(bf16[32,128,256]{2,1,0:T(8,128)(2,1)S(1)} %copy-done.6, f32[2,128,128]{2,1,0:T(8,128)S(1)} %copy-done.1, bf16[2,256,256]{2,1,0:T(8,128)(2,1)S(1)} %copy-done.7, bf16[2,128,256]{2,1,0:T(8,128)(2,1)S(1)} %copy-done.9), custom_call_target="tpu_custom_call" | custom-call | flops 4294967296 | bytes 4194304 | tf_op jit(solution)/shard_map/pallas_call | solution.py:348
  101.9 0.1 select_convert_fusion
  102.0 3.2 %collective-permute-start.1 = (bf16[32,64,128]{2,1,0:T(8,128)(2,1)S(1)}, bf16[32,64,128]{2,1,0:T(8,128)(2,1)S(1)}, u32[]{:S(2)}, u32[]{:S(2)}) collective-permute-start(bf16[32,64,128]{2,1,0:T(8,128)(2,1)S(1)} %select_convert_fusion), channel_id=1, source_target_pairs={{0,128},{128,0},{1,129},{129,1},{2,130},{130,2},{3,131},{131,3},{4... | collective-permute-start | bytes 1572872 | tf_op jit(solution)/shard_map/ppermute | solution.py:510
  105.2 20.6 %collective-permute-done.1 = bf16[32,64,128]{2,1,0:T(8,128)(2,1)S(1)} collective-permute-done((bf16[32,64,128]{2,1,0:T(8,128)(2,1)S(1)}, bf16[32,64,128]{2,1,0:T(8,128)(2,1)S(1)}, u32[]{:S(2)}, u32[]{:S(2)}) %collective-permute-start.1) | collective-permute-done | bytes 524320 | tf_op jit(solution)/shard_map/ppermute | solution.py:510
  125.8 0.3 convert_add_fusion
  126.0 1.6 copy.19
  127.6 19.4 %all-to-all-done.1.ret_ref = bf16[128,2,32,128]{3,2,1,0:T(8,128)(2,1)S(1)} async-done(((bf16[128,2,32,128]{3,2,1,0:T(8,128)(2,1)}), bf16[128,2,32,128]{3,2,1,0:T(8,128)(2,1)S(1)}, u32[]{:S(2)}, u32[]{:S(2)}) %all-to-all-start.1) | async-done | bytes 2097184 | tf_op jit(solution)/shard_map/all_to_all | solution.py:482
  147.0 6.1 %shard_map.145 = (f32[16,32,128]{2,1,0:T(8,128)}, f32[8,4096]{1,0:T(8,128)S(1)}) custom-call(bf16[128,2,32,128]{3,2,1,0:T(8,128)(2,1)S(1)} %all-to-all-done.1.ret_ref, bf16[3,128,4096]{2,1,0:T(8,128)(2,1)} %bitcast.16, f32[8,4096]{1,0:T(8,128)S(1)} %collective-permute-done.edge_ref, f32[3,3,4096]{2,1,0:T(4,128)S(1)} %copy-done, bf16[128,4096]{1,0:T(8,128)(2,1)} %bitcast.20), custom_call_target="tpu_custom_call" | custom-call | tf_op jit(solution)/shard_map/pallas_call | solution.py:412
  153.1 9.8 %all-to-all-start.2 = ((f32[256,2,128]{2,1,0:T(2,128)}), f32[256,2,128]{2,1,0:T(2,128)S(1)}, u32[]{:S(2)}, u32[]{:S(2)}) async-start(f32[256,2,128]{2,1,0:T(2,128)} %bitcast.2), calls=%async_computation.2 | async-start | bytes 524288 | tf_op jit(solution)/shard_map/all_to_all | solution.py:482
  162.9 4.1 %collective-permute-start.2 = (f32[8,4096]{1,0:T(8,128)S(1)}, f32[8,4096]{1,0:T(8,128)S(1)}, u32[]{:S(2)}, u32[]{:S(2)}) collective-permute-start(f32[8,4096]{1,0:T(8,128)S(1)} %get-tuple-element.15), channel_id=1, source_target_pairs={{1,0},{2,1},{3,2},{4,3},{5,4},{6,5},{7,6},{8,7},{9,8},{10,9},{11,1... | collective-permute-start | bytes 393224 | tf_op jit(solution)/shard_map/ppermute | solution.py:478
  167.0 11.5 %all-to-all-done.2 = f32[256,2,128]{2,1,0:T(2,128)S(1)} async-done(((f32[256,2,128]{2,1,0:T(2,128)}), f32[256,2,128]{2,1,0:T(2,128)S(1)}, u32[]{:S(2)}, u32[]{:S(2)}) %all-to-all-start.2) | async-done | bytes 262176 | tf_op jit(solution)/shard_map/all_to_all | solution.py:482
  178.5 0.3 reduce_sum.9
  178.8 0.0 collective-permute-done.2.later_ref
  178.8 0.7 broadcast_in_dim.10
  179.5 5.8 %all-to-all-start.3 = ((bf16[256,2,128]{2,1,0:T(2,128)(2,1)}), bf16[256,2,128]{2,1,0:T(2,128)(2,1)S(1)}, u32[]{:S(2)}, u32[]{:S(2)}) async-start(bf16[256,2,128]{2,1,0:T(2,128)(2,1)} %broadcast_in_dim.10), calls=%async_computation.3 | async-start | bytes 262144 | tf_op jit(solution)/shard_map/all_to_all | solution.py:482
  185.3 7.4 %shard_map.146 = bf16[3,128,4096]{2,1,0:T(8,128)(2,1)} custom-call(bf16[128,2,32,128]{3,2,1,0:T(8,128)(2,1)S(1)} %all-to-all-done.1.ret_ref, bf16[3,128,4096]{2,1,0:T(8,128)(2,1)} %bitcast.17, f32[8,4096]{1,0:T(8,128)S(1)} %collective-permute-done.edge_ref, f32[3,3,4096]{2,1,0:T(4,128)S(1)} %copy-done, bf16[128,4096]{1,0:T(8,128)(2,1)} %bitcast.21, ...), custom_call_target="tpu_custom_call" | custom-call | flops 31457280 | bytes 9437184 | tf_op jit(solution)/shard_map/pallas_call | solution.py:456
  192.8 5.4 %all-to-all-done.3 = bf16[256,2,128]{2,1,0:T(2,128)(2,1)S(1)} async-done(((bf16[256,2,128]{2,1,0:T(2,128)(2,1)}), bf16[256,2,128]{2,1,0:T(2,128)(2,1)S(1)}, u32[]{:S(2)}, u32[]{:S(2)}) %all-to-all-start.3) | async-done | bytes 131104 | tf_op jit(solution)/shard_map/all_to_all | solution.py:482
  198.2 0.1 slice_convert_fusion
  198.2 0.8 reshape.25
  (2 shorter events, 0.0 us)
Async XLA Ops:
  0.6 5.7 %copy-start = (f32[3,3,4096]{2,1,0:T(4,128)S(1)}, f32[3,3,4096]{2,1,0:T(4,128)}, u32[]{:S(2)}) copy-start(f32[3,3,4096]{2,1,0:T(4,128)} %taps_ref.7) | copy-start | bytes 442372
  1.7 8.7 %collective-permute-start = (f32[8,4096]{1,0:T(8,128)S(1)}, f32[8,4096]{1,0:T(8,128)S(1)}, u32[]{:S(2)}, u32[]{:S(2)}) collective-permute-start(f32[8,4096]{1,0:T(8,128)S(1)} %shard_map.140), channel_id=1, source_target_pairs={{0,1},{1,2},{2,3},{3,4},{4,5},{5,6},{6,7},{7,8},{8,9},{9,10},{10,1... | collective-permute-start | bytes 393224 | tf_op jit(solution)/shard_map/ppermute | solution.py:478
  13.1 63.6 %all-to-all-start = ((bf16[128,2,32,128]{3,2,1,0:T(8,128)(2,1)}), bf16[128,2,32,128]{3,2,1,0:T(8,128)(2,1)S(1)}, u32[]{:S(2)}, u32[]{:S(2)}) async-start(bf16[128,2,32,128]{3,2,1,0:T(8,128)(2,1)} %shard_map.141), calls=%async_computation | async-start | bytes 4194304 | tf_op jit(solution)/shard_map/all_to_all | solution.py:482
  26.5 2.1 %copy-start.1 = (f32[2,128,128]{2,1,0:T(8,128)S(1)}, f32[2,128,128]{2,1,0:T(8,128)}, u32[]{:S(2)}) copy-start(f32[2,128,128]{2,1,0:T(8,128)} %constant.27.clone.turn_ref) | copy-start | bytes 393220
  26.6 2.1 %copy-start.2 = (bf16[256,256]{1,0:T(8,128)(2,1)S(1)}, bf16[256,256]{1,0:T(8,128)(2,1)}, u32[]{:S(2)}) copy-start(bf16[256,256]{1,0:T(8,128)(2,1)} %constant.26.clone.fwd_a_ref) | copy-start | bytes 393220
  26.6 2.1 %copy-start.8 = (bf16[2,256,256]{2,1,0:T(8,128)(2,1)S(1)}, bf16[2,256,256]{2,1,0:T(8,128)(2,1)}, u32[]{:S(2)}) copy-start(bf16[2,256,256]{2,1,0:T(8,128)(2,1)} %constant.28.clone.fwd_b_ref) | copy-start | bytes 786436
  28.6 48.1 %copy-start.3 = (bf16[1,256,256]{2,1,0:T(8,128)(2,1)S(1)}, bf16[1,256,256]{2,1,0:T(8,128)(2,1)}, u32[]{:S(2)}) copy-start(bf16[1,256,256]{2,1,0:T(8,128)(2,1)} %constant.29.clone.fwd_b_ref) | copy-start | bytes 393220
  28.6 48.1 %copy-start.4 = (bf16[1,256,256]{2,1,0:T(8,128)(2,1)S(1)}, bf16[1,256,256]{2,1,0:T(8,128)(2,1)}, u32[]{:S(2)}) copy-start(bf16[1,256,256]{2,1,0:T(8,128)(2,1)} %constant.30.clone.inv_b_ref) | copy-start | bytes 393220
  28.7 48.1 %copy-start.5 = (bf16[1,128,256]{2,1,0:T(8,128)(2,1)S(1)}, bf16[1,128,256]{2,1,0:T(8,128)(2,1)}, u32[]{:S(2)}) copy-start(bf16[1,128,256]{2,1,0:T(8,128)(2,1)} %constant.31.clone.inv_a_ref) | copy-start | bytes 196612
  87.9 9.0 %copy-start.7 = (bf16[2,256,256]{2,1,0:T(8,128)(2,1)S(1)}, bf16[2,256,256]{2,1,0:T(8,128)(2,1)}, u32[]{:S(2)}) copy-start(bf16[2,256,256]{2,1,0:T(8,128)(2,1)} %constant.32.clone.inv_b_ref) | copy-start | bytes 786436
  87.9 9.0 %copy-start.9 = (bf16[2,128,256]{2,1,0:T(8,128)(2,1)S(1)}, bf16[2,128,256]{2,1,0:T(8,128)(2,1)}, u32[]{:S(2)}) copy-start(bf16[2,128,256]{2,1,0:T(8,128)(2,1)} %constant.33.clone.inv_a_ref) | copy-start | bytes 393220
  87.9 59.1 %all-to-all-start.1 = ((bf16[128,2,32,128]{3,2,1,0:T(8,128)(2,1)}), bf16[128,2,32,128]{3,2,1,0:T(8,128)(2,1)S(1)}, u32[]{:S(2)}, u32[]{:S(2)}) async-start(bf16[128,2,32,128]{3,2,1,0:T(8,128)(2,1)} %get-tuple-element.11), calls=%async_computation.1 | async-start | bytes 4194304 | tf_op jit(solution)/shard_map/all_to_all | solution.py:482
  96.8 1.6 copy-start.6
  102.0 23.8 %collective-permute-start.1 = (bf16[32,64,128]{2,1,0:T(8,128)(2,1)S(1)}, bf16[32,64,128]{2,1,0:T(8,128)(2,1)S(1)}, u32[]{:S(2)}, u32[]{:S(2)}) collective-permute-start(bf16[32,64,128]{2,1,0:T(8,128)(2,1)S(1)} %select_convert_fusion), channel_id=1, source_target_pairs={{0,128},{128,0},{1,129},{129,1},{2,130},{130,2},{3,131},{131,3},{4... | collective-permute-start | bytes 1572872 | tf_op jit(solution)/shard_map/ppermute | solution.py:510
  153.1 25.4 %all-to-all-start.2 = ((f32[256,2,128]{2,1,0:T(2,128)}), f32[256,2,128]{2,1,0:T(2,128)S(1)}, u32[]{:S(2)}, u32[]{:S(2)}) async-start(f32[256,2,128]{2,1,0:T(2,128)} %bitcast.2), calls=%async_computation.2 | async-start | bytes 524288 | tf_op jit(solution)/shard_map/all_to_all | solution.py:482
  162.9 15.9 %collective-permute-start.2 = (f32[8,4096]{1,0:T(8,128)S(1)}, f32[8,4096]{1,0:T(8,128)S(1)}, u32[]{:S(2)}, u32[]{:S(2)}) collective-permute-start(f32[8,4096]{1,0:T(8,128)S(1)} %get-tuple-element.15), channel_id=1, source_target_pairs={{1,0},{2,1},{3,2},{4,3},{5,4},{6,5},{7,6},{8,7},{9,8},{10,9},{11,1... | collective-permute-start | bytes 393224 | tf_op jit(solution)/shard_map/ppermute | solution.py:478
  179.5 18.7 %all-to-all-start.3 = ((bf16[256,2,128]{2,1,0:T(2,128)(2,1)}), bf16[256,2,128]{2,1,0:T(2,128)(2,1)S(1)}, u32[]{:S(2)}, u32[]{:S(2)}) async-start(bf16[256,2,128]{2,1,0:T(2,128)(2,1)} %broadcast_in_dim.10), calls=%async_computation.3 | async-start | bytes 262144 | tf_op jit(solution)/shard_map/all_to_all | solution.py:482

commit v3 on v2

--- a/solution.py
+++ b/solution.py
@@ -267,13 +267,14 @@
     in_ref, spec_ref, fwd_a_ref, turn_ref, fwd_b_ref, inv_b_ref, inv_a_ref,
     out_ref, lag_ref, rows_ref, outs_ref, *, group,
 ):
-    block = in_ref.shape[2]
+    block = out_ref.shape[2]
     part = pl.program_id(1)
+    here = pl.ds(pl.multiple_of(pl.program_id(0) * block, block), block)
 
     @pl.when(part == 0)
     def _():
         for at in range(2):
-            rows_ref[at] = in_ref[:, at].astype(jnp.float32).reshape(ROWS * block, ROWS)
+            rows_ref[at] = in_ref[:, at, here].astype(jnp.float32).reshape(ROWS * block, ROWS)
 
     cos_w, sin_w = turn_ref[0], turn_ref[1]
 
@@ -316,7 +317,7 @@
         functools.partial(conv_kernel, group=group),
         grid=(width // block, block // group),
         in_specs=[
-            pl.BlockSpec((ROWS, 2, block, ROWS), lambda i, j: (0, 0, i, 0)),
+            pl.BlockSpec(memory_space=pltpu.VMEM),
             pl.BlockSpec((group, ROWS, 2 * ROWS), lambda i, j: (i * (block // group) + j, 0, 0)),
         ]
         + [whole(tab[name].shape) for name in names],
@@ -377,7 +378,9 @@
 def sums_kernel(
     ret_ref, proj_ref, edge_ref, taps_ref, grad_ref, sums_ref, first_ref, ext_ref, turned_ref
 ):
-    fill_ext(ext_ref, proj_ref, edge_ref)
+    block = grad_ref.shape[1]
+    channels = pl.ds(pl.multiple_of(pl.program_id(0) * block, block), block)
+    fill_ext(ext_ref, proj_ref.at[:, :, channels], edge_ref)
     fill_turned(turned_ref, ret_ref)
     first_ref[...] = jnp.zeros_like(first_ref)
     sums_ref[...] = jnp.zeros_like(sums_ref)
@@ -409,24 +412,26 @@
 def tap_sums(returned, proj, edge, taps, grad_out):
     channels = proj.shape[-1]
     block = min(1024, channels)
+    specs = local_specs(block, returned.shape[2])
+    specs[1] = pl.BlockSpec(memory_space=pltpu.VMEM)
     return pl.pallas_call(
         sums_kernel,
         grid=(channels // block,),
-        in_specs=local_specs(block, returned.shape[2]),
+        in_specs=specs,
         out_specs=[
             pl.BlockSpec((16, block // ROWS, ROWS), lambda i: (0, i, 0)),
             pl.BlockSpec((8, block), lambda i: (0, i)),
         ],
         out_shape=[
-            jax.ShapeDtypeStruct((16, channels // ROWS, ROWS), jnp.float32),
-            jax.ShapeDtypeStruct((8, channels), jnp.float32),
+            pltpu.HBM((16, channels // ROWS, ROWS), jnp.float32),
+            pltpu.HBM((8, channels), jnp.float32),
         ],
         scratch_shapes=[
             pltpu.VMEM((3, ROWS + 8, block), jnp.float32),
             pltpu.VMEM((2, ROWS, block), jnp.float32),
         ],
         compiler_params=params(40),
-    )(returned, held(proj), edge, taps, held(grad_out))
+    )(returned, proj, edge, taps, held(grad_out))
 
 
 def grads_kernel(

time: 200 us -> 199 us (level)
    unnamed x22 -> x24, local copies, waits for them, and re-layouts: 5.24 us -> 3.66 us
where the time goes in v3:
time: 199 us
  waiting for transfers between devices  95.4 us (48%)
  starting transfers between devices  50.3 us (25%)
  Pallas kernels  46.4 us (23%)
  local copies, waits for them, and re-layouts  5.22 us (3%)
    all_to_all x4, waiting for transfers between devices, exchanged(): return lax.all_to_all(value, axes, split_axis=0, concat_axis=0, tiled=True)  73.3 us
    all_to_all x4, starting transfers between devices, exchanged(): return lax.all_to_all(value, axes, split_axis=0, concat_axis=0, tiled=True)  38.5 us
    ppermute x1, waiting for transfers between devices, local(): lax.ppermute(jnp.where(second, lower, upper).astype(jnp.bfloat16), 'dp',...  22.1 us
    pallas_call x1, Pallas kernels, convolve(): pl.pallas_call(functools.partial(conv_kernel, group=group), grid=(width /...  11 us
    pallas_call x1, Pallas kernels, spectrum(): pl.pallas_call(spectrum_kernel, grid=(width // block,), in_specs=[pl.Bloc...  10.4 us
    ppermute x2, starting transfers between devices, passed_along(): lax.ppermute(value, 'ctx', [(source, source + steps) for source in range(...  8.65 us
    pallas_call x1, Pallas kernels, stream_grads(): pl.pallas_call(grads_kernel, grid=(channels // block,), in_specs=local_sp...  7.79 us
    pallas_call x1, Pallas kernels, tap_sums(): pl.pallas_call(sums_kernel, grid=(channels // block,), in_specs=specs, ou...  5.91 us
  transfers between devices with their start and end apart: 7, of which 5 were waited for; matrix products, arithmetic and copies ran while one was open for 2% of the time, Pallas kernels for 13%

profile of v3, /device:TPU:1, one launch (start us, length us, event | category | flops | bytes accessed | tf_op | source)
XLA Modules:
  0.0 198.8 jit_solution(10339287121216461879)
XLA Ops:
  0.6 0.0 copy-start.1
  0.6 1.1 shard_map.140
  1.7 4.6 %collective-permute-start = (f32[8,4096]{1,0:T(8,128)S(1)}, f32[8,4096]{1,0:T(8,128)S(1)}, u32[]{:S(2)}, u32[]{:S(2)}) collective-permute-start(f32[8,4096]{1,0:T(8,128)S(1)} %shard_map.140), channel_id=1, source_target_pairs={{0,1},{1,2},{2,3},{3,4},{4,5},{5,6},{6,7},{7,8},{8,9},{9,10},{10,1... | collective-permute-start | bytes 393224 | tf_op jit(solution)/shard_map/ppermute | solution.py:483
  6.3 0.0 copy-done.1
  6.3 4.1 %shard_map.139.rough_ref = bf16[128,2,32,128]{3,2,1,0:T(8,128)(2,1)S(1)} custom-call(bf16[3,128,4096]{2,1,0:T(8,128)(2,1)} %bitcast.13, f32[3,3,4096]{2,1,0:T(4,128)S(1)} %copy-done.1, bf16[128,4096]{1,0:T(8,128)(2,1)} %bitcast.18), custom_call_target="tpu_custom_call" | custom-call | flops 20971520 | bytes 6291456 | tf_op jit(solution)/shard_map/pallas_call | solution.py:134
  10.4 0.0 collective-permute-done.edge_ref
  10.4 2.7 %shard_map.141 = bf16[128,2,32,128]{3,2,1,0:T(8,128)(2,1)} custom-call(bf16[128,2,32,128]{3,2,1,0:T(8,128)(2,1)S(1)} %shard_map.139.rough_ref, bf16[3,128,4096]{2,1,0:T(8,128)(2,1)} %bitcast.14, f32[8,4096]{1,0:T(8,128)S(1)} %collective-permute-done.edge_ref, f32[3,3,4096]{2,1,0:T(4,128)S(1)} %copy-done.1, bf16[128,4096]{1,0:T(8,128)(2,1)} %bitcast.19), custom_call_target="tpu_custom_call" | custom-call | tf_op jit(solution)/shard_map/pallas_call | solution.py:177
  13.1 13.4 %all-to-all-start = ((bf16[128,2,32,128]{3,2,1,0:T(8,128)(2,1)}), bf16[128,2,32,128]{3,2,1,0:T(8,128)(2,1)S(1)}, u32[]{:S(2)}, u32[]{:S(2)}) async-start(bf16[128,2,32,128]{3,2,1,0:T(8,128)(2,1)} %shard_map.141), calls=%async_computation | async-start | bytes 4194304 | tf_op jit(solution)/shard_map/all_to_all | solution.py:487
  26.5 0.0 copy-start.2
  26.6 0.0 copy-start.3
  26.6 0.0 copy-start.9
  26.6 2.0 %copy.16 = f32[4,8,128,128]{3,2,1,0:T(8,128)S(1)} copy(f32[4,8,128,128]{3,1,2,0:T(8,128)} %bitcast.24) | data formatting | bytes 4194304
  28.6 0.0 copy-done.2
  28.6 0.0 copy-done.3
  28.6 0.0 copy-done.9
  28.6 0.0 copy-start.4
  28.6 0.0 copy-start.5
  28.7 0.0 copy-start.6
  28.7 10.4 %shard_map.142.spec_ref = f32[32,128,256]{2,1,0:T(8,128)} custom-call(f32[32,128,128]{2,1,0:T(8,128)S(1)} %bitcast.17, bf16[256,256]{1,0:T(8,128)(2,1)S(1)} %copy-done.3, f32[2,128,128]{2,1,0:T(8,128)S(1)} %copy-done.2, bf16[2,256,256]{2,1,0:T(8,128)(2,1)S(1)} %copy-done.9), custom_call_target="tpu_custom_call" | custom-call | flops 5368709120 | bytes 6291456 | tf_op jit(solution)/shard_map/pallas_call | solution.py:218
  39.0 37.7 %all-to-all-done.in_ref = bf16[128,2,32,128]{3,2,1,0:T(8,128)(2,1)S(1)} async-done(((bf16[128,2,32,128]{3,2,1,0:T(8,128)(2,1)}), bf16[128,2,32,128]{3,2,1,0:T(8,128)(2,1)S(1)}, u32[]{:S(2)}, u32[]{:S(2)}) %all-to-all-start) | async-done | bytes 2097184 | tf_op jit(solution)/shard_map/all_to_all | solution.py:487
  76.7 0.0 copy-done.4
  76.7 0.0 copy-done.5
  76.7 0.0 copy-done.6
  76.7 11.0 %shard_map.143 = (bf16[128,2,32,128]{3,2,1,0:T(8,128)(2,1)}, bf16[32,128,256]{2,1,0:T(8,128)(2,1)}) custom-call(bf16[128,2,32,128]{3,2,1,0:T(8,128)(2,1)S(1)} %all-to-all-done.in_ref, f32[32,128,256]{2,1,0:T(8,128)} %shard_map.142.spec_ref, bf16[256,256]{1,0:T(8,128)(2,1)S(1)} %copy-done.3, f32[2,128,128]{2,1,0:T(8,128)S(1)} %copy-done.2, ...), custom_call_target="tpu_custom_call" | custom-call | tf_op jit(solution)/shard_map/pallas_call | solution.py:316
  87.7 9.4 %all-to-all-start.1 = ((bf16[128,2,32,128]{3,2,1,0:T(8,128)(2,1)}), bf16[128,2,32,128]{3,2,1,0:T(8,128)(2,1)}, u32[]{:S(2)}, u32[]{:S(2)}) async-start(bf16[128,2,32,128]{3,2,1,0:T(8,128)(2,1)} %get-tuple-element.11), calls=%async_computation.1 | async-start | bytes 4194304 | tf_op jit(solution)/shard_map/all_to_all | solution.py:487
  97.1 0.0 copy-done.7
  97.2 0.0 copy-done.8
  97.2 0.0 copy-done.10
  97.2 3.5 %shard_map.144 = f32[32,128,128]{2,1,0:T(8,128)S(1)} custom-call(bf16[32,128,256]{2,1,0:T(8,128)(2,1)S(1)} %copy-done.7, f32[2,128,128]{2,1,0:T(8,128)S(1)} %copy-done.2, bf16[2,256,256]{2,1,0:T(8,128)(2,1)S(1)} %copy-done.8, bf16[2,128,256]{2,1,0:T(8,128)(2,1)S(1)} %copy-done.10), custom_call_target="tpu_custom_call" | custom-call | flops 4294967296 | bytes 4194304 | tf_op jit(solution)/shard_map/pallas_call | solution.py:349
  100.7 0.1 select_convert_fusion
  100.8 0.0 copy-start
  100.8 3.2 %collective-permute-start.1 = (bf16[32,64,128]{2,1,0:T(8,128)(2,1)S(1)}, bf16[32,64,128]{2,1,0:T(8,128)(2,1)S(1)}, u32[]{:S(2)}, u32[]{:S(2)}) collective-permute-start(bf16[32,64,128]{2,1,0:T(8,128)(2,1)S(1)} %select_convert_fusion), channel_id=1, source_target_pairs={{0,128},{128,0},{1,129},{129,1},{2,130},{130,2},{3,131},{131,3},{4... | collective-permute-start | bytes 1572872 | tf_op jit(solution)/shard_map/ppermute | solution.py:515
  104.0 22.1 %collective-permute-done.1 = bf16[32,64,128]{2,1,0:T(8,128)(2,1)S(1)} collective-permute-done((bf16[32,64,128]{2,1,0:T(8,128)(2,1)S(1)}, bf16[32,64,128]{2,1,0:T(8,128)(2,1)S(1)}, u32[]{:S(2)}, u32[]{:S(2)}) %collective-permute-start.1) | collective-permute-done | bytes 524320 | tf_op jit(solution)/shard_map/ppermute | solution.py:515
  126.1 0.3 convert_add_fusion
  126.3 1.6 copy.19
  127.9 19.1 %all-to-all-done.1.ret_ref = bf16[128,2,32,128]{3,2,1,0:T(8,128)(2,1)} async-done(((bf16[128,2,32,128]{3,2,1,0:T(8,128)(2,1)}), bf16[128,2,32,128]{3,2,1,0:T(8,128)(2,1)}, u32[]{:S(2)}, u32[]{:S(2)}) %all-to-all-start.1) | async-done | bytes 2097184 | tf_op jit(solution)/shard_map/all_to_all | solution.py:487
  147.0 5.9 %shard_map.145 = (f32[16,32,128]{2,1,0:T(8,128)}, f32[8,4096]{1,0:T(8,128)}) custom-call(bf16[128,2,32,128]{3,2,1,0:T(8,128)(2,1)} %all-to-all-done.1.ret_ref, bf16[3,128,4096]{2,1,0:T(8,128)(2,1)S(1)} %bitcast.16, f32[8,4096]{1,0:T(8,128)S(1)} %collective-permute-done.edge_ref, f32[3,3,4096]{2,1,0:T(4,128)S(1)} %copy-done.1, bf16[128,4096]{1,0:T(8,128)(2,1)} %bitcast.20), custom_call_target="tpu_custom_call" | custom-call | tf_op jit(solution)/shard_map/pallas_call | solution.py:417
  152.9 9.8 %all-to-all-start.2 = ((f32[256,2,128]{2,1,0:T(2,128)}), f32[256,2,128]{2,1,0:T(2,128)S(1)}, u32[]{:S(2)}, u32[]{:S(2)}) async-start(f32[256,2,128]{2,1,0:T(2,128)} %bitcast.26), calls=%async_computation.2 | async-start | bytes 524288 | tf_op jit(solution)/shard_map/all_to_all | solution.py:487
  162.7 4.1 %collective-permute-start.2 = (f32[8,4096]{1,0:T(8,128)}, f32[8,4096]{1,0:T(8,128)S(1)}, u32[]{:S(2)}, u32[]{:S(2)}) collective-permute-start(f32[8,4096]{1,0:T(8,128)} %get-tuple-element.15), channel_id=1, source_target_pairs={{1,0},{2,1},{3,2},{4,3},{5,4},{6,5},{7,6},{8,7},{9,8},{10,9},{11,1... | collective-permute-start | bytes 393224 | tf_op jit(solution)/shard_map/ppermute | solution.py:483
  166.7 11.5 %all-to-all-done.2 = f32[256,2,128]{2,1,0:T(2,128)S(1)} async-done(((f32[256,2,128]{2,1,0:T(2,128)}), f32[256,2,128]{2,1,0:T(2,128)S(1)}, u32[]{:S(2)}, u32[]{:S(2)}) %all-to-all-start.2) | async-done | bytes 262176 | tf_op jit(solution)/shard_map/all_to_all | solution.py:487
  178.3 0.3 reduce_sum.9
  178.6 0.0 collective-permute-done.2.later_ref
  178.6 0.7 broadcast_in_dim.10
  179.3 5.8 %all-to-all-start.3 = ((bf16[256,2,128]{2,1,0:T(2,128)(2,1)}), bf16[256,2,128]{2,1,0:T(2,128)(2,1)S(1)}, u32[]{:S(2)}, u32[]{:S(2)}) async-start(bf16[256,2,128]{2,1,0:T(2,128)(2,1)} %broadcast_in_dim.10), calls=%async_computation.3 | async-start | bytes 262144 | tf_op jit(solution)/shard_map/all_to_all | solution.py:487
  185.1 7.8 %shard_map.146 = bf16[3,128,4096]{2,1,0:T(8,128)(2,1)} custom-call(bf16[128,2,32,128]{3,2,1,0:T(8,128)(2,1)} %all-to-all-done.1.ret_ref, bf16[3,128,4096]{2,1,0:T(8,128)(2,1)} %bitcast.15, f32[8,4096]{1,0:T(8,128)S(1)} %collective-permute-done.edge_ref, f32[3,3,4096]{2,1,0:T(4,128)S(1)} %copy-done.1, bf16[128,4096]{1,0:T(8,128)(2,1)} %bitcast.21, ...), custom_call_target="tpu_custom_call" | custom-call | flops 31457280 | bytes 9437184 | tf_op jit(solution)/shard_map/pallas_call | solution.py:461
  192.9 5.0 %all-to-all-done.3 = bf16[256,2,128]{2,1,0:T(2,128)(2,1)S(1)} async-done(((bf16[256,2,128]{2,1,0:T(2,128)(2,1)}), bf16[256,2,128]{2,1,0:T(2,128)(2,1)S(1)}, u32[]{:S(2)}, u32[]{:S(2)}) %all-to-all-start.3) | async-done | bytes 131104 | tf_op jit(solution)/shard_map/all_to_all | solution.py:487
  197.9 0.1 slice_convert_fusion
  198.0 0.8 reshape.25
  (4 shorter events, 0.0 us)
Async XLA Ops:
  0.6 5.7 %copy-start.1 = (f32[3,3,4096]{2,1,0:T(4,128)S(1)}, f32[3,3,4096]{2,1,0:T(4,128)}, u32[]{:S(2)}) copy-start(f32[3,3,4096]{2,1,0:T(4,128)} %taps_ref.7) | copy-start | bytes 442372
  1.7 8.7 %collective-permute-start = (f32[8,4096]{1,0:T(8,128)S(1)}, f32[8,4096]{1,0:T(8,128)S(1)}, u32[]{:S(2)}, u32[]{:S(2)}) collective-permute-start(f32[8,4096]{1,0:T(8,128)S(1)} %shard_map.140), channel_id=1, source_target_pairs={{0,1},{1,2},{2,3},{3,4},{4,5},{5,6},{6,7},{7,8},{8,9},{9,10},{10,1... | collective-permute-start | bytes 393224 | tf_op jit(solution)/shard_map/ppermute | solution.py:483
  13.1 63.6 %all-to-all-start = ((bf16[128,2,32,128]{3,2,1,0:T(8,128)(2,1)}), bf16[128,2,32,128]{3,2,1,0:T(8,128)(2,1)S(1)}, u32[]{:S(2)}, u32[]{:S(2)}) async-start(bf16[128,2,32,128]{3,2,1,0:T(8,128)(2,1)} %shard_map.141), calls=%async_computation | async-start | bytes 4194304 | tf_op jit(solution)/shard_map/all_to_all | solution.py:487
  26.5 2.1 %copy-start.2 = (f32[2,128,128]{2,1,0:T(8,128)S(1)}, f32[2,128,128]{2,1,0:T(8,128)}, u32[]{:S(2)}) copy-start(f32[2,128,128]{2,1,0:T(8,128)} %constant.27.clone.turn_ref) | copy-start | bytes 393220
  26.6 2.1 %copy-start.3 = (bf16[256,256]{1,0:T(8,128)(2,1)S(1)}, bf16[256,256]{1,0:T(8,128)(2,1)}, u32[]{:S(2)}) copy-start(bf16[256,256]{1,0:T(8,128)(2,1)} %constant.26.clone.fwd_a_ref) | copy-start | bytes 393220
  26.6 2.1 %copy-start.9 = (bf16[2,256,256]{2,1,0:T(8,128)(2,1)S(1)}, bf16[2,256,256]{2,1,0:T(8,128)(2,1)}, u32[]{:S(2)}) copy-start(bf16[2,256,256]{2,1,0:T(8,128)(2,1)} %constant.28.clone.fwd_b_ref) | copy-start | bytes 786436
  28.6 48.1 %copy-start.4 = (bf16[1,256,256]{2,1,0:T(8,128)(2,1)S(1)}, bf16[1,256,256]{2,1,0:T(8,128)(2,1)}, u32[]{:S(2)}) copy-start(bf16[1,256,256]{2,1,0:T(8,128)(2,1)} %constant.29.clone.fwd_b_ref) | copy-start | bytes 393220
  28.6 48.1 %copy-start.5 = (bf16[1,256,256]{2,1,0:T(8,128)(2,1)S(1)}, bf16[1,256,256]{2,1,0:T(8,128)(2,1)}, u32[]{:S(2)}) copy-start(bf16[1,256,256]{2,1,0:T(8,128)(2,1)} %constant.30.clone.inv_b_ref) | copy-start | bytes 393220
  28.7 48.1 %copy-start.6 = (bf16[1,128,256]{2,1,0:T(8,128)(2,1)S(1)}, bf16[1,128,256]{2,1,0:T(8,128)(2,1)}, u32[]{:S(2)}) copy-start(bf16[1,128,256]{2,1,0:T(8,128)(2,1)} %constant.31.clone.inv_a_ref) | copy-start | bytes 196612
  87.7 9.4 %copy-start.7 = (bf16[32,128,256]{2,1,0:T(8,128)(2,1)S(1)}, bf16[32,128,256]{2,1,0:T(8,128)(2,1)}, u32[]{:S(2)}) copy-start(bf16[32,128,256]{2,1,0:T(8,128)(2,1)} %get-tuple-element.12.products_ref) | copy-start | bytes 6291460
  87.7 9.4 %copy-start.8 = (bf16[2,256,256]{2,1,0:T(8,128)(2,1)S(1)}, bf16[2,256,256]{2,1,0:T(8,128)(2,1)}, u32[]{:S(2)}) copy-start(bf16[2,256,256]{2,1,0:T(8,128)(2,1)} %constant.32.clone.inv_b_ref) | copy-start | bytes 786436
  87.7 9.4 %copy-start.10 = (bf16[2,128,256]{2,1,0:T(8,128)(2,1)S(1)}, bf16[2,128,256]{2,1,0:T(8,128)(2,1)}, u32[]{:S(2)}) copy-start(bf16[2,128,256]{2,1,0:T(8,128)(2,1)} %constant.33.clone.inv_a_ref) | copy-start | bytes 393220
  87.7 59.2 %all-to-all-start.1 = ((bf16[128,2,32,128]{3,2,1,0:T(8,128)(2,1)}), bf16[128,2,32,128]{3,2,1,0:T(8,128)(2,1)}, u32[]{:S(2)}, u32[]{:S(2)}) async-start(bf16[128,2,32,128]{3,2,1,0:T(8,128)(2,1)} %get-tuple-element.11), calls=%async_computation.1 | async-start | bytes 4194304 | tf_op jit(solution)/shard_map/all_to_all | solution.py:487
  100.8 46.2 %copy-start = (bf16[3,1,128,4096]{3,2,1,0:T(8,128)(2,1)S(1)}, bf16[3,1,128,4096]{3,2,1,0:T(8,128)(2,1)}, u32[]{:S(2)}) copy-start(bf16[3,1,128,4096]{3,2,1,0:T(8,128)(2,1)} %param.12) | copy-start | bytes 9437188
  100.8 25.2 %collective-permute-start.1 = (bf16[32,64,128]{2,1,0:T(8,128)(2,1)S(1)}, bf16[32,64,128]{2,1,0:T(8,128)(2,1)S(1)}, u32[]{:S(2)}, u32[]{:S(2)}) collective-permute-start(bf16[32,64,128]{2,1,0:T(8,128)(2,1)S(1)} %select_convert_fusion), channel_id=1, source_target_pairs={{0,128},{128,0},{1,129},{129,1},{2,130},{130,2},{3,131},{131,3},{4... | collective-permute-start | bytes 1572872 | tf_op jit(solution)/shard_map/ppermute | solution.py:515
  152.9 25.4 %all-to-all-start.2 = ((f32[256,2,128]{2,1,0:T(2,128)}), f32[256,2,128]{2,1,0:T(2,128)S(1)}, u32[]{:S(2)}, u32[]{:S(2)}) async-start(f32[256,2,128]{2,1,0:T(2,128)} %bitcast.26), calls=%async_computation.2 | async-start | bytes 524288 | tf_op jit(solution)/shard_map/all_to_all | solution.py:487
  162.7 15.9 %collective-permute-start.2 = (f32[8,4096]{1,0:T(8,128)}, f32[8,4096]{1,0:T(8,128)S(1)}, u32[]{:S(2)}, u32[]{:S(2)}) collective-permute-start(f32[8,4096]{1,0:T(8,128)} %get-tuple-element.15), channel_id=1, source_target_pairs={{1,0},{2,1},{3,2},{4,3},{5,4},{6,5},{7,6},{8,7},{9,8},{10,9},{11,1... | collective-permute-start | bytes 393224 | tf_op jit(solution)/shard_map/ppermute | solution.py:483
  179.3 18.7 %all-to-all-start.3 = ((bf16[256,2,128]{2,1,0:T(2,128)(2,1)}), bf16[256,2,128]{2,1,0:T(2,128)(2,1)S(1)}, u32[]{:S(2)}, u32[]{:S(2)}) async-start(bf16[256,2,128]{2,1,0:T(2,128)(2,1)} %broadcast_in_dim.10), calls=%async_computation.3 | async-start | bytes 262144 | tf_op jit(solution)/shard_map/all_to_all | solution.py:487

commit v4 on v3

--- a/solution.py
+++ b/solution.py
@@ -268,19 +268,22 @@
     out_ref, lag_ref, rows_ref, outs_ref, *, group,
 ):
     block = out_ref.shape[2]
+    pitch = rows_ref.shape[1] // ROWS
     part = pl.program_id(1)
     here = pl.ds(pl.multiple_of(pl.program_id(0) * block, block), block)
 
     @pl.when(part == 0)
     def _():
         for at in range(2):
-            rows_ref[at] = in_ref[:, at, here].astype(jnp.float32).reshape(ROWS * block, ROWS)
+            rows = in_ref[:, at, here].astype(jnp.float32)
+            spare = jnp.zeros((ROWS, pitch - block, ROWS), jnp.float32)
+            rows_ref[at] = jnp.concatenate([rows, spare], axis=1).reshape(ROWS * pitch, ROWS)
 
     cos_w, sin_w = turn_ref[0], turn_ref[1]
 
     def some():
         chans = [part * group + at for at in range(group)]
-        places = [(at, pl.ds(ch, ROWS, stride=block)) for ch in chans for at in range(2)]
+        places = [(at, pl.ds(ch, ROWS, stride=pitch)) for ch in chans for at in range(2)]
         rows = [rows_ref[at, strided, :].astype(jnp.bfloat16) for at, strided in places]
         columns = jnp.concatenate(rows, axis=1)
         y = dot(fwd_a_ref[...], jnp.concatenate([columns, columns], axis=0))
@@ -307,7 +310,8 @@
     @pl.when(part == pl.num_programs(1) - 1)
     def _():
         for at in range(2):
-            out_ref[:, at] = outs_ref[at].astype(jnp.bfloat16).reshape(ROWS, block, ROWS)
+            rows = outs_ref[at].reshape(ROWS, pitch, ROWS)[:, :block]
+            out_ref[:, at] = rows.astype(jnp.bfloat16)
 
 
 def convolve(received, spec, tab, group=8, block=16):
@@ -329,7 +333,7 @@
             pltpu.HBM((ROWS, 2, width, ROWS), jnp.bfloat16),
             pltpu.HBM((width, ROWS, 2 * ROWS), jnp.bfloat16),
         ],
-        scratch_shapes=[pltpu.VMEM((2, ROWS * block, ROWS), jnp.float32)] * 2,
+        scratch_shapes=[pltpu.VMEM((2, ROWS * (block + 8), ROWS), jnp.float32)] * 2,
         compiler_params=params(40),
     )(received, held(spec), *(tab[name] for name in names))
 

time: 199 us -> 198 us (level)
  no operation moved by 1% of the time
where the time goes in v4:
time: 198 us; the launch traced here: 197 us
  waiting for transfers between devices  95.6 us (48%)
  starting transfers between devices  50.1 us (25%)
  Pallas kernels  44.5 us (22%)
  local copies, waits for them, and re-layouts  5.22 us (3%)
    all_to_all x4, waiting for transfers between devices, exchanged(): return lax.all_to_all(value, axes, split_axis=0, concat_axis=0, tiled=True)  73.3 us
    all_to_all x4, starting transfers between devices, exchanged(): return lax.all_to_all(value, axes, split_axis=0, concat_axis=0, tiled=True)  38.5 us
    ppermute x1, waiting for transfers between devices, local(): lax.ppermute(jnp.where(second, lower, upper).astype(jnp.bfloat16), 'dp',...  22.2 us
    pallas_call x1, Pallas kernels, spectrum(): pl.pallas_call(spectrum_kernel, grid=(width // block,), in_specs=[pl.Bloc...  10.4 us
    pallas_call x1, Pallas kernels, convolve(): pl.pallas_call(functools.partial(conv_kernel, group=group), grid=(width /...  9.13 us
    ppermute x2, starting transfers between devices, passed_along(): lax.ppermute(value, 'ctx', [(source, source + steps) for source in range(...  8.65 us
    pallas_call x1, Pallas kernels, stream_grads(): pl.pallas_call(grads_kernel, grid=(channels // block,), in_specs=local_sp...  7.79 us
    pallas_call x1, Pallas kernels, tap_sums(): pl.pallas_call(sums_kernel, grid=(channels // block,), in_specs=specs, ou...  5.91 us
  transfers between devices with their start and end apart: 7, of which 5 were waited for; matrix products, arithmetic and copies ran while one was open for 2% of the time, Pallas kernels for 13%

profile of v4, /device:TPU:1, one launch (start us, length us, event | category | flops | bytes accessed | tf_op | source)
XLA Modules:
  0.0 197.0 jit_solution(14738953432110693379)
XLA Ops:
  0.6 0.0 copy-start.1
  0.6 1.1 shard_map.140
  1.7 4.6 %collective-permute-start = (f32[8,4096]{1,0:T(8,128)S(1)}, f32[8,4096]{1,0:T(8,128)S(1)}, u32[]{:S(2)}, u32[]{:S(2)}) collective-permute-start(f32[8,4096]{1,0:T(8,128)S(1)} %shard_map.140), channel_id=1, source_target_pairs={{0,1},{1,2},{2,3},{3,4},{4,5},{5,6},{6,7},{7,8},{8,9},{9,10},{10,1... | collective-permute-start | bytes 393224 | tf_op jit(solution)/shard_map/ppermute | solution.py:487
  6.3 0.0 copy-done.1
  6.3 4.1 %shard_map.139.rough_ref = bf16[128,2,32,128]{3,2,1,0:T(8,128)(2,1)S(1)} custom-call(bf16[3,128,4096]{2,1,0:T(8,128)(2,1)} %bitcast.13, f32[3,3,4096]{2,1,0:T(4,128)S(1)} %copy-done.1, bf16[128,4096]{1,0:T(8,128)(2,1)} %bitcast.18), custom_call_target="tpu_custom_call" | custom-call | flops 20971520 | bytes 6291456 | tf_op jit(solution)/shard_map/pallas_call | solution.py:134
  10.4 0.0 collective-permute-done.edge_ref
  10.4 2.7 %shard_map.141 = bf16[128,2,32,128]{3,2,1,0:T(8,128)(2,1)} custom-call(bf16[128,2,32,128]{3,2,1,0:T(8,128)(2,1)S(1)} %shard_map.139.rough_ref, bf16[3,128,4096]{2,1,0:T(8,128)(2,1)} %bitcast.14, f32[8,4096]{1,0:T(8,128)S(1)} %collective-permute-done.edge_ref, f32[3,3,4096]{2,1,0:T(4,128)S(1)} %copy-done.1, bf16[128,4096]{1,0:T(8,128)(2,1)} %bitcast.19), custom_call_target="tpu_custom_call" | custom-call | tf_op jit(solution)/shard_map/pallas_call | solution.py:177
  13.1 13.4 %all-to-all-start = ((bf16[128,2,32,128]{3,2,1,0:T(8,128)(2,1)}), bf16[128,2,32,128]{3,2,1,0:T(8,128)(2,1)S(1)}, u32[]{:S(2)}, u32[]{:S(2)}) async-start(bf16[128,2,32,128]{3,2,1,0:T(8,128)(2,1)} %shard_map.141), calls=%async_computation | async-start | bytes 4194304 | tf_op jit(solution)/shard_map/all_to_all | solution.py:491
  26.5 0.0 copy-start.2
  26.6 0.0 copy-start.3
  26.6 0.0 copy-start.9
  26.6 2.0 %copy.16 = f32[4,8,128,128]{3,2,1,0:T(8,128)S(1)} copy(f32[4,8,128,128]{3,1,2,0:T(8,128)} %bitcast.24) | data formatting | bytes 4194304
  28.6 0.0 copy-done.2
  28.6 0.0 copy-done.3
  28.6 0.0 copy-done.9
  28.6 0.0 copy-start.4
  28.6 0.0 copy-start.5
  28.7 0.0 copy-start.6
  28.7 10.4 %shard_map.142.spec_ref = f32[32,128,256]{2,1,0:T(8,128)} custom-call(f32[32,128,128]{2,1,0:T(8,128)S(1)} %bitcast.17, bf16[256,256]{1,0:T(8,128)(2,1)S(1)} %copy-done.3, f32[2,128,128]{2,1,0:T(8,128)S(1)} %copy-done.2, bf16[2,256,256]{2,1,0:T(8,128)(2,1)S(1)} %copy-done.9), custom_call_target="tpu_custom_call" | custom-call | flops 5368709120 | bytes 6291456 | tf_op jit(solution)/shard_map/pallas_call | solution.py:218
  39.0 37.7 %all-to-all-done.in_ref = bf16[128,2,32,128]{3,2,1,0:T(8,128)(2,1)S(1)} async-done(((bf16[128,2,32,128]{3,2,1,0:T(8,128)(2,1)}), bf16[128,2,32,128]{3,2,1,0:T(8,128)(2,1)S(1)}, u32[]{:S(2)}, u32[]{:S(2)}) %all-to-all-start) | async-done | bytes 2097184 | tf_op jit(solution)/shard_map/all_to_all | solution.py:491
  76.7 0.0 copy-done.4
  76.7 0.0 copy-done.5
  76.7 0.0 copy-done.6
  76.7 9.1 %shard_map.143 = (bf16[128,2,32,128]{3,2,1,0:T(8,128)(2,1)}, bf16[32,128,256]{2,1,0:T(8,128)(2,1)}) custom-call(bf16[128,2,32,128]{3,2,1,0:T(8,128)(2,1)S(1)} %all-to-all-done.in_ref, f32[32,128,256]{2,1,0:T(8,128)} %shard_map.142.spec_ref, bf16[256,256]{1,0:T(8,128)(2,1)S(1)} %copy-done.3, f32[2,128,128]{2,1,0:T(8,128)S(1)} %copy-done.2, ...), custom_call_target="tpu_custom_call" | custom-call | tf_op jit(solution)/shard_map/pallas_call | solution.py:320
  85.9 9.4 %all-to-all-start.1 = ((bf16[128,2,32,128]{3,2,1,0:T(8,128)(2,1)}), bf16[128,2,32,128]{3,2,1,0:T(8,128)(2,1)}, u32[]{:S(2)}, u32[]{:S(2)}) async-start(bf16[128,2,32,128]{3,2,1,0:T(8,128)(2,1)} %get-tuple-element.11), calls=%async_computation.1 | async-start | bytes 4194304 | tf_op jit(solution)/shard_map/all_to_all | solution.py:491
  95.3 0.0 copy-done.7
  95.3 0.0 copy-done.8
  95.3 0.0 copy-done.10
  95.3 3.5 %shard_map.144 = f32[32,128,128]{2,1,0:T(8,128)S(1)} custom-call(bf16[32,128,256]{2,1,0:T(8,128)(2,1)S(1)} %copy-done.7, f32[2,128,128]{2,1,0:T(8,128)S(1)} %copy-done.2, bf16[2,256,256]{2,1,0:T(8,128)(2,1)S(1)} %copy-done.8, bf16[2,128,256]{2,1,0:T(8,128)(2,1)S(1)} %copy-done.10), custom_call_target="tpu_custom_call" | custom-call | flops 4294967296 | bytes 4194304 | tf_op jit(solution)/shard_map/pallas_call | solution.py:353
  98.8 0.1 select_convert_fusion
  98.9 0.0 copy-start
  99.0 3.0 %collective-permute-start.1 = (bf16[32,64,128]{2,1,0:T(8,128)(2,1)S(1)}, bf16[32,64,128]{2,1,0:T(8,128)(2,1)S(1)}, u32[]{:S(2)}, u32[]{:S(2)}) collective-permute-start(bf16[32,64,128]{2,1,0:T(8,128)(2,1)S(1)} %select_convert_fusion), channel_id=1, source_target_pairs={{0,128},{128,0},{1,129},{129,1},{2,130},{130,2},{3,131},{131,3},{4... | collective-permute-start | bytes 1572872 | tf_op jit(solution)/shard_map/ppermute | solution.py:519
  102.0 22.2 %collective-permute-done.1 = bf16[32,64,128]{2,1,0:T(8,128)(2,1)S(1)} collective-permute-done((bf16[32,64,128]{2,1,0:T(8,128)(2,1)S(1)}, bf16[32,64,128]{2,1,0:T(8,128)(2,1)S(1)}, u32[]{:S(2)}, u32[]{:S(2)}) %collective-permute-start.1) | collective-permute-done | bytes 524320 | tf_op jit(solution)/shard_map/ppermute | solution.py:519
  124.2 0.3 convert_add_fusion
  124.5 1.6 copy.19
  126.0 19.1 %all-to-all-done.1.ret_ref = bf16[128,2,32,128]{3,2,1,0:T(8,128)(2,1)} async-done(((bf16[128,2,32,128]{3,2,1,0:T(8,128)(2,1)}), bf16[128,2,32,128]{3,2,1,0:T(8,128)(2,1)}, u32[]{:S(2)}, u32[]{:S(2)}) %all-to-all-start.1) | async-done | bytes 2097184 | tf_op jit(solution)/shard_map/all_to_all | solution.py:491
  145.1 5.9 %shard_map.145 = (f32[16,32,128]{2,1,0:T(8,128)}, f32[8,4096]{1,0:T(8,128)}) custom-call(bf16[128,2,32,128]{3,2,1,0:T(8,128)(2,1)} %all-to-all-done.1.ret_ref, bf16[3,128,4096]{2,1,0:T(8,128)(2,1)S(1)} %bitcast.16, f32[8,4096]{1,0:T(8,128)S(1)} %collective-permute-done.edge_ref, f32[3,3,4096]{2,1,0:T(4,128)S(1)} %copy-done.1, bf16[128,4096]{1,0:T(8,128)(2,1)} %bitcast.20), custom_call_target="tpu_custom_call" | custom-call | tf_op jit(solution)/shard_map/pallas_call | solution.py:421
  151.0 9.8 %all-to-all-start.2 = ((f32[256,2,128]{2,1,0:T(2,128)}), f32[256,2,128]{2,1,0:T(2,128)S(1)}, u32[]{:S(2)}, u32[]{:S(2)}) async-start(f32[256,2,128]{2,1,0:T(2,128)} %bitcast.26), calls=%async_computation.2 | async-start | bytes 524288 | tf_op jit(solution)/shard_map/all_to_all | solution.py:491
  160.8 4.1 %collective-permute-start.2 = (f32[8,4096]{1,0:T(8,128)}, f32[8,4096]{1,0:T(8,128)S(1)}, u32[]{:S(2)}, u32[]{:S(2)}) collective-permute-start(f32[8,4096]{1,0:T(8,128)} %get-tuple-element.15), channel_id=1, source_target_pairs={{1,0},{2,1},{3,2},{4,3},{5,4},{6,5},{7,6},{8,7},{9,8},{10,9},{11,1... | collective-permute-start | bytes 393224 | tf_op jit(solution)/shard_map/ppermute | solution.py:487
  164.9 11.5 %all-to-all-done.2 = f32[256,2,128]{2,1,0:T(2,128)S(1)} async-done(((f32[256,2,128]{2,1,0:T(2,128)}), f32[256,2,128]{2,1,0:T(2,128)S(1)}, u32[]{:S(2)}, u32[]{:S(2)}) %all-to-all-start.2) | async-done | bytes 262176 | tf_op jit(solution)/shard_map/all_to_all | solution.py:491
  176.4 0.3 reduce_sum.9
  176.7 0.0 collective-permute-done.2.later_ref
  176.7 0.7 broadcast_in_dim.10
  177.4 5.8 %all-to-all-start.3 = ((bf16[256,2,128]{2,1,0:T(2,128)(2,1)}), bf16[256,2,128]{2,1,0:T(2,128)(2,1)S(1)}, u32[]{:S(2)}, u32[]{:S(2)}) async-start(bf16[256,2,128]{2,1,0:T(2,128)(2,1)} %broadcast_in_dim.10), calls=%async_computation.3 | async-start | bytes 262144 | tf_op jit(solution)/shard_map/all_to_all | solution.py:491
  183.3 7.8 %shard_map.146 = bf16[3,128,4096]{2,1,0:T(8,128)(2,1)} custom-call(bf16[128,2,32,128]{3,2,1,0:T(8,128)(2,1)} %all-to-all-done.1.ret_ref, bf16[3,128,4096]{2,1,0:T(8,128)(2,1)} %bitcast.15, f32[8,4096]{1,0:T(8,128)S(1)} %collective-permute-done.edge_ref, f32[3,3,4096]{2,1,0:T(4,128)S(1)} %copy-done.1, bf16[128,4096]{1,0:T(8,128)(2,1)} %bitcast.21, ...), custom_call_target="tpu_custom_call" | custom-call | flops 31457280 | bytes 9437184 | tf_op jit(solution)/shard_map/pallas_call | solution.py:465
  191.1 5.0 %all-to-all-done.3 = bf16[256,2,128]{2,1,0:T(2,128)(2,1)S(1)} async-done(((bf16[256,2,128]{2,1,0:T(2,128)(2,1)}), bf16[256,2,128]{2,1,0:T(2,128)(2,1)S(1)}, u32[]{:S(2)}, u32[]{:S(2)}) %all-to-all-start.3) | async-done | bytes 131104 | tf_op jit(solution)/shard_map/all_to_all | solution.py:491
  196.1 0.1 slice_convert_fusion
  196.1 0.8 reshape.25
  (4 shorter events, 0.0 us)
Async XLA Ops:
  0.6 5.7 %copy-start.1 = (f32[3,3,4096]{2,1,0:T(4,128)S(1)}, f32[3,3,4096]{2,1,0:T(4,128)}, u32[]{:S(2)}) copy-start(f32[3,3,4096]{2,1,0:T(4,128)} %taps_ref.7) | copy-start | bytes 442372
  1.7 8.7 %collective-permute-start = (f32[8,4096]{1,0:T(8,128)S(1)}, f32[8,4096]{1,0:T(8,128)S(1)}, u32[]{:S(2)}, u32[]{:S(2)}) collective-permute-start(f32[8,4096]{1,0:T(8,128)S(1)} %shard_map.140), channel_id=1, source_target_pairs={{0,1},{1,2},{2,3},{3,4},{4,5},{5,6},{6,7},{7,8},{8,9},{9,10},{10,1... | collective-permute-start | bytes 393224 | tf_op jit(solution)/shard_map/ppermute | solution.py:487
  13.1 63.6 %all-to-all-start = ((bf16[128,2,32,128]{3,2,1,0:T(8,128)(2,1)}), bf16[128,2,32,128]{3,2,1,0:T(8,128)(2,1)S(1)}, u32[]{:S(2)}, u32[]{:S(2)}) async-start(bf16[128,2,32,128]{3,2,1,0:T(8,128)(2,1)} %shard_map.141), calls=%async_computation | async-start | bytes 4194304 | tf_op jit(solution)/shard_map/all_to_all | solution.py:491
  26.5 2.1 %copy-start.2 = (f32[2,128,128]{2,1,0:T(8,128)S(1)}, f32[2,128,128]{2,1,0:T(8,128)}, u32[]{:S(2)}) copy-start(f32[2,128,128]{2,1,0:T(8,128)} %constant.27.clone.turn_ref) | copy-start | bytes 393220
  26.6 2.1 %copy-start.3 = (bf16[256,256]{1,0:T(8,128)(2,1)S(1)}, bf16[256,256]{1,0:T(8,128)(2,1)}, u32[]{:S(2)}) copy-start(bf16[256,256]{1,0:T(8,128)(2,1)} %constant.26.clone.fwd_a_ref) | copy-start | bytes 393220
  26.6 2.1 %copy-start.9 = (bf16[2,256,256]{2,1,0:T(8,128)(2,1)S(1)}, bf16[2,256,256]{2,1,0:T(8,128)(2,1)}, u32[]{:S(2)}) copy-start(bf16[2,256,256]{2,1,0:T(8,128)(2,1)} %constant.28.clone.fwd_b_ref) | copy-start | bytes 786436
  28.6 48.1 %copy-start.4 = (bf16[1,256,256]{2,1,0:T(8,128)(2,1)S(1)}, bf16[1,256,256]{2,1,0:T(8,128)(2,1)}, u32[]{:S(2)}) copy-start(bf16[1,256,256]{2,1,0:T(8,128)(2,1)} %constant.29.clone.fwd_b_ref) | copy-start | bytes 393220
  28.6 48.1 %copy-start.5 = (bf16[1,256,256]{2,1,0:T(8,128)(2,1)S(1)}, bf16[1,256,256]{2,1,0:T(8,128)(2,1)}, u32[]{:S(2)}) copy-start(bf16[1,256,256]{2,1,0:T(8,128)(2,1)} %constant.30.clone.inv_b_ref) | copy-start | bytes 393220
  28.7 48.1 %copy-start.6 = (bf16[1,128,256]{2,1,0:T(8,128)(2,1)S(1)}, bf16[1,128,256]{2,1,0:T(8,128)(2,1)}, u32[]{:S(2)}) copy-start(bf16[1,128,256]{2,1,0:T(8,128)(2,1)} %constant.31.clone.inv_a_ref) | copy-start | bytes 196612
  85.9 9.4 %copy-start.7 = (bf16[32,128,256]{2,1,0:T(8,128)(2,1)S(1)}, bf16[32,128,256]{2,1,0:T(8,128)(2,1)}, u32[]{:S(2)}) copy-start(bf16[32,128,256]{2,1,0:T(8,128)(2,1)} %get-tuple-element.12.products_ref) | copy-start | bytes 6291460
  85.9 9.4 %copy-start.8 = (bf16[2,256,256]{2,1,0:T(8,128)(2,1)S(1)}, bf16[2,256,256]{2,1,0:T(8,128)(2,1)}, u32[]{:S(2)}) copy-start(bf16[2,256,256]{2,1,0:T(8,128)(2,1)} %constant.32.clone.inv_b_ref) | copy-start | bytes 786436
  85.9 9.5 %copy-start.10 = (bf16[2,128,256]{2,1,0:T(8,128)(2,1)S(1)}, bf16[2,128,256]{2,1,0:T(8,128)(2,1)}, u32[]{:S(2)}) copy-start(bf16[2,128,256]{2,1,0:T(8,128)(2,1)} %constant.33.clone.inv_a_ref) | copy-start | bytes 393220
  85.9 59.2 %all-to-all-start.1 = ((bf16[128,2,32,128]{3,2,1,0:T(8,128)(2,1)}), bf16[128,2,32,128]{3,2,1,0:T(8,128)(2,1)}, u32[]{:S(2)}, u32[]{:S(2)}) async-start(bf16[128,2,32,128]{3,2,1,0:T(8,128)(2,1)} %get-tuple-element.11), calls=%async_computation.1 | async-start | bytes 4194304 | tf_op jit(solution)/shard_map/all_to_all | solution.py:491
  98.9 46.2 %copy-start = (bf16[3,1,128,4096]{3,2,1,0:T(8,128)(2,1)S(1)}, bf16[3,1,128,4096]{3,2,1,0:T(8,128)(2,1)}, u32[]{:S(2)}) copy-start(bf16[3,1,128,4096]{3,2,1,0:T(8,128)(2,1)} %param.12) | copy-start | bytes 9437188
  99.0 25.2 %collective-permute-start.1 = (bf16[32,64,128]{2,1,0:T(8,128)(2,1)S(1)}, bf16[32,64,128]{2,1,0:T(8,128)(2,1)S(1)}, u32[]{:S(2)}, u32[]{:S(2)}) collective-permute-start(bf16[32,64,128]{2,1,0:T(8,128)(2,1)S(1)} %select_convert_fusion), channel_id=1, source_target_pairs={{0,128},{128,0},{1,129},{129,1},{2,130},{130,2},{3,131},{131,3},{4... | collective-permute-start | bytes 1572872 | tf_op jit(solution)/shard_map/ppermute | solution.py:519
  151.0 25.4 %all-to-all-start.2 = ((f32[256,2,128]{2,1,0:T(2,128)}), f32[256,2,128]{2,1,0:T(2,128)S(1)}, u32[]{:S(2)}, u32[]{:S(2)}) async-start(f32[256,2,128]{2,1,0:T(2,128)} %bitcast.26), calls=%async_computation.2 | async-start | bytes 524288 | tf_op jit(solution)/shard_map/all_to_all | solution.py:491
  160.8 15.9 %collective-permute-start.2 = (f32[8,4096]{1,0:T(8,128)}, f32[8,4096]{1,0:T(8,128)S(1)}, u32[]{:S(2)}, u32[]{:S(2)}) collective-permute-start(f32[8,4096]{1,0:T(8,128)} %get-tuple-element.15), channel_id=1, source_target_pairs={{1,0},{2,1},{3,2},{4,3},{5,4},{6,5},{7,6},{8,7},{9,8},{10,9},{11,1... | collective-permute-start | bytes 393224 | tf_op jit(solution)/shard_map/ppermute | solution.py:487
  177.4 18.7 %all-to-all-start.3 = ((bf16[256,2,128]{2,1,0:T(2,128)(2,1)}), bf16[256,2,128]{2,1,0:T(2,128)(2,1)S(1)}, u32[]{:S(2)}, u32[]{:S(2)}) async-start(bf16[256,2,128]{2,1,0:T(2,128)(2,1)} %broadcast_in_dim.10), calls=%async_computation.3 | async-start | bytes 262144 | tf_op jit(solution)/shard_map/all_to_all | solution.py:491

commit v5 on v4

--- a/solution.py
+++ b/solution.py
@@ -415,7 +415,7 @@
 
 def tap_sums(returned, proj, edge, taps, grad_out):
     channels = proj.shape[-1]
-    block = min(1024, channels)
+    block = min(2048, channels)
     specs = local_specs(block, returned.shape[2])
     specs[1] = pl.BlockSpec(memory_space=pltpu.VMEM)
     return pl.pallas_call(

time: 198 us -> 198 us (level)
  no operation moved by 1% of the time
where the time goes in v5:
time: 198 us; the launch traced here: 197 us
  waiting for transfers between devices  95.4 us (48%)
  starting transfers between devices  50.3 us (25%)
  Pallas kernels  44.6 us (23%)
  local copies, waits for them, and re-layouts  5.22 us (3%)
    all_to_all x4, waiting for transfers between devices, exchanged(): return lax.all_to_all(value, axes, split_axis=0, concat_axis=0, tiled=True)  73.3 us
    all_to_all x4, starting transfers between devices, exchanged(): return lax.all_to_all(value, axes, split_axis=0, concat_axis=0, tiled=True)  38.5 us
    ppermute x1, waiting for transfers between devices, local(): lax.ppermute(jnp.where(second, lower, upper).astype(jnp.bfloat16), 'dp',...  22.1 us
    pallas_call x1, Pallas kernels, spectrum(): pl.pallas_call(spectrum_kernel, grid=(width // block,), in_specs=[pl.Bloc...  10.4 us
    pallas_call x1, Pallas kernels, convolve(): pl.pallas_call(functools.partial(conv_kernel, group=group), grid=(width /...  9.13 us
    ppermute x2, starting transfers between devices, passed_along(): lax.ppermute(value, 'ctx', [(source, source + steps) for source in range(...  8.65 us
    pallas_call x1, Pallas kernels, stream_grads(): pl.pallas_call(grads_kernel, grid=(channels // block,), in_specs=local_sp...  7.79 us
    pallas_call x1, Pallas kernels, tap_sums(): pl.pallas_call(sums_kernel, grid=(channels // block,), in_specs=specs, ou...  5.95 us
  transfers between devices with their start and end apart: 7, of which 5 were waited for; matrix products, arithmetic and copies ran while one was open for 2% of the time, Pallas kernels for 13%

profile of v5, /device:TPU:1, one launch (start us, length us, event | category | flops | bytes accessed | tf_op | source)
XLA Modules:
  0.0 197.0 jit_solution(4101439828435543942)
XLA Ops:
  0.6 0.0 copy-start.1
  0.6 1.1 shard_map.140
  1.7 4.6 %collective-permute-start = (f32[8,4096]{1,0:T(8,128)S(1)}, f32[8,4096]{1,0:T(8,128)S(1)}, u32[]{:S(2)}, u32[]{:S(2)}) collective-permute-start(f32[8,4096]{1,0:T(8,128)S(1)} %shard_map.140), channel_id=1, source_target_pairs={{0,1},{1,2},{2,3},{3,4},{4,5},{5,6},{6,7},{7,8},{8,9},{9,10},{10,1... | collective-permute-start | bytes 393224 | tf_op jit(solution)/shard_map/ppermute | solution.py:487
  6.3 0.0 copy-done.1
  6.3 4.1 %shard_map.139.rough_ref = bf16[128,2,32,128]{3,2,1,0:T(8,128)(2,1)S(1)} custom-call(bf16[3,128,4096]{2,1,0:T(8,128)(2,1)} %bitcast.13, f32[3,3,4096]{2,1,0:T(4,128)S(1)} %copy-done.1, bf16[128,4096]{1,0:T(8,128)(2,1)} %bitcast.18), custom_call_target="tpu_custom_call" | custom-call | flops 20971520 | bytes 6291456 | tf_op jit(solution)/shard_map/pallas_call | solution.py:134
  10.4 0.0 collective-permute-done.edge_ref
  10.4 2.7 %shard_map.141 = bf16[128,2,32,128]{3,2,1,0:T(8,128)(2,1)} custom-call(bf16[128,2,32,128]{3,2,1,0:T(8,128)(2,1)S(1)} %shard_map.139.rough_ref, bf16[3,128,4096]{2,1,0:T(8,128)(2,1)} %bitcast.14, f32[8,4096]{1,0:T(8,128)S(1)} %collective-permute-done.edge_ref, f32[3,3,4096]{2,1,0:T(4,128)S(1)} %copy-done.1, bf16[128,4096]{1,0:T(8,128)(2,1)} %bitcast.19), custom_call_target="tpu_custom_call" | custom-call | tf_op jit(solution)/shard_map/pallas_call | solution.py:177
  13.1 13.4 %all-to-all-start = ((bf16[128,2,32,128]{3,2,1,0:T(8,128)(2,1)}), bf16[128,2,32,128]{3,2,1,0:T(8,128)(2,1)S(1)}, u32[]{:S(2)}, u32[]{:S(2)}) async-start(bf16[128,2,32,128]{3,2,1,0:T(8,128)(2,1)} %shard_map.141), calls=%async_computation | async-start | bytes 4194304 | tf_op jit(solution)/shard_map/all_to_all | solution.py:491
  26.5 0.0 copy-start.2
  26.6 0.0 copy-start.3
  26.6 0.0 copy-start.9
  26.6 2.0 %copy.16 = f32[4,8,128,128]{3,2,1,0:T(8,128)S(1)} copy(f32[4,8,128,128]{3,1,2,0:T(8,128)} %bitcast.24) | data formatting | bytes 4194304
  28.6 0.0 copy-done.2
  28.6 0.0 copy-done.3
  28.6 0.0 copy-done.9
  28.6 0.0 copy-start.4
  28.6 0.0 copy-start.5
  28.7 0.0 copy-start.6
  28.7 10.4 %shard_map.142.spec_ref = f32[32,128,256]{2,1,0:T(8,128)} custom-call(f32[32,128,128]{2,1,0:T(8,128)S(1)} %bitcast.17, bf16[256,256]{1,0:T(8,128)(2,1)S(1)} %copy-done.3, f32[2,128,128]{2,1,0:T(8,128)S(1)} %copy-done.2, bf16[2,256,256]{2,1,0:T(8,128)(2,1)S(1)} %copy-done.9), custom_call_target="tpu_custom_call" | custom-call | flops 5368709120 | bytes 6291456 | tf_op jit(solution)/shard_map/pallas_call | solution.py:218
  39.0 37.7 %all-to-all-done.in_ref = bf16[128,2,32,128]{3,2,1,0:T(8,128)(2,1)S(1)} async-done(((bf16[128,2,32,128]{3,2,1,0:T(8,128)(2,1)}), bf16[128,2,32,128]{3,2,1,0:T(8,128)(2,1)S(1)}, u32[]{:S(2)}, u32[]{:S(2)}) %all-to-all-start) | async-done | bytes 2097184 | tf_op jit(solution)/shard_map/all_to_all | solution.py:491
  76.7 0.0 copy-done.4
  76.7 0.0 copy-done.5
  76.7 0.0 copy-done.6
  76.7 9.1 %shard_map.143 = (bf16[128,2,32,128]{3,2,1,0:T(8,128)(2,1)}, bf16[32,128,256]{2,1,0:T(8,128)(2,1)}) custom-call(bf16[128,2,32,128]{3,2,1,0:T(8,128)(2,1)S(1)} %all-to-all-done.in_ref, f32[32,128,256]{2,1,0:T(8,128)} %shard_map.142.spec_ref, bf16[256,256]{1,0:T(8,128)(2,1)S(1)} %copy-done.3, f32[2,128,128]{2,1,0:T(8,128)S(1)} %copy-done.2, ...), custom_call_target="tpu_custom_call" | custom-call | tf_op jit(solution)/shard_map/pallas_call | solution.py:320
  85.9 9.4 %all-to-all-start.1 = ((bf16[128,2,32,128]{3,2,1,0:T(8,128)(2,1)}), bf16[128,2,32,128]{3,2,1,0:T(8,128)(2,1)}, u32[]{:S(2)}, u32[]{:S(2)}) async-start(bf16[128,2,32,128]{3,2,1,0:T(8,128)(2,1)} %get-tuple-element.11), calls=%async_computation.1 | async-start | bytes 4194304 | tf_op jit(solution)/shard_map/all_to_all | solution.py:491
  95.3 0.0 copy-done.7
  95.3 0.0 copy-done.8
  95.3 0.0 copy-done.10
  95.3 3.5 %shard_map.144 = f32[32,128,128]{2,1,0:T(8,128)S(1)} custom-call(bf16[32,128,256]{2,1,0:T(8,128)(2,1)S(1)} %copy-done.7, f32[2,128,128]{2,1,0:T(8,128)S(1)} %copy-done.2, bf16[2,256,256]{2,1,0:T(8,128)(2,1)S(1)} %copy-done.8, bf16[2,128,256]{2,1,0:T(8,128)(2,1)S(1)} %copy-done.10), custom_call_target="tpu_custom_call" | custom-call | flops 4294967296 | bytes 4194304 | tf_op jit(solution)/shard_map/pallas_call | solution.py:353
  98.8 0.1 select_convert_fusion
  98.9 0.0 copy-start
  99.0 3.2 %collective-permute-start.1 = (bf16[32,64,128]{2,1,0:T(8,128)(2,1)S(1)}, bf16[32,64,128]{2,1,0:T(8,128)(2,1)S(1)}, u32[]{:S(2)}, u32[]{:S(2)}) collective-permute-start(bf16[32,64,128]{2,1,0:T(8,128)(2,1)S(1)} %select_convert_fusion), channel_id=1, source_target_pairs={{0,128},{128,0},{1,129},{129,1},{2,130},{130,2},{3,131},{131,3},{4... | collective-permute-start | bytes 1572872 | tf_op jit(solution)/shard_map/ppermute | solution.py:519
  102.1 22.1 %collective-permute-done.1 = bf16[32,64,128]{2,1,0:T(8,128)(2,1)S(1)} collective-permute-done((bf16[32,64,128]{2,1,0:T(8,128)(2,1)S(1)}, bf16[32,64,128]{2,1,0:T(8,128)(2,1)S(1)}, u32[]{:S(2)}, u32[]{:S(2)}) %collective-permute-start.1) | collective-permute-done | bytes 524320 | tf_op jit(solution)/shard_map/ppermute | solution.py:519
  124.2 0.3 convert_add_fusion
  124.5 1.6 copy.19
  126.0 19.1 %all-to-all-done.1.ret_ref = bf16[128,2,32,128]{3,2,1,0:T(8,128)(2,1)} async-done(((bf16[128,2,32,128]{3,2,1,0:T(8,128)(2,1)}), bf16[128,2,32,128]{3,2,1,0:T(8,128)(2,1)}, u32[]{:S(2)}, u32[]{:S(2)}) %all-to-all-start.1) | async-done | bytes 2097184 | tf_op jit(solution)/shard_map/all_to_all | solution.py:491
  145.1 6.0 %shard_map.145 = (f32[16,32,128]{2,1,0:T(8,128)}, f32[8,4096]{1,0:T(8,128)}) custom-call(bf16[128,2,32,128]{3,2,1,0:T(8,128)(2,1)} %all-to-all-done.1.ret_ref, bf16[3,128,4096]{2,1,0:T(8,128)(2,1)S(1)} %bitcast.16, f32[8,4096]{1,0:T(8,128)S(1)} %collective-permute-done.edge_ref, f32[3,3,4096]{2,1,0:T(4,128)S(1)} %copy-done.1, bf16[128,4096]{1,0:T(8,128)(2,1)} %bitcast.20), custom_call_target="tpu_custom_call" | custom-call | tf_op jit(solution)/shard_map/pallas_call | solution.py:421
  151.1 9.8 %all-to-all-start.2 = ((f32[256,2,128]{2,1,0:T(2,128)}), f32[256,2,128]{2,1,0:T(2,128)S(1)}, u32[]{:S(2)}, u32[]{:S(2)}) async-start(f32[256,2,128]{2,1,0:T(2,128)} %bitcast.26), calls=%async_computation.2 | async-start | bytes 524288 | tf_op jit(solution)/shard_map/all_to_all | solution.py:491
  160.9 4.1 %collective-permute-start.2 = (f32[8,4096]{1,0:T(8,128)}, f32[8,4096]{1,0:T(8,128)S(1)}, u32[]{:S(2)}, u32[]{:S(2)}) collective-permute-start(f32[8,4096]{1,0:T(8,128)} %get-tuple-element.15), channel_id=1, source_target_pairs={{1,0},{2,1},{3,2},{4,3},{5,4},{6,5},{7,6},{8,7},{9,8},{10,9},{11,1... | collective-permute-start | bytes 393224 | tf_op jit(solution)/shard_map/ppermute | solution.py:487
  164.9 11.5 %all-to-all-done.2 = f32[256,2,128]{2,1,0:T(2,128)S(1)} async-done(((f32[256,2,128]{2,1,0:T(2,128)}), f32[256,2,128]{2,1,0:T(2,128)S(1)}, u32[]{:S(2)}, u32[]{:S(2)}) %all-to-all-start.2) | async-done | bytes 262176 | tf_op jit(solution)/shard_map/all_to_all | solution.py:491
  176.5 0.3 reduce_sum.9
  176.7 0.0 collective-permute-done.2.later_ref
  176.7 0.7 broadcast_in_dim.10
  177.5 5.8 %all-to-all-start.3 = ((bf16[256,2,128]{2,1,0:T(2,128)(2,1)}), bf16[256,2,128]{2,1,0:T(2,128)(2,1)S(1)}, u32[]{:S(2)}, u32[]{:S(2)}) async-start(bf16[256,2,128]{2,1,0:T(2,128)(2,1)} %broadcast_in_dim.10), calls=%async_computation.3 | async-start | bytes 262144 | tf_op jit(solution)/shard_map/all_to_all | solution.py:491
  183.3 7.8 %shard_map.146 = bf16[3,128,4096]{2,1,0:T(8,128)(2,1)} custom-call(bf16[128,2,32,128]{3,2,1,0:T(8,128)(2,1)} %all-to-all-done.1.ret_ref, bf16[3,128,4096]{2,1,0:T(8,128)(2,1)} %bitcast.15, f32[8,4096]{1,0:T(8,128)S(1)} %collective-permute-done.edge_ref, f32[3,3,4096]{2,1,0:T(4,128)S(1)} %copy-done.1, bf16[128,4096]{1,0:T(8,128)(2,1)} %bitcast.21, ...), custom_call_target="tpu_custom_call" | custom-call | flops 31457280 | bytes 9437184 | tf_op jit(solution)/shard_map/pallas_call | solution.py:465
  191.1 5.0 %all-to-all-done.3 = bf16[256,2,128]{2,1,0:T(2,128)(2,1)S(1)} async-done(((bf16[256,2,128]{2,1,0:T(2,128)(2,1)}), bf16[256,2,128]{2,1,0:T(2,128)(2,1)S(1)}, u32[]{:S(2)}, u32[]{:S(2)}) %all-to-all-start.3) | async-done | bytes 131104 | tf_op jit(solution)/shard_map/all_to_all | solution.py:491
  196.1 0.1 slice_convert_fusion
  196.2 0.8 reshape.25
  (4 shorter events, 0.0 us)
Async XLA Ops:
  0.6 5.7 %copy-start.1 = (f32[3,3,4096]{2,1,0:T(4,128)S(1)}, f32[3,3,4096]{2,1,0:T(4,128)}, u32[]{:S(2)}) copy-start(f32[3,3,4096]{2,1,0:T(4,128)} %taps_ref.7) | copy-start | bytes 442372
  1.7 8.7 %collective-permute-start = (f32[8,4096]{1,0:T(8,128)S(1)}, f32[8,4096]{1,0:T(8,128)S(1)}, u32[]{:S(2)}, u32[]{:S(2)}) collective-permute-start(f32[8,4096]{1,0:T(8,128)S(1)} %shard_map.140), channel_id=1, source_target_pairs={{0,1},{1,2},{2,3},{3,4},{4,5},{5,6},{6,7},{7,8},{8,9},{9,10},{10,1... | collective-permute-start | bytes 393224 | tf_op jit(solution)/shard_map/ppermute | solution.py:487
  13.1 63.6 %all-to-all-start = ((bf16[128,2,32,128]{3,2,1,0:T(8,128)(2,1)}), bf16[128,2,32,128]{3,2,1,0:T(8,128)(2,1)S(1)}, u32[]{:S(2)}, u32[]{:S(2)}) async-start(bf16[128,2,32,128]{3,2,1,0:T(8,128)(2,1)} %shard_map.141), calls=%async_computation | async-start | bytes 4194304 | tf_op jit(solution)/shard_map/all_to_all | solution.py:491
  26.5 2.1 %copy-start.2 = (f32[2,128,128]{2,1,0:T(8,128)S(1)}, f32[2,128,128]{2,1,0:T(8,128)}, u32[]{:S(2)}) copy-start(f32[2,128,128]{2,1,0:T(8,128)} %constant.27.clone.turn_ref) | copy-start | bytes 393220
  26.6 2.1 %copy-start.3 = (bf16[256,256]{1,0:T(8,128)(2,1)S(1)}, bf16[256,256]{1,0:T(8,128)(2,1)}, u32[]{:S(2)}) copy-start(bf16[256,256]{1,0:T(8,128)(2,1)} %constant.26.clone.fwd_a_ref) | copy-start | bytes 393220
  26.6 2.1 %copy-start.9 = (bf16[2,256,256]{2,1,0:T(8,128)(2,1)S(1)}, bf16[2,256,256]{2,1,0:T(8,128)(2,1)}, u32[]{:S(2)}) copy-start(bf16[2,256,256]{2,1,0:T(8,128)(2,1)} %constant.28.clone.fwd_b_ref) | copy-start | bytes 786436
  28.6 48.1 %copy-start.4 = (bf16[1,256,256]{2,1,0:T(8,128)(2,1)S(1)}, bf16[1,256,256]{2,1,0:T(8,128)(2,1)}, u32[]{:S(2)}) copy-start(bf16[1,256,256]{2,1,0:T(8,128)(2,1)} %constant.29.clone.fwd_b_ref) | copy-start | bytes 393220
  28.6 48.1 %copy-start.5 = (bf16[1,256,256]{2,1,0:T(8,128)(2,1)S(1)}, bf16[1,256,256]{2,1,0:T(8,128)(2,1)}, u32[]{:S(2)}) copy-start(bf16[1,256,256]{2,1,0:T(8,128)(2,1)} %constant.30.clone.inv_b_ref) | copy-start | bytes 393220
  28.7 48.1 %copy-start.6 = (bf16[1,128,256]{2,1,0:T(8,128)(2,1)S(1)}, bf16[1,128,256]{2,1,0:T(8,128)(2,1)}, u32[]{:S(2)}) copy-start(bf16[1,128,256]{2,1,0:T(8,128)(2,1)} %constant.31.clone.inv_a_ref) | copy-start | bytes 196612
  85.9 9.4 %copy-start.7 = (bf16[32,128,256]{2,1,0:T(8,128)(2,1)S(1)}, bf16[32,128,256]{2,1,0:T(8,128)(2,1)}, u32[]{:S(2)}) copy-start(bf16[32,128,256]{2,1,0:T(8,128)(2,1)} %get-tuple-element.12.products_ref) | copy-start | bytes 6291460
  85.9 9.4 %copy-start.8 = (bf16[2,256,256]{2,1,0:T(8,128)(2,1)S(1)}, bf16[2,256,256]{2,1,0:T(8,128)(2,1)}, u32[]{:S(2)}) copy-start(bf16[2,256,256]{2,1,0:T(8,128)(2,1)} %constant.32.clone.inv_b_ref) | copy-start | bytes 786436
  85.9 9.5 %copy-start.10 = (bf16[2,128,256]{2,1,0:T(8,128)(2,1)S(1)}, bf16[2,128,256]{2,1,0:T(8,128)(2,1)}, u32[]{:S(2)}) copy-start(bf16[2,128,256]{2,1,0:T(8,128)(2,1)} %constant.33.clone.inv_a_ref) | copy-start | bytes 393220
  85.9 59.2 %all-to-all-start.1 = ((bf16[128,2,32,128]{3,2,1,0:T(8,128)(2,1)}), bf16[128,2,32,128]{3,2,1,0:T(8,128)(2,1)}, u32[]{:S(2)}, u32[]{:S(2)}) async-start(bf16[128,2,32,128]{3,2,1,0:T(8,128)(2,1)} %get-tuple-element.11), calls=%async_computation.1 | async-start | bytes 4194304 | tf_op jit(solution)/shard_map/all_to_all | solution.py:491
  98.9 46.2 %copy-start = (bf16[3,1,128,4096]{3,2,1,0:T(8,128)(2,1)S(1)}, bf16[3,1,128,4096]{3,2,1,0:T(8,128)(2,1)}, u32[]{:S(2)}) copy-start(bf16[3,1,128,4096]{3,2,1,0:T(8,128)(2,1)} %param.12) | copy-start | bytes 9437188
  99.0 25.2 %collective-permute-start.1 = (bf16[32,64,128]{2,1,0:T(8,128)(2,1)S(1)}, bf16[32,64,128]{2,1,0:T(8,128)(2,1)S(1)}, u32[]{:S(2)}, u32[]{:S(2)}) collective-permute-start(bf16[32,64,128]{2,1,0:T(8,128)(2,1)S(1)} %select_convert_fusion), channel_id=1, source_target_pairs={{0,128},{128,0},{1,129},{129,1},{2,130},{130,2},{3,131},{131,3},{4... | collective-permute-start | bytes 1572872 | tf_op jit(solution)/shard_map/ppermute | solution.py:519
  151.1 25.4 %all-to-all-start.2 = ((f32[256,2,128]{2,1,0:T(2,128)}), f32[256,2,128]{2,1,0:T(2,128)S(1)}, u32[]{:S(2)}, u32[]{:S(2)}) async-start(f32[256,2,128]{2,1,0:T(2,128)} %bitcast.26), calls=%async_computation.2 | async-start | bytes 524288 | tf_op jit(solution)/shard_map/all_to_all | solution.py:491
  160.9 15.9 %collective-permute-start.2 = (f32[8,4096]{1,0:T(8,128)}, f32[8,4096]{1,0:T(8,128)S(1)}, u32[]{:S(2)}, u32[]{:S(2)}) collective-permute-start(f32[8,4096]{1,0:T(8,128)} %get-tuple-element.15), channel_id=1, source_target_pairs={{1,0},{2,1},{3,2},{4,3},{5,4},{6,5},{7,6},{8,7},{9,8},{10,9},{11,1... | collective-permute-start | bytes 393224 | tf_op jit(solution)/shard_map/ppermute | solution.py:487
  177.5 18.7 %all-to-all-start.3 = ((bf16[256,2,128]{2,1,0:T(2,128)(2,1)}), bf16[256,2,128]{2,1,0:T(2,128)(2,1)S(1)}, u32[]{:S(2)}, u32[]{:S(2)}) async-start(bf16[256,2,128]{2,1,0:T(2,128)(2,1)} %broadcast_in_dim.10), calls=%async_computation.3 | async-start | bytes 262144 | tf_op jit(solution)/shard_map/all_to_all | solution.py:491

commit v6 on v4

--- a/solution.py
+++ b/solution.py
@@ -385,11 +385,14 @@
     block = grad_ref.shape[1]
     channels = pl.ds(pl.multiple_of(pl.program_id(0) * block, block), block)
     fill_ext(ext_ref, proj_ref.at[:, :, channels], edge_ref)
-    fill_turned(turned_ref, ret_ref)
+    per = ROWS // ret_ref.shape[2]
     first_ref[...] = jnp.zeros_like(first_ref)
     sums_ref[...] = jnp.zeros_like(sums_ref)
     for at, lanes in enumerate(lanes_of(grad_ref.shape[1])):
         sums = [jnp.zeros((8, ROWS), jnp.float32)] * 9
+        for which in range(2):
+            turned = ret_ref[pl.ds(at * per, per), which].reshape(ROWS, ROWS).T
+            turned_ref[which, :, lanes] = turned.astype(jnp.float32)
         for row in range(0, ROWS, STEP):
             shifted = [inputs_at(ext_ref, stream, row, lanes) for stream in range(3)]
             grads = grads_at(turned_ref, taps_ref, grad_ref, row, lanes, shifted[1], shifted[2])

time: 198 us -> 198 us (level)
  no operation moved by 1% of the time
where the time goes in v6:
time: 198 us; the launch traced here: 197 us
  waiting for transfers between devices  95.6 us (48%)
  starting transfers between devices  50.1 us (25%)
  Pallas kernels  44.5 us (22%)
  local copies, waits for them, and re-layouts  5.22 us (3%)
    all_to_all x4, waiting for transfers between devices, exchanged(): return lax.all_to_all(value, axes, split_axis=0, concat_axis=0, tiled=True)  73.3 us
    all_to_all x4, starting transfers between devices, exchanged(): return lax.all_to_all(value, axes, split_axis=0, concat_axis=0, tiled=True)  38.5 us
    ppermute x1, waiting for transfers between devices, local(): lax.ppermute(jnp.where(second, lower, upper).astype(jnp.bfloat16), 'dp',...  22.2 us
    pallas_call x1, Pallas kernels, spectrum(): pl.pallas_call(spectrum_kernel, grid=(width // block,), in_specs=[pl.Bloc...  10.4 us
    pallas_call x1, Pallas kernels, convolve(): pl.pallas_call(functools.partial(conv_kernel, group=group), grid=(width /...  9.13 us
    ppermute x2, starting transfers between devices, passed_along(): lax.ppermute(value, 'ctx', [(source, source + steps) for source in range(...  8.65 us
    pallas_call x1, Pallas kernels, stream_grads(): pl.pallas_call(grads_kernel, grid=(channels // block,), in_specs=local_sp...  7.79 us
    pallas_call x1, Pallas kernels, tap_sums(): pl.pallas_call(sums_kernel, grid=(channels // block,), in_specs=specs, ou...  5.85 us
  transfers between devices with their start and end apart: 7, of which 5 were waited for; matrix products, arithmetic and copies ran while one was open for 2% of the time, Pallas kernels for 13%

profile of v6, /device:TPU:1, one launch (start us, length us, event | category | flops | bytes accessed | tf_op | source)
XLA Modules:
  0.0 196.9 jit_solution(7879356950033559738)
XLA Ops:
  0.6 0.0 copy-start.1
  0.6 1.1 shard_map.140
  1.7 4.6 %collective-permute-start = (f32[8,4096]{1,0:T(8,128)S(1)}, f32[8,4096]{1,0:T(8,128)S(1)}, u32[]{:S(2)}, u32[]{:S(2)}) collective-permute-start(f32[8,4096]{1,0:T(8,128)S(1)} %shard_map.140), channel_id=1, source_target_pairs={{0,1},{1,2},{2,3},{3,4},{4,5},{5,6},{6,7},{7,8},{8,9},{9,10},{10,1... | collective-permute-start | bytes 393224 | tf_op jit(solution)/shard_map/ppermute | solution.py:490
  6.3 0.0 copy-done.1
  6.3 4.1 %shard_map.139.rough_ref = bf16[128,2,32,128]{3,2,1,0:T(8,128)(2,1)S(1)} custom-call(bf16[3,128,4096]{2,1,0:T(8,128)(2,1)} %bitcast.13, f32[3,3,4096]{2,1,0:T(4,128)S(1)} %copy-done.1, bf16[128,4096]{1,0:T(8,128)(2,1)} %bitcast.18), custom_call_target="tpu_custom_call" | custom-call | flops 20971520 | bytes 6291456 | tf_op jit(solution)/shard_map/pallas_call | solution.py:134
  10.4 0.0 collective-permute-done.edge_ref
  10.4 2.7 %shard_map.141 = bf16[128,2,32,128]{3,2,1,0:T(8,128)(2,1)} custom-call(bf16[128,2,32,128]{3,2,1,0:T(8,128)(2,1)S(1)} %shard_map.139.rough_ref, bf16[3,128,4096]{2,1,0:T(8,128)(2,1)} %bitcast.14, f32[8,4096]{1,0:T(8,128)S(1)} %collective-permute-done.edge_ref, f32[3,3,4096]{2,1,0:T(4,128)S(1)} %copy-done.1, bf16[128,4096]{1,0:T(8,128)(2,1)} %bitcast.19), custom_call_target="tpu_custom_call" | custom-call | tf_op jit(solution)/shard_map/pallas_call | solution.py:177
  13.1 13.4 %all-to-all-start = ((bf16[128,2,32,128]{3,2,1,0:T(8,128)(2,1)}), bf16[128,2,32,128]{3,2,1,0:T(8,128)(2,1)S(1)}, u32[]{:S(2)}, u32[]{:S(2)}) async-start(bf16[128,2,32,128]{3,2,1,0:T(8,128)(2,1)} %shard_map.141), calls=%async_computation | async-start | bytes 4194304 | tf_op jit(solution)/shard_map/all_to_all | solution.py:494
  26.5 0.0 copy-start.2
  26.6 0.0 copy-start.3
  26.6 0.0 copy-start.9
  26.6 2.0 %copy.16 = f32[4,8,128,128]{3,2,1,0:T(8,128)S(1)} copy(f32[4,8,128,128]{3,1,2,0:T(8,128)} %bitcast.24) | data formatting | bytes 4194304
  28.6 0.0 copy-done.2
  28.6 0.0 copy-done.3
  28.6 0.0 copy-done.9
  28.6 0.0 copy-start.4
  28.6 0.0 copy-start.5
  28.7 0.0 copy-start.6
  28.7 10.4 %shard_map.142.spec_ref = f32[32,128,256]{2,1,0:T(8,128)} custom-call(f32[32,128,128]{2,1,0:T(8,128)S(1)} %bitcast.17, bf16[256,256]{1,0:T(8,128)(2,1)S(1)} %copy-done.3, f32[2,128,128]{2,1,0:T(8,128)S(1)} %copy-done.2, bf16[2,256,256]{2,1,0:T(8,128)(2,1)S(1)} %copy-done.9), custom_call_target="tpu_custom_call" | custom-call | flops 5368709120 | bytes 6291456 | tf_op jit(solution)/shard_map/pallas_call | solution.py:218
  39.0 37.7 %all-to-all-done.in_ref = bf16[128,2,32,128]{3,2,1,0:T(8,128)(2,1)S(1)} async-done(((bf16[128,2,32,128]{3,2,1,0:T(8,128)(2,1)}), bf16[128,2,32,128]{3,2,1,0:T(8,128)(2,1)S(1)}, u32[]{:S(2)}, u32[]{:S(2)}) %all-to-all-start) | async-done | bytes 2097184 | tf_op jit(solution)/shard_map/all_to_all | solution.py:494
  76.7 0.0 copy-done.4
  76.7 0.0 copy-done.5
  76.7 0.0 copy-done.6
  76.7 9.1 %shard_map.143 = (bf16[128,2,32,128]{3,2,1,0:T(8,128)(2,1)}, bf16[32,128,256]{2,1,0:T(8,128)(2,1)}) custom-call(bf16[128,2,32,128]{3,2,1,0:T(8,128)(2,1)S(1)} %all-to-all-done.in_ref, f32[32,128,256]{2,1,0:T(8,128)} %shard_map.142.spec_ref, bf16[256,256]{1,0:T(8,128)(2,1)S(1)} %copy-done.3, f32[2,128,128]{2,1,0:T(8,128)S(1)} %copy-done.2, ...), custom_call_target="tpu_custom_call" | custom-call | tf_op jit(solution)/shard_map/pallas_call | solution.py:320
  85.9 9.4 %all-to-all-start.1 = ((bf16[128,2,32,128]{3,2,1,0:T(8,128)(2,1)}), bf16[128,2,32,128]{3,2,1,0:T(8,128)(2,1)}, u32[]{:S(2)}, u32[]{:S(2)}) async-start(bf16[128,2,32,128]{3,2,1,0:T(8,128)(2,1)} %get-tuple-element.11), calls=%async_computation.1 | async-start | bytes 4194304 | tf_op jit(solution)/shard_map/all_to_all | solution.py:494
  95.3 0.0 copy-done.7
  95.3 0.0 copy-done.8
  95.3 0.0 copy-done.10
  95.3 3.5 %shard_map.144 = f32[32,128,128]{2,1,0:T(8,128)S(1)} custom-call(bf16[32,128,256]{2,1,0:T(8,128)(2,1)S(1)} %copy-done.7, f32[2,128,128]{2,1,0:T(8,128)S(1)} %copy-done.2, bf16[2,256,256]{2,1,0:T(8,128)(2,1)S(1)} %copy-done.8, bf16[2,128,256]{2,1,0:T(8,128)(2,1)S(1)} %copy-done.10), custom_call_target="tpu_custom_call" | custom-call | flops 4294967296 | bytes 4194304 | tf_op jit(solution)/shard_map/pallas_call | solution.py:353
  98.8 0.1 select_convert_fusion
  98.9 0.0 copy-start
  99.0 3.0 %collective-permute-start.1 = (bf16[32,64,128]{2,1,0:T(8,128)(2,1)S(1)}, bf16[32,64,128]{2,1,0:T(8,128)(2,1)S(1)}, u32[]{:S(2)}, u32[]{:S(2)}) collective-permute-start(bf16[32,64,128]{2,1,0:T(8,128)(2,1)S(1)} %select_convert_fusion), channel_id=1, source_target_pairs={{0,128},{128,0},{1,129},{129,1},{2,130},{130,2},{3,131},{131,3},{4... | collective-permute-start | bytes 1572872 | tf_op jit(solution)/shard_map/ppermute | solution.py:522
  102.0 22.2 %collective-permute-done.1 = bf16[32,64,128]{2,1,0:T(8,128)(2,1)S(1)} collective-permute-done((bf16[32,64,128]{2,1,0:T(8,128)(2,1)S(1)}, bf16[32,64,128]{2,1,0:T(8,128)(2,1)S(1)}, u32[]{:S(2)}, u32[]{:S(2)}) %collective-permute-start.1) | collective-permute-done | bytes 524320 | tf_op jit(solution)/shard_map/ppermute | solution.py:522
  124.2 0.3 convert_add_fusion
  124.5 1.6 copy.19
  126.0 19.1 %all-to-all-done.1.ret_ref = bf16[128,2,32,128]{3,2,1,0:T(8,128)(2,1)} async-done(((bf16[128,2,32,128]{3,2,1,0:T(8,128)(2,1)}), bf16[128,2,32,128]{3,2,1,0:T(8,128)(2,1)}, u32[]{:S(2)}, u32[]{:S(2)}) %all-to-all-start.1) | async-done | bytes 2097184 | tf_op jit(solution)/shard_map/all_to_all | solution.py:494
  145.1 5.9 %shard_map.145 = (f32[16,32,128]{2,1,0:T(8,128)}, f32[8,4096]{1,0:T(8,128)}) custom-call(bf16[128,2,32,128]{3,2,1,0:T(8,128)(2,1)} %all-to-all-done.1.ret_ref, bf16[3,128,4096]{2,1,0:T(8,128)(2,1)S(1)} %bitcast.16, f32[8,4096]{1,0:T(8,128)S(1)} %collective-permute-done.edge_ref, f32[3,3,4096]{2,1,0:T(4,128)S(1)} %copy-done.1, bf16[128,4096]{1,0:T(8,128)(2,1)} %bitcast.20), custom_call_target="tpu_custom_call" | custom-call | tf_op jit(solution)/shard_map/pallas_call | solution.py:424
  151.0 9.8 %all-to-all-start.2 = ((f32[256,2,128]{2,1,0:T(2,128)}), f32[256,2,128]{2,1,0:T(2,128)S(1)}, u32[]{:S(2)}, u32[]{:S(2)}) async-start(f32[256,2,128]{2,1,0:T(2,128)} %bitcast.26), calls=%async_computation.2 | async-start | bytes 524288 | tf_op jit(solution)/shard_map/all_to_all | solution.py:494
  160.8 4.1 %collective-permute-start.2 = (f32[8,4096]{1,0:T(8,128)}, f32[8,4096]{1,0:T(8,128)S(1)}, u32[]{:S(2)}, u32[]{:S(2)}) collective-permute-start(f32[8,4096]{1,0:T(8,128)} %get-tuple-element.15), channel_id=1, source_target_pairs={{1,0},{2,1},{3,2},{4,3},{5,4},{6,5},{7,6},{8,7},{9,8},{10,9},{11,1... | collective-permute-start | bytes 393224 | tf_op jit(solution)/shard_map/ppermute | solution.py:490
  164.8 11.5 %all-to-all-done.2 = f32[256,2,128]{2,1,0:T(2,128)S(1)} async-done(((f32[256,2,128]{2,1,0:T(2,128)}), f32[256,2,128]{2,1,0:T(2,128)S(1)}, u32[]{:S(2)}, u32[]{:S(2)}) %all-to-all-start.2) | async-done | bytes 262176 | tf_op jit(solution)/shard_map/all_to_all | solution.py:494
  176.4 0.3 reduce_sum.9
  176.6 0.0 collective-permute-done.2.later_ref
  176.6 0.7 broadcast_in_dim.10
  177.4 5.8 %all-to-all-start.3 = ((bf16[256,2,128]{2,1,0:T(2,128)(2,1)}), bf16[256,2,128]{2,1,0:T(2,128)(2,1)S(1)}, u32[]{:S(2)}, u32[]{:S(2)}) async-start(bf16[256,2,128]{2,1,0:T(2,128)(2,1)} %broadcast_in_dim.10), calls=%async_computation.3 | async-start | bytes 262144 | tf_op jit(solution)/shard_map/all_to_all | solution.py:494
  183.2 7.8 %shard_map.146 = bf16[3,128,4096]{2,1,0:T(8,128)(2,1)} custom-call(bf16[128,2,32,128]{3,2,1,0:T(8,128)(2,1)} %all-to-all-done.1.ret_ref, bf16[3,128,4096]{2,1,0:T(8,128)(2,1)} %bitcast.15, f32[8,4096]{1,0:T(8,128)S(1)} %collective-permute-done.edge_ref, f32[3,3,4096]{2,1,0:T(4,128)S(1)} %copy-done.1, bf16[128,4096]{1,0:T(8,128)(2,1)} %bitcast.21, ...), custom_call_target="tpu_custom_call" | custom-call | flops 31457280 | bytes 9437184 | tf_op jit(solution)/shard_map/pallas_call | solution.py:468
  191.0 5.0 %all-to-all-done.3 = bf16[256,2,128]{2,1,0:T(2,128)(2,1)S(1)} async-done(((bf16[256,2,128]{2,1,0:T(2,128)(2,1)}), bf16[256,2,128]{2,1,0:T(2,128)(2,1)S(1)}, u32[]{:S(2)}, u32[]{:S(2)}) %all-to-all-start.3) | async-done | bytes 131104 | tf_op jit(solution)/shard_map/all_to_all | solution.py:494
  196.0 0.1 slice_convert_fusion
  196.1 0.8 reshape.25
  (4 shorter events, 0.0 us)
Async XLA Ops:
  0.6 5.7 %copy-start.1 = (f32[3,3,4096]{2,1,0:T(4,128)S(1)}, f32[3,3,4096]{2,1,0:T(4,128)}, u32[]{:S(2)}) copy-start(f32[3,3,4096]{2,1,0:T(4,128)} %taps_ref.7) | copy-start | bytes 442372
  1.7 8.7 %collective-permute-start = (f32[8,4096]{1,0:T(8,128)S(1)}, f32[8,4096]{1,0:T(8,128)S(1)}, u32[]{:S(2)}, u32[]{:S(2)}) collective-permute-start(f32[8,4096]{1,0:T(8,128)S(1)} %shard_map.140), channel_id=1, source_target_pairs={{0,1},{1,2},{2,3},{3,4},{4,5},{5,6},{6,7},{7,8},{8,9},{9,10},{10,1... | collective-permute-start | bytes 393224 | tf_op jit(solution)/shard_map/ppermute | solution.py:490
  13.1 63.6 %all-to-all-start = ((bf16[128,2,32,128]{3,2,1,0:T(8,128)(2,1)}), bf16[128,2,32,128]{3,2,1,0:T(8,128)(2,1)S(1)}, u32[]{:S(2)}, u32[]{:S(2)}) async-start(bf16[128,2,32,128]{3,2,1,0:T(8,128)(2,1)} %shard_map.141), calls=%async_computation | async-start | bytes 4194304 | tf_op jit(solution)/shard_map/all_to_all | solution.py:494
  26.5 2.1 %copy-start.2 = (f32[2,128,128]{2,1,0:T(8,128)S(1)}, f32[2,128,128]{2,1,0:T(8,128)}, u32[]{:S(2)}) copy-start(f32[2,128,128]{2,1,0:T(8,128)} %constant.27.clone.turn_ref) | copy-start | bytes 393220
  26.6 2.1 %copy-start.3 = (bf16[256,256]{1,0:T(8,128)(2,1)S(1)}, bf16[256,256]{1,0:T(8,128)(2,1)}, u32[]{:S(2)}) copy-start(bf16[256,256]{1,0:T(8,128)(2,1)} %constant.26.clone.fwd_a_ref) | copy-start | bytes 393220
  26.6 2.1 %copy-start.9 = (bf16[2,256,256]{2,1,0:T(8,128)(2,1)S(1)}, bf16[2,256,256]{2,1,0:T(8,128)(2,1)}, u32[]{:S(2)}) copy-start(bf16[2,256,256]{2,1,0:T(8,128)(2,1)} %constant.28.clone.fwd_b_ref) | copy-start | bytes 786436
  28.6 48.1 %copy-start.4 = (bf16[1,256,256]{2,1,0:T(8,128)(2,1)S(1)}, bf16[1,256,256]{2,1,0:T(8,128)(2,1)}, u32[]{:S(2)}) copy-start(bf16[1,256,256]{2,1,0:T(8,128)(2,1)} %constant.29.clone.fwd_b_ref) | copy-start | bytes 393220
  28.6 48.1 %copy-start.5 = (bf16[1,256,256]{2,1,0:T(8,128)(2,1)S(1)}, bf16[1,256,256]{2,1,0:T(8,128)(2,1)}, u32[]{:S(2)}) copy-start(bf16[1,256,256]{2,1,0:T(8,128)(2,1)} %constant.30.clone.inv_b_ref) | copy-start | bytes 393220
  28.7 48.1 %copy-start.6 = (bf16[1,128,256]{2,1,0:T(8,128)(2,1)S(1)}, bf16[1,128,256]{2,1,0:T(8,128)(2,1)}, u32[]{:S(2)}) copy-start(bf16[1,128,256]{2,1,0:T(8,128)(2,1)} %constant.31.clone.inv_a_ref) | copy-start | bytes 196612
  85.9 9.4 %copy-start.7 = (bf16[32,128,256]{2,1,0:T(8,128)(2,1)S(1)}, bf16[32,128,256]{2,1,0:T(8,128)(2,1)}, u32[]{:S(2)}) copy-start(bf16[32,128,256]{2,1,0:T(8,128)(2,1)} %get-tuple-element.12.products_ref) | copy-start | bytes 6291460
  85.9 9.4 %copy-start.8 = (bf16[2,256,256]{2,1,0:T(8,128)(2,1)S(1)}, bf16[2,256,256]{2,1,0:T(8,128)(2,1)}, u32[]{:S(2)}) copy-start(bf16[2,256,256]{2,1,0:T(8,128)(2,1)} %constant.32.clone.inv_b_ref) | copy-start | bytes 786436
  85.9 9.5 %copy-start.10 = (bf16[2,128,256]{2,1,0:T(8,128)(2,1)S(1)}, bf16[2,128,256]{2,1,0:T(8,128)(2,1)}, u32[]{:S(2)}) copy-start(bf16[2,128,256]{2,1,0:T(8,128)(2,1)} %constant.33.clone.inv_a_ref) | copy-start | bytes 393220
  85.9 59.2 %all-to-all-start.1 = ((bf16[128,2,32,128]{3,2,1,0:T(8,128)(2,1)}), bf16[128,2,32,128]{3,2,1,0:T(8,128)(2,1)}, u32[]{:S(2)}, u32[]{:S(2)}) async-start(bf16[128,2,32,128]{3,2,1,0:T(8,128)(2,1)} %get-tuple-element.11), calls=%async_computation.1 | async-start | bytes 4194304 | tf_op jit(solution)/shard_map/all_to_all | solution.py:494
  98.9 46.2 %copy-start = (bf16[3,1,128,4096]{3,2,1,0:T(8,128)(2,1)S(1)}, bf16[3,1,128,4096]{3,2,1,0:T(8,128)(2,1)}, u32[]{:S(2)}) copy-start(bf16[3,1,128,4096]{3,2,1,0:T(8,128)(2,1)} %param.12) | copy-start | bytes 9437188
  99.0 25.2 %collective-permute-start.1 = (bf16[32,64,128]{2,1,0:T(8,128)(2,1)S(1)}, bf16[32,64,128]{2,1,0:T(8,128)(2,1)S(1)}, u32[]{:S(2)}, u32[]{:S(2)}) collective-permute-start(bf16[32,64,128]{2,1,0:T(8,128)(2,1)S(1)} %select_convert_fusion), channel_id=1, source_target_pairs={{0,128},{128,0},{1,129},{129,1},{2,130},{130,2},{3,131},{131,3},{4... | collective-permute-start | bytes 1572872 | tf_op jit(solution)/shard_map/ppermute | solution.py:522
  151.0 25.4 %all-to-all-start.2 = ((f32[256,2,128]{2,1,0:T(2,128)}), f32[256,2,128]{2,1,0:T(2,128)S(1)}, u32[]{:S(2)}, u32[]{:S(2)}) async-start(f32[256,2,128]{2,1,0:T(2,128)} %bitcast.26), calls=%async_computation.2 | async-start | bytes 524288 | tf_op jit(solution)/shard_map/all_to_all | solution.py:494
  160.8 15.9 %collective-permute-start.2 = (f32[8,4096]{1,0:T(8,128)}, f32[8,4096]{1,0:T(8,128)S(1)}, u32[]{:S(2)}, u32[]{:S(2)}) collective-permute-start(f32[8,4096]{1,0:T(8,128)} %get-tuple-element.15), channel_id=1, source_target_pairs={{1,0},{2,1},{3,2},{4,3},{5,4},{6,5},{7,6},{8,7},{9,8},{10,9},{11,1... | collective-permute-start | bytes 393224 | tf_op jit(solution)/shard_map/ppermute | solution.py:490
  177.4 18.7 %all-to-all-start.3 = ((bf16[256,2,128]{2,1,0:T(2,128)(2,1)}), bf16[256,2,128]{2,1,0:T(2,128)(2,1)S(1)}, u32[]{:S(2)}, u32[]{:S(2)}) async-start(bf16[256,2,128]{2,1,0:T(2,128)(2,1)} %broadcast_in_dim.10), calls=%async_computation.3 | async-start | bytes 262144 | tf_op jit(solution)/shard_map/all_to_all | solution.py:494
